TPU v7x, 128 devices: a whole 4x4x4 slice. The times are simulated.
128 devices in a mesh: inst: 4 (over y), ctx: 16 (over z, x), head: 2 (over core).
Axes of the slice: x: 4, y: 4, z: 4, core: 2. Of those that a mesh axis runs over, the one named last changes fastest.
Arguments:
- cache: bfloat16 [2, 32, 8192, 1024], P(None, 'inst', 'ctx', 'head'), may hold values from -600 to 600, as said below
- hidden: bfloat16 [3, 32, 6144], P(None, 'inst', 'ctx'), may hold values from -14 to 14
- norm_gain: bfloat16 [6144], P('ctx'), may hold values from 0.099609375 to 1.8984375
- w_query: bfloat16 [6144, 6144], P('ctx', 'head'), may hold values from -0.078125 to 0.078125
- key_value_weight: bfloat16 [2, 6144, 1024], P(None, 'ctx', 'head'), may hold values from -0.078125 to 0.078125
- w_out: bfloat16 [6144, 6144], P('head', 'ctx'), may hold values from -0.078125 to 0.078125
- lengths: int32 [32], replicated, may hold values from 0 to 8189, as said below
- dest_inst: int32 [8], replicated, may hold values from 0 to 2, as said below
- dest_slot: int32 [8], replicated, may hold values from 0 to 7, as said below
- block_order: int32 [256], replicated, may hold values from 0 to 255, as said below
Outputs:
- new_cache: bfloat16 [2, 32, 8192, 1024], P(None, 'inst', 'ctx', 'head')
- attn_out: bfloat16 [3, 32, 6144], P(None, 'inst', ('ctx', 'head'))
Inputs may be any that keep to these rules, and one draw needn't show every extreme that they name: `cache`: keys and values; the retiring instance 4 - 1 keeps its slots in the block order of block_order, the others in position order. `lengths`: 0 marks a free slot; every slot of instance 4 - 1 holds a request; each instance below it has exactly as many free slots as requests that move to it; some request has exactly 8189. `dest_inst`: no instance takes more than 3 requests, and some instance takes exactly 3. The pairs of dest_inst and dest_slot are distinct and name free slots. A permutation of the 256 blocks of 32 positions; stored block j holds logical positions block_order[j] * 32 onward; the 16 blocks stored on one ctx device belong to the ranges of 16 different ctx devices, range c being blocks c * 16 to c * 16 + 15.
All inputs are finite; a program needn't handle non-finite values.
Results may differ from a plain program's by a relative error of at most 0.02.
The roundings to bfloat16 on the way count: a program that leaves them out, or rounds other values in their place, can miss the bound.
Values may be sent and summed in bfloat16 or wider, within the bound.
No kernel may reach another device: no remote copies, remote signals or barrier semaphores. Data moves between devices by JAX's collectives and lax.ppermute only.
A program may use at most 128 MiB of HBM per device.

v0:
```python
import jax
import jax.numpy as jnp
from jax import lax
from jax.sharding import PartitionSpec as P

MODEL_WIDTH = 6144
HEAD_SIZE = 128


ROPE_BASE = 500000.0
NORM_EPSILON = 1e-05
MASKED_SCORE = -1e30


def spread(x, axis, root):
    mine = lax.axis_index(axis) == root
    return lax.psum(jnp.where(mine, x, jnp.zeros_like(x)), axis)


def apply_rotary(vector, position):
    half_dim = vector.shape[-1] // 2
    frequency = ROPE_BASE ** (-jnp.arange(half_dim, dtype=jnp.float32) * 2.0 / vector.shape[-1])
    angles = position.astype(jnp.float32)[..., None, None] * frequency
    cosine = jnp.cos(angles)
    sine = jnp.sin(angles)
    front_half = vector[..., :half_dim]
    second = vector[..., half_dim:]
    return jnp.concatenate(
        [front_half * cosine - second * sine, second * cosine + front_half * sine], axis=-1
    )


def packing(dest_inst, target, capacity):
    amount = dest_inst.shape[0]
    heading = (dest_inst == target).astype(jnp.int32)
    placement = jnp.cumsum(heading) - 1
    select = (heading[None, :] == 1) & (
        placement[None, :] == jnp.arange(capacity, dtype=jnp.int32)[:, None]
    )
    source = jnp.sum(
        select.astype(jnp.int32) * jnp.arange(amount, dtype=jnp.int32)[None, :], axis=1
    )
    return (source, placement)


def send_order(layout, myself, amount):
    stored_row = lax.dynamic_index_in_dim(layout, myself, 0, keepdims=False)
    owners = stored_row // amount
    slot_ids = jnp.arange(amount, dtype=jnp.int32)
    return jnp.sum(
        (owners[None, :] == slot_ids[:, None]).astype(jnp.int32) * slot_ids[None, :], axis=1
    )


def receive_order(layout, myself, amount):
    slot_ids = jnp.arange(amount, dtype=jnp.int32)
    mine_mask = layout // amount == myself
    within = jnp.sum(jnp.where(mine_mask, layout % amount, 0), axis=1)
    return jnp.sum(
        (within[None, :] == slot_ids[:, None]).astype(jnp.int32) * slot_ids[None, :], axis=1
    )


def shards(
    cache,
    hidden,
    norm_gain,
    w_query,
    key_value_weight,
    w_out,
    lengths,
    dest_inst,
    dest_slot,
    block_order,
):
    inst_count = lax.axis_size("inst")
    ctx_count = lax.axis_size("ctx")
    instance = lax.axis_index("inst")
    context = lax.axis_index("ctx")
    slot_count = cache.shape[1]
    shard_len = cache.shape[2]
    feature_rows = cache.shape[3]
    step_count = hidden.shape[0]
    local_width = hidden.shape[2]
    block_len = shard_len // ctx_count
    retiring = inst_count - 1
    capacity = (slot_count + inst_count - 2) // (inst_count - 1)
    layout = block_order.reshape(ctx_count, ctx_count)
    outgoing = send_order(layout, context, ctx_count)
    incoming = receive_order(layout, context, ctx_count)
    holding = jnp.take(
        lax.all_to_all(
            jnp.take(
                cache.reshape(2, slot_count, ctx_count, block_len, feature_rows), outgoing, axis=2
            ),
            "ctx",
            split_axis=2,
            concat_axis=2,
            tiled=True,
        ),
        incoming,
        axis=2,
    ).reshape(2, slot_count, shard_len, feature_rows)
    own_source, own_place = packing(dest_inst, instance, capacity)
    every_cache, every_hidden = (
        spread(holding, "inst", retiring),
        spread(hidden, "inst", retiring),
    )
    moved_cache = jnp.take(every_cache, own_source, axis=1)
    moved_hidden = jnp.take(every_hidden, own_source, axis=1)
    slot_ids = jnp.arange(slot_count, dtype=jnp.int32)
    match = (dest_inst[:, None] == instance) & (dest_slot[:, None] == slot_ids[None, :])
    match_int = match.astype(jnp.int32)
    taken = jnp.any(match, axis=0)
    buffer_pos = jnp.sum(match_int * own_place[:, None], axis=0)
    own_len = lax.dynamic_slice_in_dim(lengths, instance * slot_count, slot_count)
    retired_len = lengths[retiring * slot_count :]
    moved_len = jnp.sum(match_int * retired_len[:, None], axis=0)
    new_len = jnp.where(instance == retiring, 0, jnp.where(taken, moved_len, own_len))
    active = new_len > 0
    slot_cache = jnp.where(
        taken[None, :, None, None], jnp.take(moved_cache, buffer_pos, axis=1), cache
    )
    x_rows = jnp.where(taken[None, :, None], jnp.take(moved_hidden, buffer_pos, axis=1), hidden)
    row_count = step_count * slot_count
    flat = x_rows.reshape(row_count, local_width).astype(jnp.float32)
    part_sum = jnp.sum(flat, axis=1)
    part_sq = jnp.sum(flat * flat, axis=1)
    scaled = (flat * norm_gain.astype(jnp.float32)).astype(jnp.bfloat16)
    part_query = jnp.dot(scaled, w_query, preferred_element_type=jnp.float32)
    part_keyval = jnp.einsum(
        "rd,jdf->jrf", scaled, key_value_weight, preferred_element_type=jnp.float32
    )
    gain_query = jnp.dot(norm_gain, w_query, preferred_element_type=jnp.float32)
    gain_keyval = jnp.einsum(
        "d,jdf->jf", norm_gain, key_value_weight, preferred_element_type=jnp.float32
    )
    sums = lax.psum((part_sum, part_sq, part_query, part_keyval, gain_query, gain_keyval), "ctx")
    mean = sums[0] / MODEL_WIDTH
    mean_sq = sums[1] / MODEL_WIDTH
    scale_rows = lax.rsqrt(mean_sq - mean * mean + NORM_EPSILON)
    query = scale_rows[:, None] * (sums[2] - mean[:, None] * sums[4][None, :])
    keyval = scale_rows[None, :, None] * (sums[3] - mean[None, :, None] * sums[5][:, None, :])
    local_kv = feature_rows // HEAD_SIZE
    local_q = query.shape[1] // HEAD_SIZE
    query_group = local_q // local_kv
    token_positions = new_len[None, :] + jnp.arange(step_count, dtype=jnp.int32)[:, None]
    query_rot = apply_rotary(
        query.reshape(step_count, slot_count, local_q, HEAD_SIZE), token_positions
    ).astype(jnp.bfloat16)
    rotated_key = apply_rotary(
        keyval[0].reshape(step_count, slot_count, local_kv, HEAD_SIZE), token_positions
    ).astype(jnp.bfloat16)
    value_new = keyval[1].reshape(step_count, slot_count, feature_rows).astype(jnp.bfloat16)
    entries = jnp.stack([rotated_key.reshape(step_count, slot_count, feature_rows), value_new])
    global_pos = context * shard_len + jnp.arange(shard_len, dtype=jnp.int32)
    keep_old = (global_pos[None, :] < new_len[:, None]) & active[:, None]
    fresh = jnp.where(keep_old[None, :, :, None], slot_cache, jnp.zeros_like(slot_cache))
    for step in range(step_count):
        hit = (global_pos[None, :] == (new_len + step)[:, None]) & active[:, None]
        fresh = jnp.where(hit[None, :, :, None], entries[:, step][:, :, None, :], fresh)
    cached_keys = fresh[0].reshape(slot_count, shard_len, local_kv, HEAD_SIZE)
    cached_values = fresh[1].reshape(slot_count, shard_len, local_kv, HEAD_SIZE)
    grouped = query_rot.reshape(step_count, slot_count, local_kv, query_group, HEAD_SIZE)
    scores = jnp.einsum(
        "tsgjd,spgd->tsgjp", grouped, cached_keys, preferred_element_type=jnp.float32
    ) * HEAD_SIZE ** (-0.5)
    visible = (global_pos[None, None, :] <= token_positions[:, :, None]) & active[None, :, None]
    visible = visible[:, :, None, None, :]
    masked = jnp.where(visible, scores, MASKED_SCORE)
    peak = lax.pmax(jnp.max(masked, axis=-1), "ctx")
    weights = jnp.where(visible, jnp.exp(masked - peak[..., None]), 0.0)
    partial_out = jnp.einsum(
        "tsgjp,spgd->tsgjd",
        weights.astype(jnp.bfloat16),
        cached_values,
        preferred_element_type=jnp.float32,
    )
    total, combined = (
        lax.psum(jnp.sum(weights, axis=-1).astype(jnp.bfloat16), "ctx").astype(jnp.float32),
        lax.psum(partial_out.astype(jnp.bfloat16), "ctx").astype(jnp.float32),
    )
    attended = (combined / jnp.where(total > 0, total, 1.0)[..., None]).astype(jnp.bfloat16)
    attended = attended.reshape(row_count, local_q * HEAD_SIZE)
    projected = jnp.dot(attended, w_out, preferred_element_type=jnp.float32)
    attn_out = lax.psum_scatter(
        projected.astype(jnp.bfloat16), "head", scatter_dimension=1, tiled=True
    )
    return (fresh, attn_out.reshape(step_count, slot_count, -1))


def solution(mesh):
    placed = (
        P(None, "inst", "ctx", "head"),
        P(None, "inst", "ctx"),
        P("ctx"),
        P("ctx", "head"),
        P(None, "ctx", "head"),
        P("head", "ctx"),
        P(),
        P(),
        P(),
        P(),
    )
    return jax.shard_map(
        shards,
        mesh=mesh,
        in_specs=placed,
        out_specs=(P(None, "inst", "ctx", "head"), P(None, "inst", ("ctx", "head"))),
        check_vma=False,
    )
```

profile of v0, /device:TPU:1, one launch (start us, length us, event | category | flops | bytes accessed | tf_op | source)
XLA Modules:
  0.0 660.8 jit_solution(6687800272535686537)
XLA Ops:
  8.3 8.3 %gather_fusion.4 = bf16[16,2,8,32,512]{4,3,2,1,0:T(8,128)(2,1)} fusion(bf16[2,8,16,32,512]{4,3,2,1,0:T(8,128)(2,1)} %bitcast.100, s32[1024]{0:T(1024)S(1)} %pad_clamp_fusion.1), kind=kCustom, calls=%fused_computation.clone | custom fusion | bytes 16777280 | tf_op jit(solution)/shard_map/jit(_take)/gather | solution.py:93
  16.6 7.6 %select_bitcast_fusion = bf16[2,8,16,32,512]{4,3,1,0,2:T(8,128)(2,1)} fusion(bf16[16,2,8,32,512]{4,3,2,1,0:T(8,128)(2,1)} %gather_fusion.4, pred[16]{0:T(512)(128)(4,1)S(1)} %compare_and_fusion.6), kind=kLoop, calls=%fused_computation.12 | loop fusion | flops 4194304 | bytes 16777232 | tf_op jit(solution)/shard_map/jit(_take)/select_n | solution.py:93
  24.3 8.6 %all-to-all-start = ((bf16[2,8,16,32,512]{4,3,1,0,2:T(8,128)(2,1)}), bf16[2,8,16,32,512]{4,3,1,0,2:T(8,128)(2,1)}, u32[]{:S(2)}, u32[]{:S(2)}) async-start(bf16[2,8,16,32,512]{4,3,1,0,2:T(8,128)(2,1)} %select_bitcast_fusion), calls=%async_computation | async-start | bytes 16777216 | tf_op jit(solution)/shard_map/all_to_all | solution.py:92
  33.3 15.1 %psum.70 = bf16[3,8,384]{2,0,1:T(4,128)(2,1)S(1)} all-reduce(bf16[3,8,384]{2,0,1:T(4,128)(2,1)S(1)} %broadcast_select_fusion), channel_id=1, replica_groups=mesh['inst'=4,'ctx'=16,'head'=2] {'inst'}, use_global_device_ids=true, to_apply=%region_5.6 | all-reduce | flops 9216 | bytes 36864 | tf_op jit(solution)/shard_map/psum | solution.py:17
  51.1 1.1 fusion.37
  52.5 105.4 %all-to-all-done = bf16[2,8,16,32,512]{4,3,1,0,2:T(8,128)(2,1)} async-done(((bf16[2,8,16,32,512]{4,3,1,0,2:T(8,128)(2,1)}), bf16[2,8,16,32,512]{4,3,1,0,2:T(8,128)(2,1)}, u32[]{:S(2)}, u32[]{:S(2)}) %all-to-all-start) | async-done | bytes 8388640 | tf_op jit(solution)/shard_map/all_to_all | solution.py:92
  157.9 8.4 %copy.95 = bf16[2,8,16,32,512]{4,3,2,1,0:T(8,128)(2,1)} copy(bf16[2,8,16,32,512]{4,3,1,0,2:T(8,128)(2,1)} %all-to-all-done) | data formatting | bytes 16777216 | tf_op jit(solution)/shard_map/all_to_all | solution.py:92
  166.4 8.2 %gather_fusion.5 = bf16[16,2,8,32,512]{4,3,2,1,0:T(8,128)(2,1)} fusion(bf16[2,8,16,32,512]{4,3,2,1,0:T(8,128)(2,1)} %copy.95, s32[1024]{0:T(1024)S(1)} %pad_clamp_fusion), kind=kCustom, calls=%fused_computation.1.clone | custom fusion | bytes 16777280 | tf_op jit(solution)/shard_map/jit(_take)/gather | solution.py:91
  174.6 7.8 %bitcast_select_fusion.1 = bf16[2,8,16,32,512]{4,3,1,0,2:T(8,128)(2,1)} fusion(bf16[16,2,8,32,512]{4,3,2,1,0:T(8,128)(2,1)} %gather_fusion.5, pred[16]{0:T(512)(128)(4,1)S(1)} %compare_and_fusion.5, pred[]{:T(512)S(6)} %eq.130), kind=kLoop, calls=%fused_computation.11 | loop fusion | flops 8388608 | bytes 16777232 | tf_op jit(solution)/shard_map/jit(_where)/select_n | solution.py:17
  182.3 8.3 %copy.96 = bf16[2,8,16,32,512]{4,3,2,1,0:T(8,128)(2,1)} copy(bf16[2,8,16,32,512]{4,3,1,0,2:T(8,128)(2,1)} %bitcast_select_fusion.1) | data formatting | bytes 16777216 | tf_op jit(solution)/shard_map/jit(_where)/select_n | solution.py:17
  191.9 56.8 %all-reduce = (f32[2,512]{1,0:T(2,128)S(1)}, f32[24]{0:T(128)S(1)}, f32[24]{0:T(128)S(1)}, f32[3072]{0:T(1024)S(1)}) all-reduce(f32[2,512]{1,0:T(2,128)S(1)} %bitcast.110, f32[24]{0:T(128)S(1)} %reduce_sum.97, f32[24]{0:T(128)S(1)} %reduce_sum.95, f32[3072]{0:T(1024)S(1)} %bitcast.108), channel_id=1, replica_groups=mesh['inst'=4,'ctx'=16,'head'=2] {'ctx'}, use_global_device_ids=true, to_apply=%region_11.12 | all-reduce | flops 4144 | bytes 33152 | tf_op jit(solution)/shard_map/psum | solution.py:138
  250.4 1.1 multiply_bitcast_fusion
  251.7 113.9 %all-reduce.6.cloned.1.call-done = bf16[2,8,512,512]{3,2,1,0:T(8,128)(2,1)} async-done(((bf16[2,8,512,512]{3,2,1,0:T(8,128)(2,1)}), bf16[2,8,512,512]{3,2,1,0:T(8,128)(2,1)}) %all-reduce.6.cloned.1.call-update) | async-done | bytes 8388624 | tf_op jit(solution)/shard_map/psum | solution.py:17
  365.6 5.9 gather_fusion.2
  371.5 2.3 select_bitcast_fusion.1
  373.8 2.1 copy.97
  375.8 6.5 gather_fusion.3
  382.3 7.0 %fusion.3 = bf16[2,8,512,512]{3,2,0,1:T(8,128)(2,1)S(1)} fusion(bf16[2,8,512,512]{3,2,1,0:T(8,128)(2,1)} %param.12, bf16[8,2,512,512]{3,2,1,0:T(8,128)(2,1)} %gather_fusion.3, pred[8]{0:T(512)(128)(4,1)S(1)} %compare_and_fusion.8, pred[8]{0:T(512)(128)(4,1)S(1)} %fusion.29, pred[8,512]{1,0:T(8,128)(4,1)S(1)} %get-tuple-element.43, ...), kind=kLoop, calls=%fused_computation.10 | loop fusion | flops 25165824 | bytes 25231376 | tf_op jit(solution)/shard_map/jit(_where)/select_n | solution.py:161
  389.4 3.8 fusion.41
  393.2 2.0 copy-done.2
  395.2 6.5 copy.100
  401.6 3.1 fusion.42
  404.7 60.4 %pmax.7 = f32[3,8,4,6]{3,0,2,1:T(4,128)S(1)} all-reduce(f32[3,8,4,6]{3,0,2,1:T(4,128)S(1)} %get-tuple-element.49), channel_id=1, replica_groups=mesh['inst'=4,'ctx'=16,'head'=2] {'ctx'}, use_global_device_ids=true, to_apply=%region_19.21 | all-reduce | flops 576 | bytes 4608 | tf_op jit(solution)/shard_map/pmax | solution.py:171
  465.7 55.9 %psum.79 = bf16[3,8,4,6]{3,0,2,1:T(4,128)(2,1)S(1)} all-reduce(bf16[3,8,4,6]{3,0,2,1:T(4,128)(2,1)S(1)} %fusion.4), channel_id=1, replica_groups=mesh['inst'=4,'ctx'=16,'head'=2] {'ctx'}, use_global_device_ids=true, to_apply=%region_22.24 | all-reduce | flops 576 | bytes 2304 | tf_op jit(solution)/shard_map/psum | solution.py:180
  521.6 6.4 copy.99
  528.0 4.1 fusion.6
  532.2 105.1 %all-reduce.8.cloned.1.call-done = bf16[3,8,4,6,128]{4,3,0,2,1:T(8,128)(2,1)} async-done(((bf16[3,8,4,6,128]{4,3,0,2,1:T(8,128)(2,1)}), bf16[3,8,4,6,128]{4,3,0,2,1:T(8,128)(2,1)}) %all-reduce.8.cloned.1.call-update) | async-done | bytes 147472 | tf_op jit(solution)/shard_map/psum | solution.py:181
  637.4 1.1 divide_convert_fusion
  638.6 2.1 convolution_convert_fusion.1
  641.5 7.7 %copy.106 = bf16[2,8,512,512]{3,2,1,0:T(8,128)(2,1)} copy(bf16[2,8,512,512]{3,2,0,1:T(8,128)(2,1)} %copy-done.2) | data formatting | bytes 16777216
  649.1 3.6 reduce-scatter.4.cloned.1.call-done
  652.8 1.5 copy.115
  (94 shorter events, 8.9 us)
Async XLA Ops:
  7.2 43.9 %copy-start = (bf16[384,3072]{1,0:T(8,128)(2,1)S(1)}, bf16[384,3072]{1,0:T(8,128)(2,1)}, u32[]{:S(2)}) copy-start(bf16[384,3072]{1,0:T(8,128)(2,1)} %param.15) | copy-start | bytes 7077892
  24.2 8.7 %copy-start.7 = (s32[8]{0:T(128)S(1)}, s32[8]{0:T(128)}, u32[]{:S(2)}) copy-start(s32[8]{0:T(128)} %param.19) | copy-start | bytes 100
  24.2 8.9 %copy-start.6 = (s32[32]{0:T(128)S(1)}, s32[32]{0:T(128)}, u32[]{:S(2)}) copy-start(s32[32]{0:T(128)} %param.18) | copy-start | bytes 388
  24.2 9.0 %copy-start.5 = (bf16[384]{0:T(512)(128)(2,1)S(1)}, bf16[384]{0:T(512)(128)(2,1)}, u32[]{:S(2)}) copy-start(bf16[384]{0:T(512)(128)(2,1)} %param.14) | copy-start | bytes 2308
  24.2 9.0 %copy-start.4 = (bf16[3,8,384]{2,1,0:T(8,128)(2,1)S(1)}, bf16[3,8,384]{2,1,0:T(8,128)(2,1)}, u32[]{:S(2)}) copy-start(bf16[3,8,384]{2,1,0:T(8,128)(2,1)} %param.13) | copy-start | bytes 55300
  24.2 24.9 %copy-start.8 = (s32[8]{0:T(128)S(1)}, s32[8]{0:T(128)}, u32[]{:S(2)}) copy-start(s32[8]{0:T(128)} %param.20) | copy-start | bytes 100
  24.2 26.0 %copy-start.3 = (bf16[2,384,512]{2,1,0:T(8,128)(2,1)S(1)}, bf16[2,384,512]{2,1,0:T(8,128)(2,1)}, u32[]{:S(2)}) copy-start(bf16[2,384,512]{2,1,0:T(8,128)(2,1)} %param.16) | copy-start | bytes 2359300
  24.3 133.7 %all-to-all-start = ((bf16[2,8,16,32,512]{4,3,1,0,2:T(8,128)(2,1)}), bf16[2,8,16,32,512]{4,3,1,0,2:T(8,128)(2,1)}, u32[]{:S(2)}, u32[]{:S(2)}) async-start(bf16[2,8,16,32,512]{4,3,1,0,2:T(8,128)(2,1)} %select_bitcast_fusion), calls=%async_computation | async-start | bytes 16777216 | tf_op jit(solution)/shard_map/all_to_all | solution.py:92
  32.9 216.2 %all-reduce.10.cloned.1.call-start = ((), (), s32[]{:S(2)}) async-start(), calls=%async_computation.5 | async-start | bytes 786432 | tf_op jit(solution)/shard_map/psum | solution.py:138
  52.2 313.4 %all-reduce.6.cloned.1.call-start = ((), (), s32[]{:S(2)}) async-start(), calls=%async_computation.2 | async-start | bytes 16777216 | tf_op jit(solution)/shard_map/psum | solution.py:17
  190.6 446.8 %all-reduce.8.cloned.1.call-start = ((), (), s32[]{:S(2)}) async-start(), calls=%async_computation.3 | async-start | bytes 393216 | tf_op jit(solution)/shard_map/psum | solution.py:181
  389.4 5.8 copy-start.2
  532.2 120.6 %reduce-scatter.4.cloned.1.call-start = ((), (), s32[]{:S(2)}) async-start(), calls=%async_computation.4 | async-start | bytes 147456
  641.4 12.8 %copy-start.1 = (bf16[384,3072]{1,0:T(8,128)(2,1)S(1)}, bf16[384,3072]{1,0:T(8,128)(2,1)}, u32[]{:S(2)}) copy-start(bf16[384,3072]{1,0:T(8,128)(2,1)} %param.15) | copy-start | bytes 7077892
Sparse Core Ops, SparseCore 0:
  52.3 149.9 all-reduce.9
  204.8 160.7 all-reduce.5
  532.3 105.0 all-reduce.7
  641.6 11.1 reduce-scatter.3
where the time goes:
time: 662 us; the launch traced here: 661 us
  waiting for transfers between devices  328 us (50%)
  blocking collectives  188 us (28%)
  local copies, waits for them, and re-layouts  79.1 us (12%)
  other arithmetic  30.5 us (5%)
  between operations  14.1 us (2%)
  matrix products  11.9 us (2%)
  starting transfers between devices  8.79 us (1%)
    psum x1, waiting for transfers between devices, spread(): return lax.psum(jnp.where(mine, x, jnp.zeros_like(x)), axis)  114 us
    all_to_all x1, waiting for transfers between devices, shards(): lax.all_to_all(jnp.take(cache.reshape(2, slot_count, ctx_count, block_len...  105 us
    psum x1, waiting for transfers between devices, shards(): lax.psum(partial_out.astype(jnp.bfloat16), 'ctx').astype(jnp.float32)  105 us
    pmax x1, blocking collectives, shards(): peak = lax.pmax(jnp.max(masked, axis=-1), 'ctx')  60.4 us
    psum x1, blocking collectives, shards(): lax.psum((part_sum, part_sq, part_query, part_keyval, gain_query, gain_ke...  56.8 us
    psum x1, blocking collectives, shards(): lax.psum(jnp.sum(weights, axis=-1).astype(jnp.bfloat16), 'ctx')  55.9 us
    psum x1, blocking collectives, spread(): return lax.psum(jnp.where(mine, x, jnp.zeros_like(x)), axis)  15.1 us
  transfers between devices with their start and end apart: 5, of which 4 were waited for; matrix products, arithmetic and copies ran while one was open for 7% of the time, Pallas kernels for 0%

commit v1 on v0

v1 whole, which is shorter than its diff:
```python
import functools

import jax
import jax.numpy as jnp
from jax import lax
from jax.experimental import pallas as pl
from jax.experimental.pallas import tpu as pltpu
from jax.sharding import PartitionSpec as P

MODEL_WIDTH = 6144
HEAD_SIZE = 128
ROPE_BASE = 500000.0
NORM_EPSILON = 1e-05
MASKED_SCORE = -1e30

INST = 4
CTX = 16
SLOTS = 8
STEPS = 3
MOVED = 3
BLOCK = 32
RANGE = 512
FEATURES = 512
HALF_ROWS = 48
STAT_ROW = 40
CHUNKS = 4
BF16 = jnp.bfloat16
F32 = jnp.float32
I32 = jnp.int32

NEW_LEN, STAYS, REQUEST = 0, 8, 16
VALID, SLOT, LENGTH, COUNT = 24, 28, 32, 36
STORED, LOGICAL = 48, 64
NEED = 80
SOURCE, TARGET = 128, 256
PLAN_SIZE = 384
LIST = 64

VMEM = pl.BlockSpec(memory_space=pltpu.VMEM)
SMEM = pl.BlockSpec(memory_space=pltpu.SMEM)
ANY = pl.BlockSpec(memory_space=pl.ANY)


def params(**more):
    return pltpu.CompilerParams(vmem_limit_bytes=60 * 1024 * 1024, **more)


def plan_kernel(ids, lengths, dest_inst, dest_slot, order, plan):
    inst = ids[0]
    ctx = ids[1]

    def clear(p, carry):
        plan[SOURCE + p] = 0
        plan[TARGET + p] = -1
        return carry

    lax.fori_loop(0, 2 * LIST, clear, 0)
    for s in range(SLOTS):
        own = jnp.where(inst == INST - 1, 0, lengths[inst * SLOTS + s])
        plan[NEW_LEN + s] = own
        plan[STAYS + s] = jnp.where(own > 0, 1, 0)
        plan[REQUEST + s] = -1
    for j in range(4):
        plan[VALID + j] = 0
        plan[SLOT + j] = 0
        plan[LENGTH + j] = 0
        plan[COUNT + j] = 0
    for b in range(CTX):
        q = order[ctx * CTX + b]
        plan[STORED + lax.shift_right_logical(q, 4)] = b
        plan[LOGICAL + lax.shift_right_logical(q, 4)] = q

    counts = []
    total = [jnp.int32(0)] * 3
    for r in range(SLOTS):
        long = lengths[(INST - 1) * SLOTS + r]
        count = lax.shift_right_logical(long + STEPS + RANGE - 1, 9)
        counts.append(count)
        to = dest_inst[r]
        total = [total[i] + jnp.where(to == i, count, 0) for i in range(3)]
    split = jnp.clip(lax.shift_right_arithmetic(total[2] + total[1] - total[0] + 1, 1), 0, total[1])
    rest = total[1] - split
    plan[NEED] = jnp.maximum(split + total[0], rest + total[2])
    plan[NEED + 1] = jnp.maximum(split, rest)

    done = [jnp.int32(0)] * 3
    rank = [jnp.int32(0)] * 3
    for r in range(SLOTS):
        to = dest_inst[r]
        count = counts[r]
        base = jnp.where(to == 0, done[0], jnp.where(to == 1, done[1], done[2]))
        place = jnp.where(to == 0, rank[0], jnp.where(to == 1, rank[1], rank[2]))

        def put(c, carry, r=r, to=to, base=base, place=place):
            e = base + c
            by_zero = jnp.logical_or(to == 0, jnp.logical_and(to == 1, e < split))
            p = jnp.where(
                to == 0,
                split + e,
                jnp.where(to == 2, LIST + rest + e, jnp.where(e < split, e, LIST + e - split)),
            )
            plan[SOURCE + p] = r * CTX + c
            plan[TARGET + p] = to * 64 + place * CTX + c
            return carry

        lax.fori_loop(0, count, put, 0)

        @pl.when(to == inst)
        def _(r=r, place=place, count=count):
            long = lengths[(INST - 1) * SLOTS + r]
            slot = dest_slot[r]
            plan[NEW_LEN + slot] = long
            plan[STAYS + slot] = 0
            plan[REQUEST + slot] = r
            plan[VALID + place] = jnp.where(long > 0, 1, 0)
            plan[SLOT + place] = slot
            plan[LENGTH + place] = long
            plan[COUNT + place] = count

        done = [done[i] + jnp.where(to == i, count, 0) for i in range(3)]
        rank = [rank[i] + jnp.where(to == i, 1, 0) for i in range(3)]


def make_plan(ids, lengths, dest_inst, dest_slot, order):
    return pl.pallas_call(
        plan_kernel,
        out_shape=jax.ShapeDtypeStruct((PLAN_SIZE,), I32),
        in_specs=[SMEM] * 5,
        out_specs=SMEM,
        name="plan",
    )(ids, lengths, dest_inst, dest_slot, order)


def pack_kernel(chunk, items, ids, plan, cache, up, down, sem):
    @pl.when(ids[0] == INST - 1)
    def _():
        for way, out in enumerate((up, down)):

            def send(i, carry, way=way, out=out):
                code = plan[SOURCE + way * LIST + chunk * items + i]
                r = lax.shift_right_logical(code, 4)
                stored = plan[STORED + lax.bitwise_and(code, 15)]
                rows = pl.ds(pl.multiple_of(stored * BLOCK, BLOCK), BLOCK)
                pltpu.make_async_copy(cache.at[:, r, rows, :], out.at[i], sem.at[way]).start()
                return carry

            lax.fori_loop(0, items, send, 0)
        for way, out in enumerate((up, down)):
            pltpu.make_async_copy(out, out, sem.at[way]).wait()


def pack(chunk, items, ids, plan, cache):
    shape = jax.ShapeDtypeStruct((items, 2, BLOCK, FEATURES), BF16)
    return pl.pallas_call(
        functools.partial(pack_kernel, chunk, items),
        out_shape=[shape, shape],
        in_specs=[SMEM, SMEM, ANY],
        out_specs=[VMEM, VMEM],
        scratch_shapes=[pltpu.SemaphoreType.DMA((2,))],
        cost_estimate=pl.CostEstimate(
            flops=0, bytes_accessed=8 * items * BLOCK * FEATURES * 2, transcendentals=0
        ),
        compiler_params=params(),
        name="pack",
    )(ids, plan, cache)


def to_lanes(column, rows):
    shape = (rows, 128)
    same = lax.broadcasted_iota(I32, shape, 0) == lax.broadcasted_iota(I32, shape, 1)
    return jnp.sum(jnp.where(same, column, 0.0), axis=0, keepdims=True)


def to_rows(lanes, rows):
    shape = (rows, 128)
    same = lax.broadcasted_iota(I32, shape, 0) == lax.broadcasted_iota(I32, shape, 1)
    return jnp.sum(jnp.where(same, lanes, 0.0), axis=1, keepdims=True)


def project_kernel(plan, hidden, by0, by1, by2, gain, w_query, w_kv, out, lhs, stats):
    step = pl.program_id(0)

    @pl.when(step == 0)
    def _():
        row = lax.broadcasted_iota(I32, (SLOTS, 1), 0)
        request = jnp.full((SLOTS, 1), -1, I32)
        for s in range(SLOTS):
            request = jnp.where(row == s, plan[REQUEST + s], request)
        scale = gain[...].astype(F32)
        sums = []
        squares = []
        for t in range(STEPS):
            x = hidden[t].astype(F32)
            moved = by0[t].astype(F32) + by1[t].astype(F32) + by2[t].astype(F32)
            for r in range(SLOTS):
                x = jnp.where(request == r, moved[r : r + 1, :], x)
            sums.append(jnp.sum(x, axis=1, keepdims=True))
            squares.append(jnp.sum(x * x, axis=1, keepdims=True))
            lhs[t * SLOTS : (t + 1) * SLOTS, :] = x * scale
        lhs[24:32, :] = jnp.where(row == 0, scale, 0.0)
        sum_lanes = to_lanes(jnp.concatenate(sums, axis=0), 24)
        square_lanes = to_lanes(jnp.concatenate(squares, axis=0), 24)
        stats[...] = jnp.where(row == 1, sum_lanes, jnp.where(row == 2, square_lanes, 0.0))

    left = lhs[...].astype(BF16)
    tail = stats[...]
    row = lax.broadcasted_iota(I32, (SLOTS, 256), 0)
    wide = jnp.concatenate([tail, tail], axis=1)

    def store(o, weight):
        got = jnp.dot(left, weight, preferred_element_type=F32)
        out[o, 0:24, :] = got[0:24]
        out[o, 24:32, :] = jnp.where(row == 0, got[24:32], wide)

    @pl.when(step < 3)
    def _():
        for o in range(4):
            store(o, w_query[:, o * 256 : (o + 1) * 256])

    @pl.when(step == 3)
    def _():
        for o in range(4):
            store(o, w_kv[o // 2, :, (o % 2) * 256 : (o % 2 + 1) * 256])


def project(plan, hidden, by, gain, w_query, w_kv):
    def whole(*shape):
        return pl.BlockSpec(shape, lambda i: (0,) * len(shape))

    small = whole(3, 8, 384)
    return pl.pallas_call(
        project_kernel,
        out_shape=jax.ShapeDtypeStruct((CTX, 32, 256), F32),
        grid=(4,),
        in_specs=[SMEM, small, small, small, small, whole(1, 384)]
        + [
            pl.BlockSpec((384, 1024), lambda i: (0, jnp.minimum(i, 2))),
            whole(2, 384, 512),
        ],
        out_specs=pl.BlockSpec((4, 32, 256), lambda i: (i, 0, 0)),
        scratch_shapes=[pltpu.VMEM((32, 384), F32), pltpu.VMEM((8, 128), F32)],
        cost_estimate=pl.CostEstimate(
            flops=2 * 32 * 384 * 4096, bytes_accessed=384 * 4096 * 2, transcendentals=0
        ),
        compiler_params=params(),
        name="project",
    )(plan, hidden, *by, gain, w_query, w_kv)


def rotate_kernel(parts, cosine, sine, out):
    total = parts[0]
    for d in range(1, CTX):
        total = total + parts[d]
    row = total[24:32]
    mean = to_rows(row[1:2, :128], 24) / MODEL_WIDTH
    square = to_rows(row[2:3, :128], 24) / MODEL_WIDTH
    scale = lax.rsqrt(square - mean * mean + NORM_EPSILON)
    value = scale * (total[0:24] - mean * row[0:1])
    for h in range(2):
        part = value[:, h * 128 : (h + 1) * 128]
        turned = part * cosine[...] + pltpu.roll(part, 64, 1) * sine[...]
        turned = turned.astype(BF16)
        for d in range(CTX):
            out[d, h] = turned


def rotate(parts, cosine, sine):
    return pl.pallas_call(
        rotate_kernel,
        out_shape=jax.ShapeDtypeStruct((CTX, 2, 24, 128), BF16),
        in_specs=[VMEM] * 3,
        out_specs=VMEM,
        compiler_params=params(),
        name="rotate",
    )(parts, cosine, sine)


def attend(keys, values, query, position, length):
    rows = 2 * HALF_ROWS
    row = lax.broadcasted_iota(I32, (rows, 128), 0)
    high = row >= HALF_ROWS
    within = jnp.where(high, row - HALF_ROWS, row)
    group = jnp.where(high, 2, 0) + jnp.where(within >= 18, 1, 0)
    q = query.astype(F32)
    wide = jnp.concatenate([jnp.where(group == g, q, 0.0) for g in range(4)], axis=1).astype(BF16)
    score = lax.dot_general(
        wide, keys, (((1,), (1,)), ((), ())), preferred_element_type=F32
    ) * (HEAD_SIZE ** -0.5)
    line = lax.broadcasted_iota(I32, (rows, 1), 0)
    line = jnp.where(line >= HALF_ROWS, line - HALF_ROWS, line)
    visible = position <= length + lax.rem(line, STEPS)
    masked = jnp.where(visible, score, MASKED_SCORE)
    peak = jnp.max(masked, axis=1, keepdims=True)
    weight = jnp.where(visible, jnp.exp(masked - peak), 0.0)
    total = jnp.sum(weight, axis=1, keepdims=True)
    mixed = jnp.dot(weight.astype(BF16), values, preferred_element_type=F32)
    out = jnp.zeros((rows, 128), F32)
    for g in range(4):
        out = out + jnp.where(group == g, mixed[:, g * 128 : (g + 1) * 128], 0.0)
    return [
        message(
            out[h * HALF_ROWS : (h + 1) * HALF_ROWS],
            peak[h * HALF_ROWS : (h + 1) * HALF_ROWS],
            total[h * HALF_ROWS : (h + 1) * HALF_ROWS],
        )
        for h in range(2)
    ]


def message(out, peak, total):
    peak = to_lanes(peak, HALF_ROWS)
    total = to_lanes(total, HALF_ROWS)
    parts = []
    for value, count in ((peak, 3), (total, 2)):
        for _ in range(count):
            part = value.astype(BF16).astype(F32)
            parts.append(part)
            value = value - part
    row = lax.broadcasted_iota(I32, (HALF_ROWS, 128), 0)
    for i, part in enumerate(parts):
        out = jnp.where(row == STAT_ROW + i, part, out)
    return out.astype(BF16)


def blank_message():
    row = lax.broadcasted_iota(I32, (HALF_ROWS, 128), 0)
    return jnp.where(row == STAT_ROW, MASKED_SCORE, 0.0).astype(BF16)


def stay_kernel(ids, plan, cache, query, entries, new_cache, sums):
    s = pl.program_id(0)
    base = ids[1] * RANGE
    length = plan[NEW_LEN + s]
    stays = plan[STAYS + s] > 0
    some = jnp.logical_and(stays, base < length + STEPS)
    full = jnp.logical_and(some, base + RANGE <= length)

    @pl.when(full)
    def _():
        new_cache[...] = cache[...]

    @pl.when(jnp.logical_and(some, jnp.logical_not(full)))
    def _():
        at = base + lax.broadcasted_iota(I32, (RANGE, 1), 0)
        for kv in range(2):
            block = jnp.where(at < length, cache[kv, 0], jnp.zeros((), BF16))
            for t in range(STEPS):
                block = jnp.where(at == length + t, entries[0, kv, t : t + 1, :], block)
            new_cache[kv, 0] = block

    @pl.when(some)
    def _():
        position = base + lax.broadcasted_iota(I32, (1, RANGE), 1)
        halves = attend(new_cache[0, 0], new_cache[1, 0], query[0], position, length)
        for h in range(2):
            sums[0, h] = halves[h]

    @pl.when(jnp.logical_not(some))
    def _():
        new_cache[...] = jnp.zeros_like(new_cache)
        for h in range(2):
            sums[0, h] = blank_message()


def stay(ids, plan, cache, query, entries):
    return pl.pallas_call(
        stay_kernel,
        out_shape=[
            jax.ShapeDtypeStruct(cache.shape, BF16),
            jax.ShapeDtypeStruct((SLOTS, 2, HALF_ROWS, 128), BF16),
        ],
        grid=(SLOTS,),
        in_specs=[
            SMEM,
            SMEM,
            pl.BlockSpec((2, 1, RANGE, FEATURES), lambda s: (0, s, 0, 0)),
            pl.BlockSpec((1, 2 * HALF_ROWS, 128), lambda s: (s, 0, 0)),
            pl.BlockSpec((1, 2, 8, FEATURES), lambda s: (s, 0, 0, 0)),
        ],
        out_specs=[
            pl.BlockSpec((2, 1, RANGE, FEATURES), lambda s: (0, s, 0, 0)),
            pl.BlockSpec((1, 2, HALF_ROWS, 128), lambda s: (s, 0, 0, 0)),
        ],
        cost_estimate=pl.CostEstimate(
            flops=0, bytes_accessed=32 * 1024 * 1024, transcendentals=0
        ),
        compiler_params=params(),
        name="stay",
    )(ids, plan, cache, query, entries)


def moved_kernel(items, ids, plan, query, entries, sums, *refs):
    count = 4 * CHUNKS - 2
    arrived, (held, new_sums, sem) = refs[:count], refs[count:]
    straight = (arrived[:CHUNKS], arrived[CHUNKS : 2 * CHUNKS])
    onward = (arrived[2 * CHUNKS : 3 * CHUNKS - 1], arrived[3 * CHUNKS - 1 :])
    inst = ids[0]

    def fetch(way, chunk, ref, target):
        def one(i, carry):
            code = plan[TARGET + way * LIST + chunk * items + i]
            inside = lax.bitwise_and(code, 63)

            @pl.when(lax.shift_right_arithmetic(code, 6) == target)
            def _():
                place = lax.shift_right_logical(inside, 4)
                c = lax.bitwise_and(inside, 15)
                pltpu.make_async_copy(ref.at[i], held.at[c, place], sem).start()

            return carry

        lax.fori_loop(0, items, one, 0)

    for way, target in ((0, 0), (1, 2)):

        @pl.when(inst == target)
        def _(way=way, target=target):
            for chunk in range(CHUNKS):
                fetch(way, chunk, straight[way][chunk], target)

    @pl.when(inst == 1)
    def _():
        for way in range(2):
            for chunk in range(CHUNKS - 1):
                fetch(way, chunk, onward[way][chunk], 1)

    new_sums[...] = sums[...]

    @pl.when(inst < INST - 1)
    def _():
        for j in range(MOVED):

            def fill(c, carry, j=j):
                pltpu.make_async_copy(arrived[0].at[0], held.at[c, j], sem).start()
                return carry

            lax.fori_loop(plan[COUNT + j], CTX, fill, 0)
        pltpu.make_async_copy(held, held, sem).wait()

    for j in range(MOVED):

        @pl.when(plan[VALID + j] > 0)
        def _(j=j):
            slot = plan[SLOT + j]
            length = plan[LENGTH + j]
            lane = lax.broadcasted_iota(I32, (1, RANGE), 1)
            position = jnp.zeros((1, RANGE), I32)
            at = lax.broadcasted_iota(I32, (BLOCK, 1), 0)
            for c in range(CTX):
                start = plan[LOGICAL + c] * BLOCK
                position = jnp.where(
                    lax.shift_right_logical(lane, 5) == c, start + lane - c * BLOCK, position
                )

                @pl.when(start + BLOCK > length)
                def _(c=c, start=start):
                    for kv in range(2):
                        block = jnp.where(start + at < length, held[c, j, kv], jnp.zeros((), BF16))
                        new = entries[slot, kv]
                        for t in range(STEPS):
                            block = jnp.where(start + at == length + t, new[t : t + 1, :], block)
                        held[c, j, kv] = block

            keys = held[:, j, 0].reshape(RANGE, FEATURES)
            values = held[:, j, 1].reshape(RANGE, FEATURES)
            halves = attend(keys, values, query[slot], position, length)
            for h in range(2):
                new_sums[slot, h] = halves[h]


def attend_moved(items, ids, plan, query, entries, sums, arrived):
    return pl.pallas_call(
        functools.partial(moved_kernel, items),
        out_shape=[
            jax.ShapeDtypeStruct((CTX, MOVED, 2, BLOCK, FEATURES), BF16),
            jax.ShapeDtypeStruct(sums.shape, BF16),
        ],
        in_specs=[SMEM, SMEM, VMEM, VMEM, VMEM] + [ANY] * len(arrived),
        out_specs=[VMEM, VMEM],
        scratch_shapes=[pltpu.SemaphoreType.DMA(())],
        cost_estimate=pl.CostEstimate(
            flops=0, bytes_accessed=16 * 1024 * 1024, transcendentals=0
        ),
        compiler_params=params(),
        name="moved",
    )(ids, plan, query, entries, sums, *arrived)


def merge_kernel(parts, out):
    blocks = [parts[d].astype(F32) for d in range(CTX)]
    peaks = []
    totals = []
    for block in blocks:
        stat = block[STAT_ROW : STAT_ROW + 8]
        peaks.append(stat[0:1] + stat[1:2] + stat[2:3])
        totals.append(stat[3:4] + stat[4:5])
    peak = functools.reduce(jnp.maximum, peaks)
    factors = [jnp.exp(p - peak) for p in peaks]
    total = functools.reduce(jnp.add, [f * t for f, t in zip(factors, totals)])
    under = to_rows(jnp.where(total > 0, total, 1.0), HALF_ROWS)
    mixed = functools.reduce(
        jnp.add, [to_rows(f, HALF_ROWS) * b for f, b in zip(factors, blocks)]
    )
    attended = (mixed / under).astype(BF16)
    for d in range(CTX):
        out[d] = attended


def merge(parts):
    return pl.pallas_call(
        merge_kernel,
        out_shape=jax.ShapeDtypeStruct(parts.shape, BF16),
        in_specs=[VMEM],
        out_specs=VMEM,
        compiler_params=params(),
        name="merge",
    )(parts)


def place_kernel(plan, within, received, cache, new_cache, held, read_sem, write_sem):
    for j in range(MOVED):

        @pl.when(plan[VALID + j] > 0)
        def _(j=j):
            def one(d, carry):
                rows = pl.ds(pl.multiple_of(within[d] * BLOCK, BLOCK), BLOCK)
                pltpu.make_async_copy(
                    received.at[d, j], held.at[j, :, rows, :], read_sem.at[j]
                ).start()
                return carry

            lax.fori_loop(0, CTX, one, 0)

    for j in range(MOVED):

        @pl.when(plan[VALID + j] > 0)
        def _(j=j):
            pltpu.make_async_copy(held.at[j], held.at[j], read_sem.at[j]).wait()
            pltpu.make_async_copy(
                held.at[j], new_cache.at[:, plan[SLOT + j]], write_sem.at[j]
            ).start()

    for j in range(MOVED):

        @pl.when(plan[VALID + j] > 0)
        def _(j=j):
            pltpu.make_async_copy(
                held.at[j], new_cache.at[:, plan[SLOT + j]], write_sem.at[j]
            ).wait()


def place(plan, within, received, cache):
    return pl.pallas_call(
        place_kernel,
        out_shape=jax.ShapeDtypeStruct(cache.shape, BF16),
        in_specs=[SMEM, SMEM, ANY, ANY],
        out_specs=ANY,
        scratch_shapes=[
            pltpu.VMEM((MOVED, 2, RANGE, FEATURES), BF16),
            pltpu.SemaphoreType.DMA((MOVED,)),
            pltpu.SemaphoreType.DMA((MOVED,)),
        ],
        input_output_aliases={3: 0},
        compiler_params=params(),
        name="place",
    )(plan, within, received, cache)


def swap(x):
    return lax.all_to_all(x, "ctx", split_axis=0, concat_axis=0, tiled=True)


def after(*values):
    return lax.optimization_barrier(values)


def shards(
    cache,
    hidden,
    norm_gain,
    w_query,
    key_value_weight,
    w_out,
    lengths,
    dest_inst,
    dest_slot,
    block_order,
):
    instance = lax.axis_index("inst")
    context = lax.axis_index("ctx")
    head = lax.axis_index("head")
    ids = jnp.stack([instance, context]).astype(I32)
    by = [lax.ppermute(hidden, "inst", [(INST - 1, i)]) for i in range(INST - 1)]
    plan = make_plan(ids, lengths, dest_inst, dest_slot, block_order)
    by, plan = after(by, plan)
    layout = block_order.reshape(CTX, CTX)
    within = jnp.sum(jnp.where(layout // CTX == context, layout % CTX, 0), axis=1)
    new_len = plan[NEW_LEN : NEW_LEN + SLOTS]
    token = new_len[None, :] + jnp.arange(STEPS, dtype=I32)[:, None]
    half = HEAD_SIZE // 2
    frequency = ROPE_BASE ** (-jnp.arange(half, dtype=F32) * 2.0 / HEAD_SIZE)
    angles = token.astype(F32).reshape(24, 1) * frequency
    is_value = context >= 14
    cosine = jnp.where(is_value, 1.0, jnp.cos(angles))
    sine = jnp.where(is_value, 0.0, jnp.sin(angles))
    cosine = jnp.concatenate([cosine, cosine], axis=1)
    sine = jnp.concatenate([-sine, sine], axis=1)

    items = LIST // CHUNKS
    up, down, up_on, down_on = [], [], [], []

    def send(chunk, plan):
        one, two = pack(chunk, items, ids, plan, cache)
        up.append(lax.ppermute(one, "inst", [(INST - 1, 0)]))
        down.append(lax.ppermute(two, "inst", [(INST - 1, 2)]))
        if chunk < CHUNKS - 1:
            up_on.append(lax.ppermute(up[-1], "inst", [(0, 1)]))
            down_on.append(lax.ppermute(down[-1], "inst", [(2, 1)]))
        return one

    send(0, plan)
    packed = send(1, plan)
    hidden, cosine, sine, within, packed = after(hidden, cosine, sine, within, packed)
    parts = swap(project(plan, hidden, by, norm_gain[None], w_query, key_value_weight))
    parts, plan_2 = after(parts, plan)
    packed = send(2, plan_2)
    parts, packed = after(parts, packed)
    turned = swap(rotate(parts, cosine, sine))
    turned, plan_3 = after(turned, plan)
    packed = send(3, plan_3)
    turned, packed = after(turned, packed)
    turned = turned.reshape(32, STEPS, SLOTS, HEAD_SIZE)
    query = turned[:24].reshape(2, 12, STEPS, SLOTS, HEAD_SIZE).transpose(3, 0, 1, 2, 4)
    query = query.reshape(SLOTS, 2, 36, HEAD_SIZE)
    query = jnp.pad(query, ((0, 0), (0, 0), (0, HALF_ROWS - 36), (0, 0)))
    query = query.reshape(SLOTS, 2 * HALF_ROWS, HEAD_SIZE)
    entries = turned[24:].reshape(2, 4, STEPS, SLOTS, HEAD_SIZE).transpose(3, 0, 2, 1, 4)
    entries = entries.reshape(SLOTS, 2, STEPS, FEATURES)
    entries = jnp.pad(entries, ((0, 0), (0, 0), (0, 8 - STEPS), (0, 0)))
    query, entries, up_on[0], down_on[0] = after(query, entries, up_on[0], down_on[0])

    new_cache, sums = stay(ids, plan, cache, query, entries)
    held, sums = attend_moved(
        items, ids, plan, query, entries, sums, up + down + up_on + down_on
    )
    received = swap(held)
    received, sums = after(received, sums)
    attended = swap(merge(swap(sums.reshape(CTX, HALF_ROWS, HEAD_SIZE))))
    new_cache = place(plan, within, received, new_cache)

    attended = attended[:, :36].reshape(SLOTS, 2, 12, STEPS, HEAD_SIZE)
    attended = attended.transpose(3, 0, 1, 2, 4).reshape(24, 24 * HEAD_SIZE)
    projected = jnp.dot(attended, w_out, preferred_element_type=F32)
    mine, other = projected[:, :192], projected[:, 192:]
    first = head == 0
    keep = jnp.where(first, mine, other)
    send = jnp.where(first, other, mine).astype(BF16)
    got = lax.ppermute(send, "head", [(0, 1), (1, 0)])
    attn_out = (keep + got.astype(F32)).astype(BF16)
    return new_cache, attn_out.reshape(STEPS, SLOTS, 192)


def solution(mesh):
    placed = (
        P(None, "inst", "ctx", "head"),
        P(None, "inst", "ctx"),
        P("ctx"),
        P("ctx", "head"),
        P(None, "ctx", "head"),
        P("head", "ctx"),
        P(),
        P(),
        P(),
        P(),
    )
    return jax.shard_map(
        shards,
        mesh=mesh,
        in_specs=placed,
        out_specs=(P(None, "inst", "ctx", "head"), P(None, "inst", ("ctx", "head"))),
        check_vma=False,
    )
```

time: 662 us -> 231 us (0.35)
  the two profiles are of different devices: /device:TPU:1 before, /device:TPU:9 now
where the time goes in v1:
time: 231 us; the launch traced here: 228 us
  blocking collectives  72.4 us (31%)
  waiting for transfers between devices  63.1 us (27%)
  Pallas kernels  41.9 us (18%)
  starting transfers between devices  36.6 us (16%)
  local copies, waits for them, and re-layouts  9.21 us (4%)
  other arithmetic  2.86 us (1%)
    all_to_all x3, blocking collectives, swap(): return lax.all_to_all(x, 'ctx', split_axis=0, concat_axis=0, tiled=True)  72.4 us
    ppermute x3, waiting for transfers between devices, send(): down_on.append(lax.ppermute(down[-1], 'inst', [(2, 1)]))  33.9 us
    ppermute x3, waiting for transfers between devices, send(): up_on.append(lax.ppermute(up[-1], 'inst', [(0, 1)]))  16.5 us
    all_to_all x2, waiting for transfers between devices, swap(): return lax.all_to_all(x, 'ctx', split_axis=0, concat_axis=0, tiled=True)  12.7 us
    pallas_call x1, Pallas kernels, stay(): pl.pallas_call(stay_kernel, out_shape=[jax.ShapeDtypeStruct(cache.shape,...  10.7 us
    pallas_call x4, Pallas kernels, pack(): pl.pallas_call(functools.partial(pack_kernel, chunk, items), out_shape=[s...  8.34 us
    all_to_all x2, starting transfers between devices, swap(): return lax.all_to_all(x, 'ctx', split_axis=0, concat_axis=0, tiled=True)  7.69 us
    pallas_call x1, Pallas kernels, attend_moved(): pl.pallas_call(functools.partial(moved_kernel, items), out_shape=[jax.Sha...  7.54 us
  transfers between devices with their start and end apart: 20, of which 6 were waited for; matrix products, arithmetic and copies ran while one was open for 4% of the time, Pallas kernels for 12%

profile of v1, /device:TPU:9, one launch (start us, length us, event | category | flops | bytes accessed | tf_op | source)
XLA Modules:
  0.0 227.6 jit_solution(15652931095837526586)
XLA Ops:
  0.6 1.4 collective-permute-start.1
  6.7 3.6 %plan.1 = s32[384]{0:T(512)} custom-call(s32[2]{0:T(128)} %pad_add_fusion.ids, s32[32]{0:T(128)} %lengths.1, s32[8]{0:T(128)} %dest_inst.1, s32[8]{0:T(128)} %dest_slot.1, s32[256]{0:T(256)} %order.1), custom_call_target="tpu_custom_call" | custom-call | tf_op jit(solution)/shard_map/plan/pallas_call | solution.py:125
  10.4 2.0 pack.7
  12.5 2.2 pack.4
  15.4 1.6 collective-permute-start.5
  17.0 1.6 collective-permute-start.10
  18.7 1.6 collective-permute-start.7
  21.2 4.3 %project.1 = f32[16,32,256]{2,1,0:T(8,128)} custom-call(s32[384]{0:T(512)} %plan.1, bf16[3,8,384]{2,1,0:T(8,128)(2,1)} %hidden, bf16[3,8,384]{2,1,0:T(8,128)(2,1)} %copy-done.7, bf16[3,8,384]{2,1,0:T(8,128)(2,1)} %copy-done.6, bf16[3,8,384]{2,1,0:T(8,128)(2,1)} %copy-done.8, bf16[1,384]{1,0:T(2,128)(2,1)} %broadcast_in_dim.17.gain, ...), custom_call_target="tpu_custom_call" | custom-call | flops 100663296 | bytes 3145728 | tf_op jit(solution)/shard_map/project/pallas_call | solution.py:231
  25.5 18.2 %all_to_all.25.parts = f32[16,32,256]{2,1,0:T(8,128)} all-to-all(f32[16,32,256]{2,1,0:T(8,128)} %project.1), channel_id=1, replica_groups=mesh['inst'=4,'ctx'=16,'head'=2] {'ctx'}, dimensions={0} | all-to-all | bytes 1048576 | tf_op jit(solution)/shard_map/all_to_all | solution.py:570
  43.7 2.0 pack.5
  45.7 1.9 rotate.1
  47.7 4.2 %all-to-all-start.1 = ((bf16[16,2,24,128]{3,2,1,0:T(8,128)(2,1)}), bf16[16,2,24,128]{3,2,1,0:T(8,128)(2,1)}, u32[]{:S(2)}, u32[]{:S(2)}) async-start(bf16[16,2,24,128]{3,2,1,0:T(8,128)(2,1)} %rotate.1), calls=%async_computation.1 | async-start | bytes 393216 | tf_op jit(solution)/shard_map/all_to_all | solution.py:570
  51.9 1.7 collective-permute-start.11
  53.5 5.5 %all-to-all-done.1 = bf16[16,2,24,128]{3,2,1,0:T(8,128)(2,1)} async-done(((bf16[16,2,24,128]{3,2,1,0:T(8,128)(2,1)}), bf16[16,2,24,128]{3,2,1,0:T(8,128)(2,1)}, u32[]{:S(2)}, u32[]{:S(2)}) %all-to-all-start.1) | async-done | bytes 196640 | tf_op jit(solution)/shard_map/all_to_all | solution.py:570
  59.1 2.1 pack.6
  61.2 1.7 collective-permute-start.8
  63.6 1.3 collective-permute-start.4
  66.2 1.6 collective-permute-start.9
  70.5 16.5 %collective-permute-done.4.refs_8_ = bf16[16,2,32,512]{3,2,1,0:T(8,128)(2,1)S(1)} collective-permute-done((bf16[16,2,32,512]{3,2,1,0:T(8,128)(2,1)S(1)}, bf16[16,2,32,512]{3,2,1,0:T(8,128)(2,1)S(1)}, u32[]{:S(2)}, u32[]{:S(2)}) %collective-permute-start.4) | collective-permute-done | bytes 1048608 | tf_op jit(solution)/shard_map/ppermute | solution.py:617
  88.3 5.7 %collective-permute-done.6.refs_11_ = bf16[16,2,32,512]{3,2,1,0:T(8,128)(2,1)S(1)} collective-permute-done((bf16[16,2,32,512]{3,2,1,0:T(8,128)(2,1)}, bf16[16,2,32,512]{3,2,1,0:T(8,128)(2,1)S(1)}, u32[]{:S(2)}, u32[]{:S(2)}) %collective-permute-start.6) | collective-permute-done | bytes 1048608 | tf_op jit(solution)/shard_map/ppermute | solution.py:618
  98.7 1.5 reshape.68
  102.3 10.7 %stay.1 = (bf16[2,8,512,512]{3,2,1,0:T(8,128)(2,1)}, bf16[8,2,48,128]{3,2,1,0:T(8,128)(2,1)}) custom-call(s32[2]{0:T(128)} %pad_add_fusion.ids, s32[384]{0:T(512)} %plan.1, bf16[2,8,512,512]{3,2,1,0:T(8,128)(2,1)} %cache.9, bf16[8,96,128]{2,1,0:T(8,128)(2,1)} %bitcast.23, bf16[8,2,8,512]{3,2,1,0:T(8,128)(2,1)} %pad.9.entries), custom_call_target="tpu_custom_call" | custom-call | bytes 33554432 | tf_op jit(solution)/shard_map/stay/pallas_call | solution.py:366
  113.1 4.4 %collective-permute-done.15.refs_12_ = bf16[16,2,32,512]{3,2,1,0:T(8,128)(2,1)} collective-permute-done((bf16[16,2,32,512]{3,2,1,0:T(8,128)(2,1)}, bf16[16,2,32,512]{3,2,1,0:T(8,128)(2,1)}, u32[]{:S(2)}, u32[]{:S(2)}) %collective-permute-start.15) | collective-permute-done | bytes 1048608 | tf_op jit(solution)/shard_map/ppermute | solution.py:618
  117.5 23.7 %collective-permute-done.16.refs_13_ = bf16[16,2,32,512]{3,2,1,0:T(8,128)(2,1)} collective-permute-done((bf16[16,2,32,512]{3,2,1,0:T(8,128)(2,1)}, bf16[16,2,32,512]{3,2,1,0:T(8,128)(2,1)}, u32[]{:S(2)}, u32[]{:S(2)}) %collective-permute-start.16) | collective-permute-done | bytes 1048608 | tf_op jit(solution)/shard_map/ppermute | solution.py:618
  141.2 7.5 %moved.1 = (bf16[16,3,2,32,512]{4,3,2,1,0:T(8,128)(2,1)}, bf16[8,2,48,128]{3,2,1,0:T(8,128)(2,1)}) custom-call(s32[2]{0:T(128)} %pad_add_fusion.ids, s32[384]{0:T(512)} %plan.1, bf16[8,96,128]{2,1,0:T(8,128)(2,1)} %bitcast.24, bf16[8,2,8,512]{3,2,1,0:T(8,128)(2,1)} %pad.9.entries, bf16[8,2,48,128]{3,2,1,0:T(8,128)(2,1)} %get-tuple-element.55.sums, ...), custom_call_target="tpu_custom_call" | custom-call | bytes 16777216 | tf_op jit(solution)/shard_map/moved/pallas_call | solution.py:472
  148.8 43.7 %all_to_all.26.received = bf16[16,3,2,32,512]{4,3,2,1,0:T(8,128)(2,1)} all-to-all(bf16[16,3,2,32,512]{4,3,2,1,0:T(8,128)(2,1)} %get-tuple-element.61), channel_id=1, replica_groups=mesh['inst'=4,'ctx'=16,'head'=2] {'ctx'}, dimensions={0} | all-to-all | bytes 6291456 | tf_op jit(solution)/shard_map/all_to_all | solution.py:570
  192.5 10.5 %all_to_all.27.parts = bf16[16,48,128]{2,1,0:T(8,128)(2,1)} all-to-all(bf16[16,48,128]{2,1,0:T(8,128)(2,1)S(1)} %bitcast.28), channel_id=1, replica_groups=mesh['inst'=4,'ctx'=16,'head'=2] {'ctx'}, dimensions={0} | all-to-all | bytes 393216 | tf_op jit(solution)/shard_map/all_to_all | solution.py:570
  203.0 1.8 merge.1
  204.8 3.5 %all-to-all-start.4 = ((bf16[16,48,128]{2,1,0:T(8,128)(2,1)}), bf16[16,48,128]{2,1,0:T(8,128)(2,1)S(1)}, u32[]{:S(2)}, u32[]{:S(2)}) async-start(bf16[16,48,128]{2,1,0:T(8,128)(2,1)} %merge.1), calls=%async_computation.4 | async-start | bytes 393216 | tf_op jit(solution)/shard_map/all_to_all | solution.py:570
  208.3 7.1 %all-to-all-done.4 = bf16[16,48,128]{2,1,0:T(8,128)(2,1)S(1)} async-done(((bf16[16,48,128]{2,1,0:T(8,128)(2,1)}), bf16[16,48,128]{2,1,0:T(8,128)(2,1)S(1)}, u32[]{:S(2)}, u32[]{:S(2)}) %all-to-all-start.4) | async-done | bytes 196640 | tf_op jit(solution)/shard_map/all_to_all | solution.py:570
  216.1 7.1 %collective-permute-start.17 = (bf16[24,192]{1,0:T(8,128)(2,1)S(1)}, bf16[24,192]{1,0:T(8,128)(2,1)S(1)}, u32[]{:S(2)}, u32[]{:S(2)}) collective-permute-start(bf16[24,192]{1,0:T(8,128)(2,1)S(1)} %select_convert_fusion), channel_id=1, source_target_pairs={{0,1},{1,0},{2,3},{3,2},{4,5},{5,4},{6,7},{7,6},{8,9},{9,8},{10,11... | collective-permute-start | bytes 27656 | tf_op jit(solution)/shard_map/ppermute | solution.py:658
  223.2 3.7 %place.1 = bf16[2,8,512,512]{3,2,1,0:T(8,128)(2,1)} custom-call(s32[384]{0:T(512)} %plan.1, s32[16]{0:T(128)} %fusion.5.within, bf16[16,3,2,32,512]{4,3,2,1,0:T(8,128)(2,1)} %all_to_all.26.received, bf16[2,8,512,512]{3,2,1,0:T(8,128)(2,1)} %get-tuple-element.64.cache), custom_call_target="tpu_custom_call", output_to_operand_aliasing={{}: (3, {})} | custom-call | tf_op jit(solution)/shard_map/place/pallas_call | solution.py:553
  (65 shorter events, 20.3 us)
Async XLA Ops:
  0.6 214.9 %copy-start = (bf16[3072,384]{1,0:T(8,128)(2,1)S(1)}, bf16[3072,384]{1,0:T(8,128)(2,1)}, u32[]{:S(2)}) copy-start(bf16[3072,384]{1,0:T(8,128)(2,1)} %param.15) | copy-start | bytes 7077892
  0.6 9.7 %collective-permute-start.1 = (bf16[3,8,384]{2,1,0:T(8,128)(2,1)}, bf16[3,8,384]{2,1,0:T(8,128)(2,1)S(1)}, u32[]{:S(2)}, u32[]{:S(2)}) collective-permute-start(bf16[3,8,384]{2,1,0:T(8,128)(2,1)} %hidden), channel_id=1, source_target_pairs={{96,32},{97,33},{98,34},{99,35},{100,36},{101,37},{102,38},{103,39... | collective-permute-start | bytes 55304 | tf_op jit(solution)/shard_map/ppermute | solution.py:593
  2.1 8.3 %collective-permute-start = (bf16[3,8,384]{2,1,0:T(8,128)(2,1)}, bf16[3,8,384]{2,1,0:T(8,128)(2,1)S(1)}, u32[]{:S(2)}, u32[]{:S(2)}) collective-permute-start(bf16[3,8,384]{2,1,0:T(8,128)(2,1)} %hidden), channel_id=1, source_target_pairs={{96,0},{97,1},{98,2},{99,3},{100,4},{101,5},{102,6},{103,7},{104,8... | collective-permute-start | bytes 55304 | tf_op jit(solution)/shard_map/ppermute | solution.py:593
  2.7 7.6 %collective-permute-start.2 = (bf16[3,8,384]{2,1,0:T(8,128)(2,1)}, bf16[3,8,384]{2,1,0:T(8,128)(2,1)S(1)}, u32[]{:S(2)}, u32[]{:S(2)}) collective-permute-start(bf16[3,8,384]{2,1,0:T(8,128)(2,1)} %hidden), channel_id=1, source_target_pairs={{96,64},{97,65},{98,66},{99,67},{100,68},{101,69},{102,70},{103,71... | collective-permute-start | bytes 55304 | tf_op jit(solution)/shard_map/ppermute | solution.py:593
  10.3 2.1 copy-start.6
  10.4 2.1 copy-start.7
  10.4 2.1 copy-start.8
  12.5 7.8 %slice-start = ((s32[384]{0:T(512)}), s32[8]{0:T(128)S(1)}, s32[]{:S(2)}) async-start(s32[384]{0:T(512)} %plan.1), calls=%async_computation.5 | async-start | bytes 1024 | tf_op jit(solution)/shard_map/slice | solution.py:598
  14.6 46.5 %collective-permute-start.3 = (bf16[16,2,32,512]{3,2,1,0:T(8,128)(2,1)}, bf16[16,2,32,512]{3,2,1,0:T(8,128)(2,1)S(1)}, u32[]{:S(2)}, u32[]{:S(2)}) collective-permute-start(bf16[16,2,32,512]{3,2,1,0:T(8,128)(2,1)} %get-tuple-element.51), channel_id=1, source_target_pairs={{96,0},{97,1},{98,2},{99,3},{100,4},{101,5},{102,6},{103,7},{104,8... | collective-permute-start | bytes 3145736 | tf_op jit(solution)/shard_map/ppermute | solution.py:614
  15.4 47.5 %collective-permute-start.5 = (bf16[16,2,32,512]{3,2,1,0:T(8,128)(2,1)}, bf16[16,2,32,512]{3,2,1,0:T(8,128)(2,1)}, u32[]{:S(2)}, u32[]{:S(2)}) collective-permute-start(bf16[16,2,32,512]{3,2,1,0:T(8,128)(2,1)} %get-tuple-element.52), channel_id=1, source_target_pairs={{96,64},{97,65},{98,66},{99,67},{100,68},{101,69},{102,70},{103,71... | collective-permute-start | bytes 3145736 | tf_op jit(solution)/shard_map/ppermute | solution.py:615
  17.0 46.6 %collective-permute-start.10 = (bf16[16,2,32,512]{3,2,1,0:T(8,128)(2,1)}, bf16[16,2,32,512]{3,2,1,0:T(8,128)(2,1)}, u32[]{:S(2)}, u32[]{:S(2)}) collective-permute-start(bf16[16,2,32,512]{3,2,1,0:T(8,128)(2,1)} %get-tuple-element.56), channel_id=1, source_target_pairs={{96,64},{97,65},{98,66},{99,67},{100,68},{101,69},{102,70},{103,71... | collective-permute-start | bytes 3145736 | tf_op jit(solution)/shard_map/ppermute | solution.py:615
  18.7 46.2 %collective-permute-start.7 = (bf16[16,2,32,512]{3,2,1,0:T(8,128)(2,1)}, bf16[16,2,32,512]{3,2,1,0:T(8,128)(2,1)}, u32[]{:S(2)}, u32[]{:S(2)}) collective-permute-start(bf16[16,2,32,512]{3,2,1,0:T(8,128)(2,1)} %get-tuple-element.35), channel_id=1, source_target_pairs={{96,0},{97,1},{98,2},{99,3},{100,4},{101,5},{102,6},{103,7},{104,8... | collective-permute-start | bytes 3145736 | tf_op jit(solution)/shard_map/ppermute | solution.py:614
  47.7 11.4 %all-to-all-start.1 = ((bf16[16,2,24,128]{3,2,1,0:T(8,128)(2,1)}), bf16[16,2,24,128]{3,2,1,0:T(8,128)(2,1)}, u32[]{:S(2)}, u32[]{:S(2)}) async-start(bf16[16,2,24,128]{3,2,1,0:T(8,128)(2,1)} %rotate.1), calls=%async_computation.1 | async-start | bytes 393216 | tf_op jit(solution)/shard_map/all_to_all | solution.py:570
  51.9 14.4 %collective-permute-start.11 = (bf16[16,2,32,512]{3,2,1,0:T(8,128)(2,1)}, bf16[16,2,32,512]{3,2,1,0:T(8,128)(2,1)}, u32[]{:S(2)}, u32[]{:S(2)}) collective-permute-start(bf16[16,2,32,512]{3,2,1,0:T(8,128)(2,1)} %get-tuple-element.57), channel_id=1, source_target_pairs={{96,64},{97,65},{98,66},{99,67},{100,68},{101,69},{102,70},{103,71... | collective-permute-start | bytes 3145736 | tf_op jit(solution)/shard_map/ppermute | solution.py:615
  61.2 51.9 %copy-start.1 = (bf16[16,2,32,512]{3,2,1,0:T(8,128)(2,1)}, bf16[16,2,32,512]{3,2,1,0:T(8,128)(2,1)S(1)}, u32[]{:S(2)}) copy-start(bf16[16,2,32,512]{3,2,1,0:T(8,128)(2,1)S(1)} %collective-permute-done.3.refs_0_) | copy-start | bytes 3145732
  61.2 6.7 %collective-permute-start.8 = (bf16[16,2,32,512]{3,2,1,0:T(8,128)(2,1)}, bf16[16,2,32,512]{3,2,1,0:T(8,128)(2,1)}, u32[]{:S(2)}, u32[]{:S(2)}) collective-permute-start(bf16[16,2,32,512]{3,2,1,0:T(8,128)(2,1)} %get-tuple-element.43), channel_id=1, source_target_pairs={{96,0},{97,1},{98,2},{99,3},{100,4},{101,5},{102,6},{103,7},{104,8... | collective-permute-start | bytes 3145736 | tf_op jit(solution)/shard_map/ppermute | solution.py:614
  62.9 6.3 %collective-permute-start.12 = (bf16[16,2,32,512]{3,2,1,0:T(8,128)(2,1)}, bf16[16,2,32,512]{3,2,1,0:T(8,128)(2,1)S(1)}, u32[]{:S(2)}, u32[]{:S(2)}) collective-permute-start(bf16[16,2,32,512]{3,2,1,0:T(8,128)(2,1)} %get-tuple-element.58), channel_id=1, source_target_pairs={{96,64},{97,65},{98,66},{99,67},{100,68},{101,69},{102,70},{103,71... | collective-permute-start | bytes 3145736 | tf_op jit(solution)/shard_map/ppermute | solution.py:615
  63.6 23.4 %collective-permute-start.4 = (bf16[16,2,32,512]{3,2,1,0:T(8,128)(2,1)S(1)}, bf16[16,2,32,512]{3,2,1,0:T(8,128)(2,1)S(1)}, u32[]{:S(2)}, u32[]{:S(2)}) collective-permute-start(bf16[16,2,32,512]{3,2,1,0:T(8,128)(2,1)S(1)} %collective-permute-done.3.refs_0_), channel_id=1, source_target_pairs={{0,32},{1,33},{2,34},{3,35},{4,36},{5,37},{6,38},{7,39},{8,40},{9,... | collective-permute-start | bytes 3145736 | tf_op jit(solution)/shard_map/ppermute | solution.py:617
  64.9 29.1 %collective-permute-start.6 = (bf16[16,2,32,512]{3,2,1,0:T(8,128)(2,1)}, bf16[16,2,32,512]{3,2,1,0:T(8,128)(2,1)S(1)}, u32[]{:S(2)}, u32[]{:S(2)}) collective-permute-start(bf16[16,2,32,512]{3,2,1,0:T(8,128)(2,1)} %collective-permute-done.5.refs_4_), channel_id=1, source_target_pairs={{64,32},{65,33},{66,34},{67,35},{68,36},{69,37},{70,38},{71,39},{7... | collective-permute-start | bytes 3145736 | tf_op jit(solution)/shard_map/ppermute | solution.py:618
  66.2 46.9 %collective-permute-start.9 = (bf16[16,2,32,512]{3,2,1,0:T(8,128)(2,1)}, bf16[16,2,32,512]{3,2,1,0:T(8,128)(2,1)}, u32[]{:S(2)}, u32[]{:S(2)}) collective-permute-start(bf16[16,2,32,512]{3,2,1,0:T(8,128)(2,1)} %get-tuple-element.49), channel_id=1, source_target_pairs={{96,0},{97,1},{98,2},{99,3},{100,4},{101,5},{102,6},{103,7},{104,8... | collective-permute-start | bytes 3145736 | tf_op jit(solution)/shard_map/ppermute | solution.py:614
  67.9 49.6 %collective-permute-start.15 = (bf16[16,2,32,512]{3,2,1,0:T(8,128)(2,1)}, bf16[16,2,32,512]{3,2,1,0:T(8,128)(2,1)}, u32[]{:S(2)}, u32[]{:S(2)}) collective-permute-start(bf16[16,2,32,512]{3,2,1,0:T(8,128)(2,1)} %collective-permute-done.10.refs_5_), channel_id=1, source_target_pairs={{64,32},{65,33},{66,34},{67,35},{68,36},{69,37},{70,38},{71,39},{7... | collective-permute-start | bytes 3145736 | tf_op jit(solution)/shard_map/ppermute | solution.py:618
  69.2 17.8 %copy-start.2 = (bf16[16,2,32,512]{3,2,1,0:T(8,128)(2,1)}, bf16[16,2,32,512]{3,2,1,0:T(8,128)(2,1)S(1)}, u32[]{:S(2)}) copy-start(bf16[16,2,32,512]{3,2,1,0:T(8,128)(2,1)S(1)} %collective-permute-done.12.refs_7_) | copy-start | bytes 3145732
  69.2 48.3 %collective-permute-start.13 = (bf16[16,2,32,512]{3,2,1,0:T(8,128)(2,1)}, bf16[16,2,32,512]{3,2,1,0:T(8,128)(2,1)}, u32[]{:S(2)}, u32[]{:S(2)}) collective-permute-start(bf16[16,2,32,512]{3,2,1,0:T(8,128)(2,1)} %collective-permute-done.7.refs_1_), channel_id=1, source_target_pairs={{0,32},{1,33},{2,34},{3,35},{4,36},{5,37},{6,38},{7,39},{8,40},{9,... | collective-permute-start | bytes 3145736 | tf_op jit(solution)/shard_map/ppermute | solution.py:617
  87.0 1.3 copy-start.3
  87.0 54.2 %collective-permute-start.16 = (bf16[16,2,32,512]{3,2,1,0:T(8,128)(2,1)}, bf16[16,2,32,512]{3,2,1,0:T(8,128)(2,1)}, u32[]{:S(2)}, u32[]{:S(2)}) collective-permute-start(bf16[16,2,32,512]{3,2,1,0:T(8,128)(2,1)} %collective-permute-done.11.refs_6_), channel_id=1, source_target_pairs={{64,32},{65,33},{66,34},{67,35},{68,36},{69,37},{70,38},{71,39},{7... | collective-permute-start | bytes 3145736 | tf_op jit(solution)/shard_map/ppermute | solution.py:618
  94.0 1.0 copy-start.4
  95.0 46.2 %collective-permute-start.14 = (bf16[16,2,32,512]{3,2,1,0:T(8,128)(2,1)}, bf16[16,2,32,512]{3,2,1,0:T(8,128)(2,1)}, u32[]{:S(2)}, u32[]{:S(2)}) collective-permute-start(bf16[16,2,32,512]{3,2,1,0:T(8,128)(2,1)} %collective-permute-done.8.refs_2_), channel_id=1, source_target_pairs={{0,32},{1,33},{2,34},{3,35},{4,36},{5,37},{6,38},{7,39},{8,40},{9,... | collective-permute-start | bytes 3145736 | tf_op jit(solution)/shard_map/ppermute | solution.py:617
  148.8 43.7 %copy-start.5 = (bf16[8,2,48,128]{3,2,1,0:T(8,128)(2,1)S(1)}, bf16[8,2,48,128]{3,2,1,0:T(8,128)(2,1)}, u32[]{:S(2)}) copy-start(bf16[8,2,48,128]{3,2,1,0:T(8,128)(2,1)} %get-tuple-element.65) | copy-start | bytes 589828
  204.8 10.7 %all-to-all-start.4 = ((bf16[16,48,128]{2,1,0:T(8,128)(2,1)}), bf16[16,48,128]{2,1,0:T(8,128)(2,1)S(1)}, u32[]{:S(2)}, u32[]{:S(2)}) async-start(bf16[16,48,128]{2,1,0:T(8,128)(2,1)} %merge.1), calls=%async_computation.4 | async-start | bytes 393216 | tf_op jit(solution)/shard_map/all_to_all | solution.py:570
  216.1 10.8 %collective-permute-start.17 = (bf16[24,192]{1,0:T(8,128)(2,1)S(1)}, bf16[24,192]{1,0:T(8,128)(2,1)S(1)}, u32[]{:S(2)}, u32[]{:S(2)}) collective-permute-start(bf16[24,192]{1,0:T(8,128)(2,1)S(1)} %select_convert_fusion), channel_id=1, source_target_pairs={{0,1},{1,0},{2,3},{3,2},{4,5},{5,4},{6,7},{7,6},{8,9},{9,8},{10,11... | collective-permute-start | bytes 27656 | tf_op jit(solution)/shard_map/ppermute | solution.py:658

commit v2 on v1

--- a/solution.py
+++ b/solution.py
@@ -23,31 +23,33 @@
 FEATURES = 512
 HALF_ROWS = 48
 STAT_ROW = 40
-CHUNKS = 4
+CHUNKS = 2
+ITEMS = (12, 15, 18, 21, 24, 28, 33)
 BF16 = jnp.bfloat16
 F32 = jnp.float32
 I32 = jnp.int32
 
 NEW_LEN, STAYS, REQUEST = 0, 8, 16
 VALID, SLOT, LENGTH, COUNT = 24, 28, 32, 36
-STORED, LOGICAL = 48, 64
-NEED = 80
-SOURCE, TARGET = 128, 256
-PLAN_SIZE = 384
-LIST = 64
+STORED, LOGICAL, WITHIN = 48, 64, 80
+NEED = 96
+SOURCE, TARGET = 128, 272
+PLAN_SIZE = 416
+LIST = 72
 
 VMEM = pl.BlockSpec(memory_space=pltpu.VMEM)
 SMEM = pl.BlockSpec(memory_space=pltpu.SMEM)
 ANY = pl.BlockSpec(memory_space=pl.ANY)
-
-
-def params(**more):
-    return pltpu.CompilerParams(vmem_limit_bytes=60 * 1024 * 1024, **more)
-
-
-def plan_kernel(ids, lengths, dest_inst, dest_slot, order, plan):
-    inst = ids[0]
-    ctx = ids[1]
+HBM = pl.BlockSpec(memory_space=pltpu.HBM)
+
+
+def params(mib):
+    return pltpu.CompilerParams(vmem_limit_bytes=mib * 1024 * 1024)
+
+
+def plan_kernel(lengths, dest_inst, dest_slot, order, plan):
+    inst = lax.axis_index("inst")
+    ctx = lax.axis_index("ctx")
 
     def clear(p, carry):
         plan[SOURCE + p] = 0
@@ -70,6 +72,17 @@
         plan[STORED + lax.shift_right_logical(q, 4)] = b
         plan[LOGICAL + lax.shift_right_logical(q, 4)] = q
 
+    def search(d, carry):
+        found = jnp.int32(0)
+        for b in range(CTX):
+            q = order[d * CTX + b]
+            mine = lax.shift_right_logical(q, 4) == ctx
+            found = jnp.where(mine, lax.bitwise_and(q, CTX - 1), found)
+        plan[WITHIN + d] = found
+        return carry
+
+    lax.fori_loop(0, CTX, search, 0)
+
     counts = []
     total = [jnp.int32(0)] * 3
     for r in range(SLOTS):
@@ -78,10 +91,21 @@
         counts.append(count)
         to = dest_inst[r]
         total = [total[i] + jnp.where(to == i, count, 0) for i in range(3)]
-    split = jnp.clip(lax.shift_right_arithmetic(total[2] + total[1] - total[0] + 1, 1), 0, total[1])
+    def weigh(part, best):
+        rest = total[1] - part
+        cost = jnp.maximum(
+            lax.shift_right_logical(jnp.maximum(part + total[0], rest + total[2]) + 1, 1),
+            jnp.maximum(part, rest),
+        )
+        better = cost < best[0]
+        return jnp.where(better, cost, best[0]), jnp.where(better, part, best[1])
+
+    least, split = lax.fori_loop(0, total[1] + 1, weigh, (jnp.int32(1000), jnp.int32(0)))
     rest = total[1] - split
-    plan[NEED] = jnp.maximum(split + total[0], rest + total[2])
-    plan[NEED + 1] = jnp.maximum(split, rest)
+    size = jnp.int32(0)
+    for items in ITEMS[:-1]:
+        size = size + jnp.where(least > items, 1, 0)
+    plan[NEED] = size
 
     done = [jnp.int32(0)] * 3
     rank = [jnp.int32(0)] * 3
@@ -121,18 +145,18 @@
         rank = [rank[i] + jnp.where(to == i, 1, 0) for i in range(3)]
 
 
-def make_plan(ids, lengths, dest_inst, dest_slot, order):
+def make_plan(lengths, dest_inst, dest_slot, order):
     return pl.pallas_call(
         plan_kernel,
         out_shape=jax.ShapeDtypeStruct((PLAN_SIZE,), I32),
-        in_specs=[SMEM] * 5,
+        in_specs=[SMEM] * 4,
         out_specs=SMEM,
         name="plan",
-    )(ids, lengths, dest_inst, dest_slot, order)
-
-
-def pack_kernel(chunk, items, ids, plan, cache, up, down, sem):
-    @pl.when(ids[0] == INST - 1)
+    )(lengths, dest_inst, dest_slot, order)
+
+
+def pack_kernel(chunk, items, plan, cache, up, down, sem):
+    @pl.when(lax.axis_index("inst") == INST - 1)
     def _():
         for way, out in enumerate((up, down)):
 
@@ -149,20 +173,20 @@
             pltpu.make_async_copy(out, out, sem.at[way]).wait()
 
 
-def pack(chunk, items, ids, plan, cache):
+def pack(chunk, items, plan, cache):
     shape = jax.ShapeDtypeStruct((items, 2, BLOCK, FEATURES), BF16)
     return pl.pallas_call(
         functools.partial(pack_kernel, chunk, items),
         out_shape=[shape, shape],
-        in_specs=[SMEM, SMEM, ANY],
+        in_specs=[SMEM, HBM],
         out_specs=[VMEM, VMEM],
         scratch_shapes=[pltpu.SemaphoreType.DMA((2,))],
         cost_estimate=pl.CostEstimate(
             flops=0, bytes_accessed=8 * items * BLOCK * FEATURES * 2, transcendentals=0
         ),
-        compiler_params=params(),
+        compiler_params=params(16),
         name="pack",
-    )(ids, plan, cache)
+    )(plan, cache)
 
 
 def to_lanes(column, rows):
@@ -242,7 +266,7 @@
         cost_estimate=pl.CostEstimate(
             flops=2 * 32 * 384 * 4096, bytes_accessed=384 * 4096 * 2, transcendentals=0
         ),
-        compiler_params=params(),
+        compiler_params=params(12),
         name="project",
     )(plan, hidden, *by, gain, w_query, w_kv)
 
@@ -270,7 +294,7 @@
         out_shape=jax.ShapeDtypeStruct((CTX, 2, 24, 128), BF16),
         in_specs=[VMEM] * 3,
         out_specs=VMEM,
-        compiler_params=params(),
+        compiler_params=params(8),
         name="rotate",
     )(parts, cosine, sine)
 
@@ -327,9 +351,9 @@
     return jnp.where(row == STAT_ROW, MASKED_SCORE, 0.0).astype(BF16)
 
 
-def stay_kernel(ids, plan, cache, query, entries, new_cache, sums):
+def stay_kernel(plan, cache, query, entries, new_cache, sums):
     s = pl.program_id(0)
-    base = ids[1] * RANGE
+    base = lax.axis_index("ctx") * RANGE
     length = plan[NEW_LEN + s]
     stays = plan[STAYS + s] > 0
     some = jnp.logical_and(stays, base < length + STEPS)
@@ -362,7 +386,7 @@
             sums[0, h] = blank_message()
 
 
-def stay(ids, plan, cache, query, entries):
+def stay(plan, cache, query, entries):
     return pl.pallas_call(
         stay_kernel,
         out_shape=[
@@ -371,7 +395,6 @@
         ],
         grid=(SLOTS,),
         in_specs=[
-            SMEM,
             SMEM,
             pl.BlockSpec((2, 1, RANGE, FEATURES), lambda s: (0, s, 0, 0)),
             pl.BlockSpec((1, 2 * HALF_ROWS, 128), lambda s: (s, 0, 0)),
@@ -384,17 +407,17 @@
         cost_estimate=pl.CostEstimate(
             flops=0, bytes_accessed=32 * 1024 * 1024, transcendentals=0
         ),
-        compiler_params=params(),
+        compiler_params=params(24),
         name="stay",
-    )(ids, plan, cache, query, entries)
-
-
-def moved_kernel(items, ids, plan, query, entries, sums, *refs):
+    )(plan, cache, query, entries)
+
+
+def gather_kernel(items, plan, entries, *refs):
     count = 4 * CHUNKS - 2
-    arrived, (held, new_sums, sem) = refs[:count], refs[count:]
+    arrived, (held, sem) = refs[:count], refs[count:]
     straight = (arrived[:CHUNKS], arrived[CHUNKS : 2 * CHUNKS])
     onward = (arrived[2 * CHUNKS : 3 * CHUNKS - 1], arrived[3 * CHUNKS - 1 :])
-    inst = ids[0]
+    inst = lax.axis_index("inst")
 
     def fetch(way, chunk, ref, target):
         def one(i, carry):
@@ -424,8 +447,6 @@
             for chunk in range(CHUNKS - 1):
                 fetch(way, chunk, onward[way][chunk], 1)
 
-    new_sums[...] = sums[...]
-
     @pl.when(inst < INST - 1)
     def _():
         for j in range(MOVED):
@@ -443,17 +464,13 @@
         def _(j=j):
             slot = plan[SLOT + j]
             length = plan[LENGTH + j]
-            lane = lax.broadcasted_iota(I32, (1, RANGE), 1)
-            position = jnp.zeros((1, RANGE), I32)
             at = lax.broadcasted_iota(I32, (BLOCK, 1), 0)
-            for c in range(CTX):
+
+            def cut(c, carry):
                 start = plan[LOGICAL + c] * BLOCK
-                position = jnp.where(
-                    lax.shift_right_logical(lane, 5) == c, start + lane - c * BLOCK, position
-                )
 
                 @pl.when(start + BLOCK > length)
-                def _(c=c, start=start):
+                def _():
                     for kv in range(2):
                         block = jnp.where(start + at < length, held[c, j, kv], jnp.zeros((), BF16))
                         new = entries[slot, kv]
@@ -461,29 +478,55 @@
                             block = jnp.where(start + at == length + t, new[t : t + 1, :], block)
                         held[c, j, kv] = block
 
+                return carry
+
+            lax.fori_loop(0, CTX, cut, 0)
+
+
+def gather(items, plan, entries, arrived):
+    return pl.pallas_call(
+        functools.partial(gather_kernel, items),
+        out_shape=jax.ShapeDtypeStruct((CTX, MOVED, 2, BLOCK, FEATURES), BF16),
+        in_specs=[SMEM, VMEM] + [HBM] * len(arrived),
+        out_specs=VMEM,
+        scratch_shapes=[pltpu.SemaphoreType.DMA(())],
+        cost_estimate=pl.CostEstimate(flops=0, bytes_accessed=8 * 1024 * 1024, transcendentals=0),
+        compiler_params=params(12),
+        name="gather",
+    )(plan, entries, *arrived)
+
+
+def moved_kernel(plan, query, held, sums, new_sums):
+    new_sums[...] = sums[...]
+    lane = lax.broadcasted_iota(I32, (1, RANGE), 1)
+    position = jnp.zeros((1, RANGE), I32)
+    for c in range(CTX):
+        start = plan[LOGICAL + c] * BLOCK
+        position = jnp.where(
+            lax.shift_right_logical(lane, 5) == c, start + lane - c * BLOCK, position
+        )
+    for j in range(MOVED):
+
+        @pl.when(plan[VALID + j] > 0)
+        def _(j=j):
+            slot = plan[SLOT + j]
             keys = held[:, j, 0].reshape(RANGE, FEATURES)
             values = held[:, j, 1].reshape(RANGE, FEATURES)
-            halves = attend(keys, values, query[slot], position, length)
+            halves = attend(keys, values, query[slot], position, plan[LENGTH + j])
             for h in range(2):
                 new_sums[slot, h] = halves[h]
 
 
-def attend_moved(items, ids, plan, query, entries, sums, arrived):
-    return pl.pallas_call(
-        functools.partial(moved_kernel, items),
-        out_shape=[
-            jax.ShapeDtypeStruct((CTX, MOVED, 2, BLOCK, FEATURES), BF16),
-            jax.ShapeDtypeStruct(sums.shape, BF16),
-        ],
-        in_specs=[SMEM, SMEM, VMEM, VMEM, VMEM] + [ANY] * len(arrived),
-        out_specs=[VMEM, VMEM],
-        scratch_shapes=[pltpu.SemaphoreType.DMA(())],
-        cost_estimate=pl.CostEstimate(
-            flops=0, bytes_accessed=16 * 1024 * 1024, transcendentals=0
-        ),
-        compiler_params=params(),
+def attend_moved(plan, query, held, sums):
+    return pl.pallas_call(
+        moved_kernel,
+        out_shape=jax.ShapeDtypeStruct(sums.shape, BF16),
+        in_specs=[SMEM, VMEM, VMEM, VMEM],
+        out_specs=VMEM,
+        cost_estimate=pl.CostEstimate(flops=0, bytes_accessed=12 * 1024 * 1024, transcendentals=0),
+        compiler_params=params(12),
         name="moved",
-    )(ids, plan, query, entries, sums, *arrived)
+    )(plan, query, held, sums)
 
 
 def merge_kernel(parts, out):
@@ -512,18 +555,18 @@
         out_shape=jax.ShapeDtypeStruct(parts.shape, BF16),
         in_specs=[VMEM],
         out_specs=VMEM,
-        compiler_params=params(),
+        compiler_params=params(8),
         name="merge",
     )(parts)
 
 
-def place_kernel(plan, within, received, cache, new_cache, held, read_sem, write_sem):
+def place_kernel(plan, received, cache, new_cache, held, read_sem, write_sem):
     for j in range(MOVED):
 
         @pl.when(plan[VALID + j] > 0)
         def _(j=j):
             def one(d, carry):
-                rows = pl.ds(pl.multiple_of(within[d] * BLOCK, BLOCK), BLOCK)
+                rows = pl.ds(pl.multiple_of(plan[WITHIN + d] * BLOCK, BLOCK), BLOCK)
                 pltpu.make_async_copy(
                     received.at[d, j], held.at[j, :, rows, :], read_sem.at[j]
                 ).start()
@@ -549,21 +592,21 @@
             ).wait()
 
 
-def place(plan, within, received, cache):
+def place(plan, received, cache):
     return pl.pallas_call(
         place_kernel,
         out_shape=jax.ShapeDtypeStruct(cache.shape, BF16),
-        in_specs=[SMEM, SMEM, ANY, ANY],
-        out_specs=ANY,
+        in_specs=[SMEM, ANY, HBM],
+        out_specs=HBM,
         scratch_shapes=[
             pltpu.VMEM((MOVED, 2, RANGE, FEATURES), BF16),
             pltpu.SemaphoreType.DMA((MOVED,)),
             pltpu.SemaphoreType.DMA((MOVED,)),
         ],
-        input_output_aliases={3: 0},
-        compiler_params=params(),
+        input_output_aliases={2: 0},
+        compiler_params=params(12),
         name="place",
-    )(plan, within, received, cache)
+    )(plan, received, cache)
 
 
 def swap(x):
@@ -586,49 +629,47 @@
     dest_slot,
     block_order,
 ):
-    instance = lax.axis_index("inst")
-    context = lax.axis_index("ctx")
-    head = lax.axis_index("head")
-    ids = jnp.stack([instance, context]).astype(I32)
     by = [lax.ppermute(hidden, "inst", [(INST - 1, i)]) for i in range(INST - 1)]
-    plan = make_plan(ids, lengths, dest_inst, dest_slot, block_order)
-    by, plan = after(by, plan)
-    layout = block_order.reshape(CTX, CTX)
-    within = jnp.sum(jnp.where(layout // CTX == context, layout % CTX, 0), axis=1)
+    plan = make_plan(lengths, dest_inst, dest_slot, block_order)
+    *by, plan = after(*by, plan)
+    operands = (plan, cache, hidden, by, norm_gain[None], w_query, key_value_weight, w_out)
+    return lax.switch(
+        plan[NEED], [functools.partial(decode, items) for items in ITEMS], *operands
+    )
+
+
+def angles(plan):
     new_len = plan[NEW_LEN : NEW_LEN + SLOTS]
     token = new_len[None, :] + jnp.arange(STEPS, dtype=I32)[:, None]
     half = HEAD_SIZE // 2
     frequency = ROPE_BASE ** (-jnp.arange(half, dtype=F32) * 2.0 / HEAD_SIZE)
-    angles = token.astype(F32).reshape(24, 1) * frequency
-    is_value = context >= 14
-    cosine = jnp.where(is_value, 1.0, jnp.cos(angles))
-    sine = jnp.where(is_value, 0.0, jnp.sin(angles))
-    cosine = jnp.concatenate([cosine, cosine], axis=1)
-    sine = jnp.concatenate([-sine, sine], axis=1)
-
-    items = LIST // CHUNKS
-    up, down, up_on, down_on = [], [], [], []
-
-    def send(chunk, plan):
-        one, two = pack(chunk, items, ids, plan, cache)
-        up.append(lax.ppermute(one, "inst", [(INST - 1, 0)]))
-        down.append(lax.ppermute(two, "inst", [(INST - 1, 2)]))
-        if chunk < CHUNKS - 1:
-            up_on.append(lax.ppermute(up[-1], "inst", [(0, 1)]))
-            down_on.append(lax.ppermute(down[-1], "inst", [(2, 1)]))
-        return one
-
-    send(0, plan)
-    packed = send(1, plan)
-    hidden, cosine, sine, within, packed = after(hidden, cosine, sine, within, packed)
-    parts = swap(project(plan, hidden, by, norm_gain[None], w_query, key_value_weight))
-    parts, plan_2 = after(parts, plan)
-    packed = send(2, plan_2)
-    parts, packed = after(parts, packed)
+    angle = token.astype(F32).reshape(24, 1) * frequency
+    is_value = lax.axis_index("ctx") >= 14
+    cosine = jnp.where(is_value, 1.0, jnp.cos(angle))
+    sine = jnp.where(is_value, 0.0, jnp.sin(angle))
+    return jnp.concatenate([cosine, cosine], axis=1), jnp.concatenate([-sine, sine], axis=1)
+
+
+def send(items, chunk, plan, cache):
+    one, two = pack(chunk, items, plan, cache)
+    return (
+        lax.ppermute(one, "inst", [(INST - 1, 0)]),
+        lax.ppermute(two, "inst", [(INST - 1, 2)]),
+        one,
+    )
+
+
+def decode(items, plan, cache, hidden, by, gain, w_query, w_kv, w_out):
+    up_0, down_0, packed = send(items, 0, plan, cache)
+    hidden, plan, packed = after(hidden, plan, packed)
+    cosine, sine = angles(plan)
+    projected = project(plan, hidden, by, gain, w_query, w_kv)
+    projected, cosine, sine, plan = after(projected, cosine, sine, plan)
+    up_1, down_1, packed = send(items, 1, plan, cache)
+    parts, up_0, down_0, packed = after(swap(projected), up_0, down_0, packed)
+    up_on = lax.ppermute(up_0, "inst", [(0, 1)])
+    down_on = lax.ppermute(down_0, "inst", [(2, 1)])
     turned = swap(rotate(parts, cosine, sine))
-    turned, plan_3 = after(turned, plan)
-    packed = send(3, plan_3)
-    turned, packed = after(turned, packed)
     turned = turned.reshape(32, STEPS, SLOTS, HEAD_SIZE)
     query = turned[:24].reshape(2, 12, STEPS, SLOTS, HEAD_SIZE).transpose(3, 0, 1, 2, 4)
     query = query.reshape(SLOTS, 2, 36, HEAD_SIZE)
@@ -637,25 +678,25 @@
     entries = turned[24:].reshape(2, 4, STEPS, SLOTS, HEAD_SIZE).transpose(3, 0, 2, 1, 4)
     entries = entries.reshape(SLOTS, 2, STEPS, FEATURES)
     entries = jnp.pad(entries, ((0, 0), (0, 0), (0, 8 - STEPS), (0, 0)))
-    query, entries, up_on[0], down_on[0] = after(query, entries, up_on[0], down_on[0])
-
-    new_cache, sums = stay(ids, plan, cache, query, entries)
-    held, sums = attend_moved(
-        items, ids, plan, query, entries, sums, up + down + up_on + down_on
-    )
-    received = swap(held)
-    received, sums = after(received, sums)
-    attended = swap(merge(swap(sums.reshape(CTX, HALF_ROWS, HEAD_SIZE))))
-    new_cache = place(plan, within, received, new_cache)
+
+    new_cache, sums = stay(plan, cache, query, entries)
+    entries, sums = after(entries, sums)
+    held = gather(items, plan, entries, [up_0, up_1, down_0, down_1, up_on, down_on])
+    sums = attend_moved(plan, query, held, sums)
+    sums, held = after(swap(sums.reshape(CTX, HALF_ROWS, HEAD_SIZE)), held)
+    sums, received = after(sums, swap(held))
+    attended = swap(merge(sums))
+    new_cache = place(plan, received, new_cache)
+    attended, new_cache = after(attended, new_cache)
 
     attended = attended[:, :36].reshape(SLOTS, 2, 12, STEPS, HEAD_SIZE)
     attended = attended.transpose(3, 0, 1, 2, 4).reshape(24, 24 * HEAD_SIZE)
     projected = jnp.dot(attended, w_out, preferred_element_type=F32)
     mine, other = projected[:, :192], projected[:, 192:]
-    first = head == 0
+    first = lax.axis_index("head") == 0
     keep = jnp.where(first, mine, other)
-    send = jnp.where(first, other, mine).astype(BF16)
-    got = lax.ppermute(send, "head", [(0, 1), (1, 0)])
+    send_half = jnp.where(first, other, mine).astype(BF16)
+    got = lax.ppermute(send_half, "head", [(0, 1), (1, 0)])
     attn_out = (keep + got.astype(F32)).astype(BF16)
     return new_cache, attn_out.reshape(STEPS, SLOTS, 192)
 

time: 231 us -> 170 us (0.74)
  the two profiles are of different devices: /device:TPU:9 before, /device:TPU:1 now
where the time goes in v2:
time: 170 us; the launch traced here: 172 us
  blocking collectives  67.5 us (40%)
  Pallas kernels  34.4 us (20%)
  waiting for transfers between devices  33.4 us (20%)
  starting transfers between devices  29.6 us (17%)
  local copies, waits for them, and re-layouts  2.2 us (1%)
  matrix products  2.08 us (1%)
    all_to_all x3, blocking collectives, swap(): return lax.all_to_all(x, 'ctx', split_axis=0, concat_axis=0, tiled=True)  67.5 us
    ppermute x2, waiting for transfers between devices, send(): lax.ppermute(one, 'inst', [(INST - 1, 0)])  24 us
    all_to_all x2, starting transfers between devices, swap(): return lax.all_to_all(x, 'ctx', split_axis=0, concat_axis=0, tiled=True)  11.2 us
    pallas_call x1, Pallas kernels, stay(): pl.pallas_call(stay_kernel, out_shape=[jax.ShapeDtypeStruct(cache.shape,...  10.9 us
    all_to_all x2, waiting for transfers between devices, swap(): return lax.all_to_all(x, 'ctx', split_axis=0, concat_axis=0, tiled=True)  7.53 us
    ppermute x1, starting transfers between devices, decode(): got = lax.ppermute(send_half, 'head', [(0, 1), (1, 0)])  6.24 us
    pallas_call x1, Pallas kernels, make_plan(): pl.pallas_call(plan_kernel, out_shape=jax.ShapeDtypeStruct((PLAN_SIZE,),...  4.64 us
    pallas_call x2, Pallas kernels, pack(): pl.pallas_call(functools.partial(pack_kernel, chunk, items), out_shape=[s...  4.59 us
  transfers between devices with their start and end apart: 12, of which 6 were waited for; matrix products, arithmetic and copies ran while one was open for 1% of the time, Pallas kernels for 15%

profile of v2, /device:TPU:1, one launch (start us, length us, event | category | flops | bytes accessed | tf_op | source)
XLA Modules:
  0.0 172.0 jit_solution(10591215180630241236)
XLA Ops:
  1.3 1.3 collective-permute-start.49
  3.3 0.7 broadcast_in_dim.67
  4.0 4.6 %plan.1 = s32[416]{0:T(512)S(1)} custom-call(s32[32]{0:T(128)} %lengths.1, s32[8]{0:T(128)} %dest_inst.1, s32[8]{0:T(128)} %dest_slot.1, s32[256]{0:T(256)} %order.1), custom_call_target="tpu_custom_call" | custom-call | tf_op jit(solution)/shard_map/plan/pallas_call | solution.py:149
  8.6 1.1 collective-permute-done.49
  10.9 161.1 %conditional.1 = (bf16[2,8,512,512]{3,2,1,0:T(8,128)(2,1)}, bf16[3,8,192]{2,1,0:T(8,128)(2,1)}) conditional(s32[]{:T(128)} %bitcast.77, (s32[416]{0:T(512)S(1)}, bf16[2,8,512,512]{3,2,1,0:T(8,128)(2,1)}, bf16[3,8,384]{2,1,0:T(8,128)(2,1)}, bf16[3,8,384]{2,1,0:T(8,128)(2,1)S(1)}, bf16[3,8,384]{2,1,0:T(8,128)(2,1)S(1)}, ...), branch_computations={%region_0.1_spmd, %region_1.2_spmd, %region_2.3_spmd, %region_3.4_... | conditional | flops 157321904 | bytes 144751184 | solution.py:636
  11.8 2.3 %pack.22 = (bf16[24,2,32,512]{3,2,1,0:T(8,128)(2,1)}, bf16[24,2,32,512]{3,2,1,0:T(8,128)(2,1)}) custom-call(s32[416]{0:T(512)S(1)} %get-tuple-element.284.plan, bf16[2,8,512,512]{3,2,1,0:T(8,128)(2,1)} %get-tuple-element.274.cache), custom_call_target="tpu_custom_call" | custom-call | bytes 6291456 | tf_op jit(solution)/shard_map/cond/branch_4_fun/pack/pallas_call | solution.py:178
  14.1 0.8 collective-permute-start.29
  14.9 1.3 collective-permute-start.28
  16.3 4.0 %project.11 = f32[16,32,256]{2,1,0:T(8,128)} custom-call(s32[416]{0:T(512)S(1)} %get-tuple-element.284.plan, bf16[3,8,384]{2,1,0:T(8,128)(2,1)S(1)} %copy-done.10, bf16[3,8,384]{2,1,0:T(8,128)(2,1)S(1)} %copy-done.18, bf16[3,8,384]{2,1,0:T(8,128)(2,1)S(1)} %get-tuple-element.279.by1, bf16[3,8,384]{2,1,0:T(8,128)(2,1)S(1)} %copy-done.27, ...), custom_call_target="tpu_custom_call" | custom-call | flops 100663296 | bytes 3145728 | tf_op jit(solution)/shard_map/cond/branch_4_fun/project/pallas_call | solution.py:255
  20.5 7.6 %all-to-all-start.20 = ((f32[16,32,256]{2,1,0:T(8,128)}), f32[16,32,256]{2,1,0:T(8,128)S(1)}, u32[]{:S(2)}, u32[]{:S(2)}) async-start(f32[16,32,256]{2,1,0:T(8,128)} %project.11), calls=%async_computation.20 | async-start | bytes 1048576 | tf_op jit(solution)/shard_map/cond/branch_4_fun/all_to_all | solution.py:613
  28.2 2.3 %pack.23 = (bf16[24,2,32,512]{3,2,1,0:T(8,128)(2,1)}, bf16[24,2,32,512]{3,2,1,0:T(8,128)(2,1)}) custom-call(s32[416]{0:T(512)S(1)} %get-tuple-element.284.plan, bf16[2,8,512,512]{3,2,1,0:T(8,128)(2,1)} %get-tuple-element.274.cache), custom_call_target="tpu_custom_call" | custom-call | bytes 6291456 | tf_op jit(solution)/shard_map/cond/branch_4_fun/pack/pallas_call | solution.py:178
  30.5 1.9 %collective-permute-start.31 = (bf16[24,2,32,512]{3,2,1,0:T(8,128)(2,1)}, bf16[24,2,32,512]{3,2,1,0:T(8,128)(2,1)}, u32[]{:S(2)}, u32[]{:S(2)}) collective-permute-start(bf16[24,2,32,512]{3,2,1,0:T(8,128)(2,1)} %get-tuple-element.295), channel_id=1, source_target_pairs={{96,64},{97,65},{98,66},{99,67},{100,68},{101,69},{102,70},{103,71... | collective-permute-start | bytes 4718600 | tf_op jit(solution)/shard_map/cond/branch_4_fun/ppermute | solution.py:657
  32.4 1.3 collective-permute-start.30
  33.7 4.0 %all-to-all-done.20.parts = f32[16,32,256]{2,1,0:T(8,128)S(1)} async-done(((f32[16,32,256]{2,1,0:T(8,128)}), f32[16,32,256]{2,1,0:T(8,128)S(1)}, u32[]{:S(2)}, u32[]{:S(2)}) %all-to-all-start.20) | async-done | bytes 524320 | tf_op jit(solution)/shard_map/cond/branch_4_fun/all_to_all | solution.py:613
  37.7 20.5 %collective-permute-done.28.refs_0_ = bf16[24,2,32,512]{3,2,1,0:T(8,128)(2,1)} collective-permute-done((bf16[24,2,32,512]{3,2,1,0:T(8,128)(2,1)}, bf16[24,2,32,512]{3,2,1,0:T(8,128)(2,1)}, u32[]{:S(2)}, u32[]{:S(2)}) %collective-permute-start.28) | collective-permute-done | bytes 1572896 | tf_op jit(solution)/shard_map/cond/branch_4_fun/ppermute | solution.py:656
  58.2 2.4 %collective-permute-start.32 = (bf16[24,2,32,512]{3,2,1,0:T(8,128)(2,1)}, bf16[24,2,32,512]{3,2,1,0:T(8,128)(2,1)}, u32[]{:S(2)}, u32[]{:S(2)}) collective-permute-start(bf16[24,2,32,512]{3,2,1,0:T(8,128)(2,1)} %collective-permute-done.28.refs_0_), channel_id=1, source_target_pairs={{0,32},{1,33},{2,34},{3,35},{4,36},{5,37},{6,38},{7,39},{8,40},{9,... | collective-permute-start | bytes 4718600 | tf_op jit(solution)/shard_map/cond/branch_4_fun/ppermute | solution.py:670
  60.7 1.9 %collective-permute-start.33 = (bf16[24,2,32,512]{3,2,1,0:T(8,128)(2,1)S(1)}, bf16[24,2,32,512]{3,2,1,0:T(8,128)(2,1)}, u32[]{:S(2)}, u32[]{:S(2)}) collective-permute-start(bf16[24,2,32,512]{3,2,1,0:T(8,128)(2,1)S(1)} %collective-permute-done.29.refs_2_), channel_id=1, source_target_pairs={{64,32},{65,33},{66,34},{67,35},{68,36},{69,37},{70,38},{71,39},{7... | collective-permute-start | bytes 4718600 | tf_op jit(solution)/shard_map/cond/branch_4_fun/ppermute | solution.py:671
  62.8 14.6 %all_to_all.152 = bf16[16,2,24,128]{3,2,1,0:T(8,128)(2,1)S(1)} all-to-all(bf16[16,2,24,128]{3,2,1,0:T(8,128)(2,1)S(1)} %rotate.11), channel_id=1, replica_groups=mesh['inst'=4,'ctx'=16,'head'=2] {'ctx'}, dimensions={0} | all-to-all | bytes 393216 | tf_op jit(solution)/shard_map/cond/branch_4_fun/all_to_all | solution.py:613
  77.6 10.9 %stay.11 = (bf16[2,8,512,512]{3,2,1,0:T(8,128)(2,1)}, bf16[8,2,48,128]{3,2,1,0:T(8,128)(2,1)S(1)}) custom-call(s32[416]{0:T(512)S(1)} %get-tuple-element.284.plan, bf16[2,8,512,512]{3,2,1,0:T(8,128)(2,1)} %get-tuple-element.274.cache, bf16[8,96,128]{2,1,0:T(8,128)(2,1)S(1)} %bitcast.156, bf16[8,2,8,512]{3,2,1,0:T(8,128)(2,1)S(1)} %pad.39.entries), custom_call_target="tpu_custom_call" | custom-call | bytes 33554432 | tf_op jit(solution)/shard_map/cond/branch_4_fun/stay/pallas_call | solution.py:390
  88.5 3.4 %collective-permute-done.30.refs_1_ = bf16[24,2,32,512]{3,2,1,0:T(8,128)(2,1)} collective-permute-done((bf16[24,2,32,512]{3,2,1,0:T(8,128)(2,1)}, bf16[24,2,32,512]{3,2,1,0:T(8,128)(2,1)}, u32[]{:S(2)}, u32[]{:S(2)}) %collective-permute-start.30) | collective-permute-done | bytes 1572896 | tf_op jit(solution)/shard_map/cond/branch_4_fun/ppermute | solution.py:656
  91.9 3.8 %gather.11.held = bf16[16,3,2,32,512]{4,3,2,1,0:T(8,128)(2,1)S(1)} custom-call(s32[416]{0:T(512)S(1)} %get-tuple-element.284.plan, bf16[8,2,8,512]{3,2,1,0:T(8,128)(2,1)S(1)} %pad.39.entries, bf16[24,2,32,512]{3,2,1,0:T(8,128)(2,1)} %collective-permute-done.28.refs_0_, bf16[24,2,32,512]{3,2,1,0:T(8,128)(2,1)} %collective-permute-done.30.refs_1_, ...), custom_call_target="tpu_custom_call" | custom-call | bytes 8388608 | tf_op jit(solution)/shard_map/cond/branch_4_fun/gather/pallas_call | solution.py:487
  95.8 1.7 moved.11
  97.5 14.7 %all_to_all.153.parts = bf16[16,48,128]{2,1,0:T(8,128)(2,1)S(1)} all-to-all(bf16[16,48,128]{2,1,0:T(8,128)(2,1)S(1)} %bitcast.166), channel_id=1, replica_groups=mesh['inst'=4,'ctx'=16,'head'=2] {'ctx'}, dimensions={0} | all-to-all | bytes 393216 | tf_op jit(solution)/shard_map/cond/branch_4_fun/all_to_all | solution.py:613
  112.2 38.3 %all_to_all.154.received = bf16[16,3,2,32,512]{4,3,2,1,0:T(8,128)(2,1)S(1)} all-to-all(bf16[16,3,2,32,512]{4,3,2,1,0:T(8,128)(2,1)S(1)} %gather.11.held), channel_id=1, replica_groups=mesh['inst'=4,'ctx'=16,'head'=2] {'ctx'}, dimensions={0} | all-to-all | bytes 6291456 | tf_op jit(solution)/shard_map/cond/branch_4_fun/all_to_all | solution.py:613
  150.4 0.9 merge.11
  151.3 3.5 %all-to-all-start.24 = ((bf16[16,48,128]{2,1,0:T(8,128)(2,1)}), bf16[16,48,128]{2,1,0:T(8,128)(2,1)S(1)}, u32[]{:S(2)}, u32[]{:S(2)}) async-start(bf16[16,48,128]{2,1,0:T(8,128)(2,1)} %merge.11), calls=%async_computation.24 | async-start | bytes 393216 | tf_op jit(solution)/shard_map/cond/branch_4_fun/all_to_all | solution.py:613
  154.9 3.6 %place.11 = bf16[2,8,512,512]{3,2,1,0:T(8,128)(2,1)} custom-call(s32[416]{0:T(512)S(1)} %get-tuple-element.284.plan, bf16[16,3,2,32,512]{4,3,2,1,0:T(8,128)(2,1)S(1)} %all_to_all.154.received, bf16[2,8,512,512]{3,2,1,0:T(8,128)(2,1)} %get-tuple-element.301.cache), custom_call_target="tpu_custom_call", output_to_operand_aliasing={{}: (2, {})} | custom-call | tf_op jit(solution)/shard_map/cond/branch_4_fun/place/pallas_call | solution.py:596
  158.5 3.5 %all-to-all-done.24 = bf16[16,48,128]{2,1,0:T(8,128)(2,1)S(1)} async-done(((bf16[16,48,128]{2,1,0:T(8,128)(2,1)}), bf16[16,48,128]{2,1,0:T(8,128)(2,1)S(1)}, u32[]{:S(2)}, u32[]{:S(2)}) %all-to-all-start.24) | async-done | bytes 196640 | tf_op jit(solution)/shard_map/cond/branch_4_fun/all_to_all | solution.py:613
  162.1 2.1 %fusion.32 = f32[24,384]{1,0:T(8,128)S(1)} fusion(bf16[24,3072]{1,0:T(8,128)(2,1)S(1)} %bitcast.173, bf16[3072,384]{1,0:T(8,128)(2,1)} %get-tuple-element.304), kind=kOutput, calls=%fused_computation.95 | convolution fusion | flops 56623104 | bytes 2543616 | tf_op jit(solution)/shard_map/cond/branch_4_fun/dot_general | solution.py:694
  164.3 6.2 %collective-permute-start.34 = (bf16[24,192]{1,0:T(8,128)(2,1)S(1)}, bf16[24,192]{1,0:T(8,128)(2,1)S(1)}, u32[]{:S(2)}, u32[]{:S(2)}) collective-permute-start(bf16[24,192]{1,0:T(8,128)(2,1)S(1)} %select_convert_fusion.4), channel_id=1, source_target_pairs={{0,1},{1,0},{2,3},{3,2},{4,5},{5,4},{6,7},{7,6},{8,9},{9,8},{10,11... | collective-permute-start | bytes 27656 | tf_op jit(solution)/shard_map/cond/branch_4_fun/ppermute | solution.py:699
  170.5 0.8 collective-permute-done.34
  171.4 0.7 fusion.18
  (40 shorter events, 3.4 us)
Async XLA Ops:
  0.6 8.0 %collective-permute-start.50 = (bf16[3,8,384]{2,1,0:T(8,128)(2,1)}, bf16[3,8,384]{2,1,0:T(8,128)(2,1)S(1)}, u32[]{:S(2)}, u32[]{:S(2)}) collective-permute-start(bf16[3,8,384]{2,1,0:T(8,128)(2,1)} %param.18), channel_id=1, source_target_pairs={{96,32},{97,33},{98,34},{99,35},{100,36},{101,37},{102,38},{103,39... | collective-permute-start | bytes 55304 | tf_op jit(solution)/shard_map/ppermute | solution.py:632
  1.3 8.4 %collective-permute-start.49 = (bf16[3,8,384]{2,1,0:T(8,128)(2,1)}, bf16[3,8,384]{2,1,0:T(8,128)(2,1)S(1)}, u32[]{:S(2)}, u32[]{:S(2)}) collective-permute-start(bf16[3,8,384]{2,1,0:T(8,128)(2,1)} %param.18), channel_id=1, source_target_pairs={{96,0},{97,1},{98,2},{99,3},{100,4},{101,5},{102,6},{103,7},{104,8... | collective-permute-start | bytes 55304 | tf_op jit(solution)/shard_map/ppermute | solution.py:632
  2.6 7.1 %collective-permute-start.51 = (bf16[3,8,384]{2,1,0:T(8,128)(2,1)}, bf16[3,8,384]{2,1,0:T(8,128)(2,1)S(1)}, u32[]{:S(2)}, u32[]{:S(2)}) collective-permute-start(bf16[3,8,384]{2,1,0:T(8,128)(2,1)} %param.18), channel_id=1, source_target_pairs={{96,64},{97,65},{98,66},{99,67},{100,68},{101,69},{102,70},{103,71... | collective-permute-start | bytes 55304 | tf_op jit(solution)/shard_map/ppermute | solution.py:632
  11.2 0.6 copy-start.17
  11.2 0.6 copy-start.26
  11.8 4.5 %copy-start.4 = (bf16[2,384,512]{2,1,0:T(8,128)(2,1)S(1)}, bf16[2,384,512]{2,1,0:T(8,128)(2,1)}, u32[]{:S(2)}) copy-start(bf16[2,384,512]{2,1,0:T(8,128)(2,1)} %get-tuple-element.283.w_kv) | copy-start | bytes 2359300 | tf_op jit(solution)/shard_map/cond
  11.8 4.5 %copy-start.10 = (bf16[3,8,384]{2,1,0:T(8,128)(2,1)S(1)}, bf16[3,8,384]{2,1,0:T(8,128)(2,1)}, u32[]{:S(2)}) copy-start(bf16[3,8,384]{2,1,0:T(8,128)(2,1)} %get-tuple-element.277.hidden) | copy-start | bytes 55300 | tf_op jit(solution)/shard_map/cond
  11.8 4.5 %copy-start.18 = (bf16[3,8,384]{2,1,0:T(8,128)(2,1)S(1)}, bf16[3,8,384]{2,1,0:T(8,128)(2,1)}, u32[]{:S(2)}) copy-start(bf16[3,8,384]{2,1,0:T(8,128)(2,1)} %copy-done.17) | copy-start | bytes 55300 | tf_op jit(solution)/shard_map/cond
  11.8 4.5 %copy-start.27 = (bf16[3,8,384]{2,1,0:T(8,128)(2,1)S(1)}, bf16[3,8,384]{2,1,0:T(8,128)(2,1)}, u32[]{:S(2)}) copy-start(bf16[3,8,384]{2,1,0:T(8,128)(2,1)} %copy-done.26) | copy-start | bytes 55300 | tf_op jit(solution)/shard_map/cond
  14.1 23.6 %collective-permute-start.29 = (bf16[24,2,32,512]{3,2,1,0:T(8,128)(2,1)}, bf16[24,2,32,512]{3,2,1,0:T(8,128)(2,1)S(1)}, u32[]{:S(2)}, u32[]{:S(2)}) collective-permute-start(bf16[24,2,32,512]{3,2,1,0:T(8,128)(2,1)} %get-tuple-element.286), channel_id=1, source_target_pairs={{96,64},{97,65},{98,66},{99,67},{100,68},{101,69},{102,70},{103,71... | collective-permute-start | bytes 4718600 | tf_op jit(solution)/shard_map/cond/branch_4_fun/ppermute | solution.py:657
  14.9 43.3 %collective-permute-start.28 = (bf16[24,2,32,512]{3,2,1,0:T(8,128)(2,1)}, bf16[24,2,32,512]{3,2,1,0:T(8,128)(2,1)}, u32[]{:S(2)}, u32[]{:S(2)}) collective-permute-start(bf16[24,2,32,512]{3,2,1,0:T(8,128)(2,1)} %get-tuple-element.275), channel_id=1, source_target_pairs={{96,0},{97,1},{98,2},{99,3},{100,4},{101,5},{102,6},{103,7},{104,8... | collective-permute-start | bytes 4718600 | tf_op jit(solution)/shard_map/cond/branch_4_fun/ppermute | solution.py:656
  20.5 17.2 %all-to-all-start.20 = ((f32[16,32,256]{2,1,0:T(8,128)}), f32[16,32,256]{2,1,0:T(8,128)S(1)}, u32[]{:S(2)}, u32[]{:S(2)}) async-start(f32[16,32,256]{2,1,0:T(8,128)} %project.11), calls=%async_computation.20 | async-start | bytes 1048576 | tf_op jit(solution)/shard_map/cond/branch_4_fun/all_to_all | solution.py:613
  30.5 58.0 %collective-permute-start.31 = (bf16[24,2,32,512]{3,2,1,0:T(8,128)(2,1)}, bf16[24,2,32,512]{3,2,1,0:T(8,128)(2,1)}, u32[]{:S(2)}, u32[]{:S(2)}) collective-permute-start(bf16[24,2,32,512]{3,2,1,0:T(8,128)(2,1)} %get-tuple-element.295), channel_id=1, source_target_pairs={{96,64},{97,65},{98,66},{99,67},{100,68},{101,69},{102,70},{103,71... | collective-permute-start | bytes 4718600 | tf_op jit(solution)/shard_map/cond/branch_4_fun/ppermute | solution.py:657
  32.4 59.6 %collective-permute-start.30 = (bf16[24,2,32,512]{3,2,1,0:T(8,128)(2,1)}, bf16[24,2,32,512]{3,2,1,0:T(8,128)(2,1)}, u32[]{:S(2)}, u32[]{:S(2)}) collective-permute-start(bf16[24,2,32,512]{3,2,1,0:T(8,128)(2,1)} %get-tuple-element.287), channel_id=1, source_target_pairs={{96,0},{97,1},{98,2},{99,3},{100,4},{101,5},{102,6},{103,7},{104,8... | collective-permute-start | bytes 4718600 | tf_op jit(solution)/shard_map/cond/branch_4_fun/ppermute | solution.py:656
  58.2 33.7 %collective-permute-start.32 = (bf16[24,2,32,512]{3,2,1,0:T(8,128)(2,1)}, bf16[24,2,32,512]{3,2,1,0:T(8,128)(2,1)}, u32[]{:S(2)}, u32[]{:S(2)}) collective-permute-start(bf16[24,2,32,512]{3,2,1,0:T(8,128)(2,1)} %collective-permute-done.28.refs_0_), channel_id=1, source_target_pairs={{0,32},{1,33},{2,34},{3,35},{4,36},{5,37},{6,38},{7,39},{8,40},{9,... | collective-permute-start | bytes 4718600 | tf_op jit(solution)/shard_map/cond/branch_4_fun/ppermute | solution.py:670
  60.7 31.3 %collective-permute-start.33 = (bf16[24,2,32,512]{3,2,1,0:T(8,128)(2,1)S(1)}, bf16[24,2,32,512]{3,2,1,0:T(8,128)(2,1)}, u32[]{:S(2)}, u32[]{:S(2)}) collective-permute-start(bf16[24,2,32,512]{3,2,1,0:T(8,128)(2,1)S(1)} %collective-permute-done.29.refs_2_), channel_id=1, source_target_pairs={{64,32},{65,33},{66,34},{67,35},{68,36},{69,37},{70,38},{71,39},{7... | collective-permute-start | bytes 4718600 | tf_op jit(solution)/shard_map/cond/branch_4_fun/ppermute | solution.py:671
  151.3 10.7 %all-to-all-start.24 = ((bf16[16,48,128]{2,1,0:T(8,128)(2,1)}), bf16[16,48,128]{2,1,0:T(8,128)(2,1)S(1)}, u32[]{:S(2)}, u32[]{:S(2)}) async-start(bf16[16,48,128]{2,1,0:T(8,128)(2,1)} %merge.11), calls=%async_computation.24 | async-start | bytes 393216 | tf_op jit(solution)/shard_map/cond/branch_4_fun/all_to_all | solution.py:613
  164.3 7.1 %collective-permute-start.34 = (bf16[24,192]{1,0:T(8,128)(2,1)S(1)}, bf16[24,192]{1,0:T(8,128)(2,1)S(1)}, u32[]{:S(2)}, u32[]{:S(2)}) collective-permute-start(bf16[24,192]{1,0:T(8,128)(2,1)S(1)} %select_convert_fusion.4), channel_id=1, source_target_pairs={{0,1},{1,0},{2,3},{3,2},{4,5},{5,4},{6,7},{7,6},{8,9},{9,8},{10,11... | collective-permute-start | bytes 27656 | tf_op jit(solution)/shard_map/cond/branch_4_fun/ppermute | solution.py:699

commit v3 on v2

--- a/solution.py
+++ b/solution.py
@@ -24,15 +24,15 @@
 HALF_ROWS = 48
 STAT_ROW = 40
 CHUNKS = 2
-ITEMS = (12, 15, 18, 21, 24, 28, 33)
+ITEMS = ((16, 24), (20, 24), (23, 25), (26, 28), (32, 40))
 BF16 = jnp.bfloat16
 F32 = jnp.float32
 I32 = jnp.int32
 
 NEW_LEN, STAYS, REQUEST = 0, 8, 16
 VALID, SLOT, LENGTH, COUNT = 24, 28, 32, 36
-STORED, LOGICAL, WITHIN = 48, 64, 80
-NEED = 96
+STORED, LOGICAL = 48, 64
+NEED = 80
 SOURCE, TARGET = 128, 272
 PLAN_SIZE = 416
 LIST = 72
@@ -51,12 +51,6 @@
     inst = lax.axis_index("inst")
     ctx = lax.axis_index("ctx")
 
-    def clear(p, carry):
-        plan[SOURCE + p] = 0
-        plan[TARGET + p] = -1
-        return carry
-
-    lax.fori_loop(0, 2 * LIST, clear, 0)
     for s in range(SLOTS):
         own = jnp.where(inst == INST - 1, 0, lengths[inst * SLOTS + s])
         plan[NEW_LEN + s] = own
@@ -72,17 +66,6 @@
         plan[STORED + lax.shift_right_logical(q, 4)] = b
         plan[LOGICAL + lax.shift_right_logical(q, 4)] = q
 
-    def search(d, carry):
-        found = jnp.int32(0)
-        for b in range(CTX):
-            q = order[d * CTX + b]
-            mine = lax.shift_right_logical(q, 4) == ctx
-            found = jnp.where(mine, lax.bitwise_and(q, CTX - 1), found)
-        plan[WITHIN + d] = found
-        return carry
-
-    lax.fori_loop(0, CTX, search, 0)
-
     counts = []
     total = [jnp.int32(0)] * 3
     for r in range(SLOTS):
@@ -93,18 +76,19 @@
         total = [total[i] + jnp.where(to == i, count, 0) for i in range(3)]
     def weigh(part, best):
         rest = total[1] - part
-        cost = jnp.maximum(
-            lax.shift_right_logical(jnp.maximum(part + total[0], rest + total[2]) + 1, 1),
-            jnp.maximum(part, rest),
-        )
-        better = cost < best[0]
-        return jnp.where(better, cost, best[0]), jnp.where(better, part, best[1])
-
-    least, split = lax.fori_loop(0, total[1] + 1, weigh, (jnp.int32(1000), jnp.int32(0)))
+        need = jnp.maximum(part + total[0], rest + total[2])
+        onward = jnp.maximum(part, rest)
+        size = jnp.int32(0)
+        for one, two in ITEMS[:-1]:
+            small = jnp.logical_or(need > one + two, onward > one)
+            size = size + jnp.where(small, 1, 0)
+        size = size * 256 + need + jnp.where(onward > ITEMS[-1][0], 128, 0)
+        better = size < best[0]
+        return jnp.where(better, size, best[0]), jnp.where(better, part, best[1])
+
+    size, split = lax.fori_loop(0, total[1] + 1, weigh, (jnp.int32(4096), jnp.int32(0)))
+    size = lax.shift_right_logical(size, 8)
     rest = total[1] - split
-    size = jnp.int32(0)
-    for items in ITEMS[:-1]:
-        size = size + jnp.where(least > items, 1, 0)
     plan[NEED] = size
 
     done = [jnp.int32(0)] * 3
@@ -115,16 +99,16 @@
         base = jnp.where(to == 0, done[0], jnp.where(to == 1, done[1], done[2]))
         place = jnp.where(to == 0, rank[0], jnp.where(to == 1, rank[1], rank[2]))
 
-        def put(c, carry, r=r, to=to, base=base, place=place):
-            e = base + c
-            by_zero = jnp.logical_or(to == 0, jnp.logical_and(to == 1, e < split))
-            p = jnp.where(
-                to == 0,
-                split + e,
-                jnp.where(to == 2, LIST + rest + e, jnp.where(e < split, e, LIST + e - split)),
-            )
-            plan[SOURCE + p] = r * CTX + c
-            plan[TARGET + p] = to * 64 + place * CTX + c
+        front = jnp.where(to == 0, split, jnp.where(to == 1, 0, LIST + rest)) + base
+        back = jnp.where(to == 1, LIST + base - split, front)
+        turn = split - base
+        source = r * CTX
+        target = to * 64 + place * CTX
+
+        def put(c, carry, front=front, back=back, turn=turn, source=source, target=target):
+            p = c + jnp.where(c < turn, front, back)
+            plan[SOURCE + p] = source + c
+            plan[TARGET + p] = target + c
             return carry
 
         lax.fori_loop(0, count, put, 0)
@@ -144,6 +128,14 @@
         done = [done[i] + jnp.where(to == i, count, 0) for i in range(3)]
         rank = [rank[i] + jnp.where(to == i, 1, 0) for i in range(3)]
 
+    def clear(p, carry):
+        plan[SOURCE + p] = 0
+        plan[TARGET + p] = -1
+        return carry
+
+    lax.fori_loop(split + total[0], LIST, clear, 0)
+    lax.fori_loop(LIST + rest + total[2], 2 * LIST, clear, 0)
+
 
 def make_plan(lengths, dest_inst, dest_slot, order):
     return pl.pallas_call(
@@ -155,36 +147,45 @@
     )(lengths, dest_inst, dest_slot, order)
 
 
-def pack_kernel(chunk, items, plan, cache, up, down, sem):
+def pack_kernel(first, items, plan, cache, up, down, held, read_sem, write_sem):
     @pl.when(lax.axis_index("inst") == INST - 1)
     def _():
-        for way, out in enumerate((up, down)):
-
-            def send(i, carry, way=way, out=out):
-                code = plan[SOURCE + way * LIST + chunk * items + i]
+        for way in range(2):
+
+            def read(i, carry, way=way):
+                code = plan[SOURCE + way * LIST + first + i]
                 r = lax.shift_right_logical(code, 4)
                 stored = plan[STORED + lax.bitwise_and(code, 15)]
                 rows = pl.ds(pl.multiple_of(stored * BLOCK, BLOCK), BLOCK)
-                pltpu.make_async_copy(cache.at[:, r, rows, :], out.at[i], sem.at[way]).start()
+                pltpu.make_async_copy(
+                    cache.at[:, r, rows, :], held.at[way, i], read_sem.at[way]
+                ).start()
                 return carry
 
-            lax.fori_loop(0, items, send, 0)
+            lax.fori_loop(0, items, read, 0)
         for way, out in enumerate((up, down)):
-            pltpu.make_async_copy(out, out, sem.at[way]).wait()
-
-
-def pack(chunk, items, plan, cache):
-    shape = jax.ShapeDtypeStruct((items, 2, BLOCK, FEATURES), BF16)
-    return pl.pallas_call(
-        functools.partial(pack_kernel, chunk, items),
-        out_shape=[shape, shape],
+            pltpu.make_async_copy(held.at[way], held.at[way], read_sem.at[way]).wait()
+            pltpu.make_async_copy(held.at[way], out, write_sem.at[way]).start()
+        for way, out in enumerate((up, down)):
+            pltpu.make_async_copy(held.at[way], out, write_sem.at[way]).wait()
+
+
+def pack(first, items, plan, cache):
+    shape = (items, 2, BLOCK, FEATURES)
+    return pl.pallas_call(
+        functools.partial(pack_kernel, first, items),
+        out_shape=[jax.ShapeDtypeStruct(shape, BF16)] * 2,
         in_specs=[SMEM, HBM],
-        out_specs=[VMEM, VMEM],
-        scratch_shapes=[pltpu.SemaphoreType.DMA((2,))],
+        out_specs=[HBM, HBM],
+        scratch_shapes=[
+            pltpu.VMEM((2, *shape), BF16),
+            pltpu.SemaphoreType.DMA((2,)),
+            pltpu.SemaphoreType.DMA((2,)),
+        ],
         cost_estimate=pl.CostEstimate(
             flops=0, bytes_accessed=8 * items * BLOCK * FEATURES * 2, transcendentals=0
         ),
-        compiler_params=params(16),
+        compiler_params=params(56),
         name="pack",
     )(plan, cache)
 
@@ -201,7 +202,9 @@
     return jnp.sum(jnp.where(same, lanes, 0.0), axis=1, keepdims=True)
 
 
-def project_kernel(plan, hidden, by0, by1, by2, gain, w_query, w_kv, out, lhs, stats):
+def project_kernel(
+    plan, order, hidden, by0, by1, by2, gain, w_query, w_kv, out, within, lhs, stats
+):
     step = pl.program_id(0)
 
     @pl.when(step == 0)
@@ -225,6 +228,18 @@
         sum_lanes = to_lanes(jnp.concatenate(sums, axis=0), 24)
         square_lanes = to_lanes(jnp.concatenate(squares, axis=0), 24)
         stats[...] = jnp.where(row == 1, sum_lanes, jnp.where(row == 2, square_lanes, 0.0))
+        ctx = lax.axis_index("ctx")
+
+        def search(d, carry):
+            found = jnp.int32(0)
+            for b in range(CTX):
+                q = order[d * CTX + b]
+                mine = lax.shift_right_logical(q, 4) == ctx
+                found = jnp.where(mine, lax.bitwise_and(q, CTX - 1), found)
+            within[d] = found
+            return carry
+
+        lax.fori_loop(0, CTX, search, 0)
 
     left = lhs[...].astype(BF16)
     tail = stats[...]
@@ -247,28 +262,31 @@
             store(o, w_kv[o // 2, :, (o % 2) * 256 : (o % 2 + 1) * 256])
 
 
-def project(plan, hidden, by, gain, w_query, w_kv):
+def project(plan, order, hidden, by, gain, w_query, w_kv):
     def whole(*shape):
         return pl.BlockSpec(shape, lambda i: (0,) * len(shape))
 
     small = whole(3, 8, 384)
     return pl.pallas_call(
         project_kernel,
-        out_shape=jax.ShapeDtypeStruct((CTX, 32, 256), F32),
+        out_shape=[
+            jax.ShapeDtypeStruct((CTX, 32, 256), F32),
+            jax.ShapeDtypeStruct((CTX,), I32),
+        ],
         grid=(4,),
-        in_specs=[SMEM, small, small, small, small, whole(1, 384)]
+        in_specs=[SMEM, SMEM, small, small, small, small, whole(1, 384)]
         + [
             pl.BlockSpec((384, 1024), lambda i: (0, jnp.minimum(i, 2))),
             whole(2, 384, 512),
         ],
-        out_specs=pl.BlockSpec((4, 32, 256), lambda i: (i, 0, 0)),
+        out_specs=[pl.BlockSpec((4, 32, 256), lambda i: (i, 0, 0)), SMEM],
         scratch_shapes=[pltpu.VMEM((32, 384), F32), pltpu.VMEM((8, 128), F32)],
         cost_estimate=pl.CostEstimate(
             flops=2 * 32 * 384 * 4096, bytes_accessed=384 * 4096 * 2, transcendentals=0
         ),
         compiler_params=params(12),
         name="project",
-    )(plan, hidden, *by, gain, w_query, w_kv)
+    )(plan, order, hidden, *by, gain, w_query, w_kv)
 
 
 def rotate_kernel(parts, cosine, sine, out):
@@ -420,19 +438,21 @@
     inst = lax.axis_index("inst")
 
     def fetch(way, chunk, ref, target):
+        first = sum(items[:chunk])
+
         def one(i, carry):
-            code = plan[TARGET + way * LIST + chunk * items + i]
+            code = plan[TARGET + way * LIST + first + i]
             inside = lax.bitwise_and(code, 63)
 
             @pl.when(lax.shift_right_arithmetic(code, 6) == target)
             def _():
                 place = lax.shift_right_logical(inside, 4)
                 c = lax.bitwise_and(inside, 15)
-                pltpu.make_async_copy(ref.at[i], held.at[c, place], sem).start()
+                pltpu.make_async_copy(ref.at[i], held.at[c, place], sem.at[c, place]).start()
 
             return carry
 
-        lax.fori_loop(0, items, one, 0)
+        lax.fori_loop(0, items[chunk], one, 0)
 
     for way, target in ((0, 0), (1, 2)):
 
@@ -447,29 +467,27 @@
             for chunk in range(CHUNKS - 1):
                 fetch(way, chunk, onward[way][chunk], 1)
 
-    @pl.when(inst < INST - 1)
-    def _():
-        for j in range(MOVED):
-
-            def fill(c, carry, j=j):
-                pltpu.make_async_copy(arrived[0].at[0], held.at[c, j], sem).start()
-                return carry
-
-            lax.fori_loop(plan[COUNT + j], CTX, fill, 0)
-        pltpu.make_async_copy(held, held, sem).wait()
-
     for j in range(MOVED):
 
         @pl.when(plan[VALID + j] > 0)
         def _(j=j):
             slot = plan[SLOT + j]
             length = plan[LENGTH + j]
+            count = plan[COUNT + j]
             at = lax.broadcasted_iota(I32, (BLOCK, 1), 0)
 
             def cut(c, carry):
                 start = plan[LOGICAL + c] * BLOCK
 
-                @pl.when(start + BLOCK > length)
+                @pl.when(c < count)
+                def _():
+                    pltpu.make_async_copy(held.at[c, j], held.at[c, j], sem.at[c, j]).wait()
+
+                @pl.when(start >= length + STEPS)
+                def _():
+                    held[c, j] = jnp.zeros((2, BLOCK, FEATURES), BF16)
+
+                @pl.when(jnp.logical_and(start + BLOCK > length, start < length + STEPS))
                 def _():
                     for kv in range(2):
                         block = jnp.where(start + at < length, held[c, j, kv], jnp.zeros((), BF16))
@@ -487,9 +505,9 @@
     return pl.pallas_call(
         functools.partial(gather_kernel, items),
         out_shape=jax.ShapeDtypeStruct((CTX, MOVED, 2, BLOCK, FEATURES), BF16),
-        in_specs=[SMEM, VMEM] + [HBM] * len(arrived),
+        in_specs=[SMEM, VMEM] + [ANY] * len(arrived),
         out_specs=VMEM,
-        scratch_shapes=[pltpu.SemaphoreType.DMA(())],
+        scratch_shapes=[pltpu.SemaphoreType.DMA((CTX, MOVED))],
         cost_estimate=pl.CostEstimate(flops=0, bytes_accessed=8 * 1024 * 1024, transcendentals=0),
         compiler_params=params(12),
         name="gather",
@@ -560,13 +578,13 @@
     )(parts)
 
 
-def place_kernel(plan, received, cache, new_cache, held, read_sem, write_sem):
+def place_kernel(plan, within, received, cache, new_cache, held, read_sem, write_sem):
     for j in range(MOVED):
 
         @pl.when(plan[VALID + j] > 0)
         def _(j=j):
             def one(d, carry):
-                rows = pl.ds(pl.multiple_of(plan[WITHIN + d] * BLOCK, BLOCK), BLOCK)
+                rows = pl.ds(pl.multiple_of(within[d] * BLOCK, BLOCK), BLOCK)
                 pltpu.make_async_copy(
                     received.at[d, j], held.at[j, :, rows, :], read_sem.at[j]
                 ).start()
@@ -592,21 +610,21 @@
             ).wait()
 
 
-def place(plan, received, cache):
+def place(plan, within, received, cache):
     return pl.pallas_call(
         place_kernel,
         out_shape=jax.ShapeDtypeStruct(cache.shape, BF16),
-        in_specs=[SMEM, ANY, HBM],
+        in_specs=[SMEM, SMEM, ANY, HBM],
         out_specs=HBM,
         scratch_shapes=[
             pltpu.VMEM((MOVED, 2, RANGE, FEATURES), BF16),
             pltpu.SemaphoreType.DMA((MOVED,)),
             pltpu.SemaphoreType.DMA((MOVED,)),
         ],
-        input_output_aliases={2: 0},
+        input_output_aliases={3: 0},
         compiler_params=params(12),
         name="place",
-    )(plan, received, cache)
+    )(plan, within, received, cache)
 
 
 def swap(x):
@@ -629,10 +647,13 @@
     dest_slot,
     block_order,
 ):
-    by = [lax.ppermute(hidden, "inst", [(INST - 1, i)]) for i in range(INST - 1)]
+    by = [up(hidden), down(hidden)]
+    by.append(lax.ppermute(by[0], "inst", [(0, 1)]))
     plan = make_plan(lengths, dest_inst, dest_slot, block_order)
     *by, plan = after(*by, plan)
-    operands = (plan, cache, hidden, by, norm_gain[None], w_query, key_value_weight, w_out)
+    operands = (
+        plan, block_order, cache, hidden, by, norm_gain[None], w_query, key_value_weight, w_out
+    )
     return lax.switch(
         plan[NEED], [functools.partial(decode, items) for items in ITEMS], *operands
     )
@@ -650,25 +671,31 @@
     return jnp.concatenate([cosine, cosine], axis=1), jnp.concatenate([-sine, sine], axis=1)
 
 
-def send(items, chunk, plan, cache):
-    one, two = pack(chunk, items, plan, cache)
-    return (
-        lax.ppermute(one, "inst", [(INST - 1, 0)]),
-        lax.ppermute(two, "inst", [(INST - 1, 2)]),
-        one,
+def up(x):
+    return lax.ppermute(x, "inst", [(INST - 1, 0)])
+
+
+def down(x):
+    return lax.ppermute(x, "inst", [(INST - 1, 2)])
+
+
+def pass_on(from_up, from_down):
+    return lax.ppermute(from_up, "inst", [(0, 1)]), lax.ppermute(from_down, "inst", [(2, 1)])
+
+
+def decode(items, plan, order, cache, hidden, by, gain, w_query, w_kv, w_out):
+    packed_up, packed_down = pack(0, items[0], plan, cache)
+    up_0, down_0 = up(packed_up), down(packed_down)
+    hidden, plan, packed_up = after(hidden, plan, packed_up)
+    cosine, sine = angles(plan)
+    projected, within = project(plan, order, hidden, by, gain, w_query, w_kv)
+    projected, cosine, sine, plan = after(projected, cosine, sine, plan)
+    packed_up, packed_down = pack(items[0], items[1], plan, cache)
+    parts, up_0, down_0, packed_up, packed_down = after(
+        swap(projected), up_0, down_0, packed_up, packed_down
     )
-
-
-def decode(items, plan, cache, hidden, by, gain, w_query, w_kv, w_out):
-    up_0, down_0, packed = send(items, 0, plan, cache)
-    hidden, plan, packed = after(hidden, plan, packed)
-    cosine, sine = angles(plan)
-    projected = project(plan, hidden, by, gain, w_query, w_kv)
-    projected, cosine, sine, plan = after(projected, cosine, sine, plan)
-    up_1, down_1, packed = send(items, 1, plan, cache)
-    parts, up_0, down_0, packed = after(swap(projected), up_0, down_0, packed)
-    up_on = lax.ppermute(up_0, "inst", [(0, 1)])
-    down_on = lax.ppermute(down_0, "inst", [(2, 1)])
+    up_1, down_1 = up(packed_up), down(packed_down)
+    up_on, down_on = pass_on(up_0, down_0)
     turned = swap(rotate(parts, cosine, sine))
     turned = turned.reshape(32, STEPS, SLOTS, HEAD_SIZE)
     query = turned[:24].reshape(2, 12, STEPS, SLOTS, HEAD_SIZE).transpose(3, 0, 1, 2, 4)
@@ -681,12 +708,13 @@
 
     new_cache, sums = stay(plan, cache, query, entries)
     entries, sums = after(entries, sums)
-    held = gather(items, plan, entries, [up_0, up_1, down_0, down_1, up_on, down_on])
+    arrived = [up_0, up_1, down_0, down_1, up_on, down_on]
+    held = gather(items, plan, entries, arrived)
     sums = attend_moved(plan, query, held, sums)
     sums, held = after(swap(sums.reshape(CTX, HALF_ROWS, HEAD_SIZE)), held)
     sums, received = after(sums, swap(held))
     attended = swap(merge(sums))
-    new_cache = place(plan, received, new_cache)
+    new_cache = place(plan, within, received, new_cache)
     attended, new_cache = after(attended, new_cache)
 
     attended = attended[:, :36].reshape(SLOTS, 2, 12, STEPS, HEAD_SIZE)

time: 170 us -> 162 us (0.953); the launches traced: 172 us -> 160 us
  waiting for transfers between devices: 33.4 us -> 20.1 us
  Pallas kernels: 34.4 us -> 32.2 us
  starting transfers between devices: 29.6 us -> 31.5 us
  blocking collectives: 67.5 us -> 69.3 us
    ppermute x9, waiting for transfers between devices: 25.1 us -> 8.01 us  [the longest x3 7.99 us: up(): return lax.ppermute(x, 'inst', [(INST - 1, 0)])]
    all_to_all x2, waiting for transfers between devices: 7.53 us -> 11.2 us  [swap(): return lax.all_to_all(x, 'ctx', split_axis=0, concat_axis=0, tiled=True)]
    pallas_call x3, Pallas kernels: 8.59 us -> 5.77 us  [the longest x1 4.53 us: project(): pl.pallas_call(project_kernel, out_shape=[jax.ShapeDtypeStruct((CTX, 32,...]
    all_to_all x3, blocking collectives: 67.5 us -> 69.3 us  [swap(): return lax.all_to_all(x, 'ctx', split_axis=0, concat_axis=0, tiled=True)]
where the time goes in v3:
time: 162 us; the launch traced here: 160 us
  blocking collectives  69.3 us (43%)
  Pallas kernels  32.2 us (20%)
  starting transfers between devices  31.5 us (19%)
  waiting for transfers between devices  20.1 us (12%)
  local copies, waits for them, and re-layouts  2.59 us (2%)
  matrix products  2.08 us (1%)
    all_to_all x3, blocking collectives, swap(): return lax.all_to_all(x, 'ctx', split_axis=0, concat_axis=0, tiled=True)  69.3 us
    all_to_all x2, starting transfers between devices, swap(): return lax.all_to_all(x, 'ctx', split_axis=0, concat_axis=0, tiled=True)  11.7 us
    all_to_all x2, waiting for transfers between devices, swap(): return lax.all_to_all(x, 'ctx', split_axis=0, concat_axis=0, tiled=True)  11.2 us
    pallas_call x1, Pallas kernels, stay(): pl.pallas_call(stay_kernel, out_shape=[jax.ShapeDtypeStruct(cache.shape,...  10.7 us
    ppermute x3, waiting for transfers between devices, up(): return lax.ppermute(x, 'inst', [(INST - 1, 0)])  7.99 us
    ppermute x1, starting transfers between devices, decode(): got = lax.ppermute(send_half, 'head', [(0, 1), (1, 0)])  7.38 us
    pallas_call x1, Pallas kernels, place(): pl.pallas_call(place_kernel, out_shape=jax.ShapeDtypeStruct(cache.shape,...  4.81 us
    pallas_call x1, Pallas kernels, project(): pl.pallas_call(project_kernel, out_shape=[jax.ShapeDtypeStruct((CTX, 32,...  4.53 us
  transfers between devices with their start and end apart: 12, of which 6 were waited for; matrix products, arithmetic and copies ran while one was open for 1% of the time, Pallas kernels for 15%

profile of v3, /device:TPU:1, one launch (start us, length us, event | category | flops | bytes accessed | tf_op | source)
XLA Modules:
  0.0 160.4 jit_solution(16638090952406816179)
XLA Ops:
  0.6 1.3 collective-permute-start.35
  2.6 4.2 %collective-permute-done.35 = bf16[3,8,384]{2,1,0:T(8,128)(2,1)S(1)} collective-permute-done((bf16[3,8,384]{2,1,0:T(8,128)(2,1)}, bf16[3,8,384]{2,1,0:T(8,128)(2,1)S(1)}, u32[]{:S(2)}, u32[]{:S(2)}) %collective-permute-start.35) | collective-permute-done | bytes 18464 | tf_op jit(solution)/shard_map/ppermute | solution.py:675
  6.8 1.3 collective-permute-start.37
  8.1 0.7 broadcast_in_dim.49
  8.8 3.2 %plan.1 = s32[416]{0:T(512)S(1)} custom-call(s32[32]{0:T(128)} %lengths.1, s32[8]{0:T(128)} %dest_inst.1, s32[8]{0:T(128)} %dest_slot.1, s32[256]{0:T(256)} %order.1), custom_call_target="tpu_custom_call" | custom-call | tf_op jit(solution)/shard_map/plan/pallas_call | solution.py:141
  13.3 147.1 %conditional.1 = (bf16[2,8,512,512]{3,2,1,0:T(8,128)(2,1)}, bf16[3,8,192]{2,1,0:T(8,128)(2,1)}) conditional(s32[]{:T(128)} %bitcast.55, (s32[416]{0:T(512)S(1)}, bf16[2,8,512,512]{3,2,1,0:T(8,128)(2,1)}, bf16[3,8,384]{2,1,0:T(8,128)(2,1)}, s32[256]{0:T(256)}, bf16[3,8,384]{2,1,0:T(8,128)(2,1)S(1)}, ...), branch_computations={%region_0.1_spmd, %region_1.2_spmd, %region_2.3_spmd, %region_3.4_... | conditional | flops 157321904 | bytes 165431856 | solution.py:657
  13.9 0.7 collective-permute-start.1
  14.7 1.3 collective-permute-start
  16.1 4.5 %project.5 = (f32[16,32,256]{2,1,0:T(8,128)}, s32[16]{0:T(128)S(1)}) custom-call(s32[416]{0:T(512)S(1)} %get-tuple-element.124.plan, s32[256]{0:T(256)S(1)} %copy-done.21, bf16[3,8,384]{2,1,0:T(8,128)(2,1)S(1)} %copy-done.16, bf16[3,8,384]{2,1,0:T(8,128)(2,1)S(1)} %get-tuple-element.117.by0, bf16[3,8,384]{2,1,0:T(8,128)(2,1)S(1)} %get-tuple-element.118.by1, ...), custom_call_target="tpu_custom_call" | custom-call | flops 100663296 | bytes 3145728 | tf_op jit(solution)/shard_map/cond/branch_0_fun/project/pallas_call | solution.py:270
  20.8 8.2 %all-to-all-start = ((f32[16,32,256]{2,1,0:T(8,128)}), f32[16,32,256]{2,1,0:T(8,128)S(1)}, u32[]{:S(2)}, u32[]{:S(2)}) async-start(f32[16,32,256]{2,1,0:T(8,128)} %get-tuple-element.125), calls=%async_computation | async-start | bytes 1048576 | tf_op jit(solution)/shard_map/cond/branch_0_fun/all_to_all | solution.py:631
  29.6 8.9 %all-to-all-done.parts = f32[16,32,256]{2,1,0:T(8,128)S(1)} async-done(((f32[16,32,256]{2,1,0:T(8,128)}), f32[16,32,256]{2,1,0:T(8,128)S(1)}, u32[]{:S(2)}, u32[]{:S(2)}) %all-to-all-start) | async-done | bytes 524320 | tf_op jit(solution)/shard_map/cond/branch_0_fun/all_to_all | solution.py:631
  38.5 1.8 %collective-permute-done.refs_0_ = bf16[16,2,32,512]{3,2,1,0:T(8,128)(2,1)S(1)} collective-permute-done((bf16[16,2,32,512]{3,2,1,0:T(8,128)(2,1)}, bf16[16,2,32,512]{3,2,1,0:T(8,128)(2,1)S(1)}, u32[]{:S(2)}, u32[]{:S(2)}) %collective-permute-start) | collective-permute-done | bytes 1048608 | tf_op jit(solution)/shard_map/cond/branch_0_fun/ppermute | solution.py:675
  40.3 1.0 copy-done.8
  41.3 1.3 collective-permute-start.2
  42.6 1.9 %collective-permute-start.3 = (bf16[24,2,32,512]{3,2,1,0:T(8,128)(2,1)}, bf16[24,2,32,512]{3,2,1,0:T(8,128)(2,1)}, u32[]{:S(2)}, u32[]{:S(2)}) collective-permute-start(bf16[24,2,32,512]{3,2,1,0:T(8,128)(2,1)} %get-tuple-element.137), channel_id=1, source_target_pairs={{96,64},{97,65},{98,66},{99,67},{100,68},{101,69},{102,70},{103,71... | collective-permute-start | bytes 4718600 | tf_op jit(solution)/shard_map/cond/branch_0_fun/ppermute | solution.py:679
  44.5 2.3 %collective-permute-start.4 = (bf16[16,2,32,512]{3,2,1,0:T(8,128)(2,1)}, bf16[16,2,32,512]{3,2,1,0:T(8,128)(2,1)}, u32[]{:S(2)}, u32[]{:S(2)}) collective-permute-start(bf16[16,2,32,512]{3,2,1,0:T(8,128)(2,1)} %copy-done.8), channel_id=1, source_target_pairs={{0,32},{1,33},{2,34},{3,35},{4,36},{5,37},{6,38},{7,39},{8,40},{9,... | collective-permute-start | bytes 3145736 | tf_op jit(solution)/shard_map/cond/branch_0_fun/ppermute | solution.py:683
  46.8 1.7 %collective-permute-start.5 = (bf16[16,2,32,512]{3,2,1,0:T(8,128)(2,1)S(1)}, bf16[16,2,32,512]{3,2,1,0:T(8,128)(2,1)}, u32[]{:S(2)}, u32[]{:S(2)}) collective-permute-start(bf16[16,2,32,512]{3,2,1,0:T(8,128)(2,1)S(1)} %collective-permute-done.1.refs_2_), channel_id=1, source_target_pairs={{64,32},{65,33},{66,34},{67,35},{68,36},{69,37},{70,38},{71,39},{7... | collective-permute-start | bytes 3145736 | tf_op jit(solution)/shard_map/cond/branch_0_fun/ppermute | solution.py:683
  48.7 15.6 %all_to_all.100 = bf16[16,2,24,128]{3,2,1,0:T(8,128)(2,1)S(1)} all-to-all(bf16[16,2,24,128]{3,2,1,0:T(8,128)(2,1)S(1)} %rotate.5), channel_id=1, replica_groups=mesh['inst'=4,'ctx'=16,'head'=2] {'ctx'}, dimensions={0} | all-to-all | bytes 393216 | tf_op jit(solution)/shard_map/cond/branch_0_fun/all_to_all | solution.py:631
  64.6 10.7 %stay.5 = (bf16[2,8,512,512]{3,2,1,0:T(8,128)(2,1)}, bf16[8,2,48,128]{3,2,1,0:T(8,128)(2,1)S(1)}) custom-call(s32[416]{0:T(512)S(1)} %get-tuple-element.124.plan, bf16[2,8,512,512]{3,2,1,0:T(8,128)(2,1)} %get-tuple-element.112.cache, bf16[8,96,128]{2,1,0:T(8,128)(2,1)S(1)} %bitcast.106, bf16[8,2,8,512]{3,2,1,0:T(8,128)(2,1)S(1)} %pad.23.entries), custom_call_target="tpu_custom_call" | custom-call | bytes 33554432 | tf_op jit(solution)/shard_map/cond/branch_0_fun/stay/pallas_call | solution.py:408
  75.3 2.0 %collective-permute-done.2.refs_1_ = bf16[24,2,32,512]{3,2,1,0:T(8,128)(2,1)S(1)} collective-permute-done((bf16[24,2,32,512]{3,2,1,0:T(8,128)(2,1)}, bf16[24,2,32,512]{3,2,1,0:T(8,128)(2,1)S(1)}, u32[]{:S(2)}, u32[]{:S(2)}) %collective-permute-start.2) | collective-permute-done | bytes 1572896 | tf_op jit(solution)/shard_map/cond/branch_0_fun/ppermute | solution.py:675
  77.3 4.3 %gather.5.held = bf16[16,3,2,32,512]{4,3,2,1,0:T(8,128)(2,1)S(1)} custom-call(s32[416]{0:T(512)S(1)} %get-tuple-element.124.plan, bf16[8,2,8,512]{3,2,1,0:T(8,128)(2,1)S(1)} %pad.23.entries, bf16[16,2,32,512]{3,2,1,0:T(8,128)(2,1)S(1)} %copy-done.9, bf16[24,2,32,512]{3,2,1,0:T(8,128)(2,1)S(1)} %collective-permute-done.2.refs_1_, ...), custom_call_target="tpu_custom_call" | custom-call | bytes 8388608 | tf_op jit(solution)/shard_map/cond/branch_0_fun/gather/pallas_call | solution.py:505
  81.6 2.3 %moved.5 = bf16[8,2,48,128]{3,2,1,0:T(8,128)(2,1)S(1)} custom-call(s32[416]{0:T(512)S(1)} %get-tuple-element.124.plan, bf16[8,96,128]{2,1,0:T(8,128)(2,1)S(1)} %bitcast.107, bf16[16,3,2,32,512]{4,3,2,1,0:T(8,128)(2,1)S(1)} %gather.5.held, bf16[8,2,48,128]{3,2,1,0:T(8,128)(2,1)S(1)} %get-tuple-element.138.sums), custom_call_target="tpu_custom_call" | custom-call | bytes 12582912 | tf_op jit(solution)/shard_map/cond/branch_0_fun/moved/pallas_call | solution.py:539
  83.9 16.1 %all_to_all.101.parts = bf16[16,48,128]{2,1,0:T(8,128)(2,1)S(1)} all-to-all(bf16[16,48,128]{2,1,0:T(8,128)(2,1)S(1)} %bitcast.116), channel_id=1, replica_groups=mesh['inst'=4,'ctx'=16,'head'=2] {'ctx'}, dimensions={0} | all-to-all | bytes 393216 | tf_op jit(solution)/shard_map/cond/branch_0_fun/all_to_all | solution.py:631
  100.0 37.6 %all_to_all.102.received = bf16[16,3,2,32,512]{4,3,2,1,0:T(8,128)(2,1)S(1)} all-to-all(bf16[16,3,2,32,512]{4,3,2,1,0:T(8,128)(2,1)S(1)} %gather.5.held), channel_id=1, replica_groups=mesh['inst'=4,'ctx'=16,'head'=2] {'ctx'}, dimensions={0} | all-to-all | bytes 6291456 | tf_op jit(solution)/shard_map/cond/branch_0_fun/all_to_all | solution.py:631
  137.6 0.9 merge.5
  138.5 3.5 %all-to-all-start.4 = ((bf16[16,48,128]{2,1,0:T(8,128)(2,1)}), bf16[16,48,128]{2,1,0:T(8,128)(2,1)S(1)}, u32[]{:S(2)}, u32[]{:S(2)}) async-start(bf16[16,48,128]{2,1,0:T(8,128)(2,1)} %merge.5), calls=%async_computation.4 | async-start | bytes 393216 | tf_op jit(solution)/shard_map/cond/branch_0_fun/all_to_all | solution.py:631
  142.1 4.8 %place.5 = bf16[2,8,512,512]{3,2,1,0:T(8,128)(2,1)} custom-call(s32[416]{0:T(512)S(1)} %get-tuple-element.124.plan, s32[16]{0:T(128)S(1)} %get-tuple-element.142.within, bf16[16,3,2,32,512]{4,3,2,1,0:T(8,128)(2,1)S(1)} %all_to_all.102.received, bf16[2,8,512,512]{3,2,1,0:T(8,128)(2,1)} %get-tuple-element.144.cache), custom_call_target="tpu_custom_call", output_to_operand_aliasing={{}: (3, {})} | custom-call | tf_op jit(solution)/shard_map/cond/branch_0_fun/place/pallas_call | solution.py:614
  146.9 2.3 %all-to-all-done.4 = bf16[16,48,128]{2,1,0:T(8,128)(2,1)S(1)} async-done(((bf16[16,48,128]{2,1,0:T(8,128)(2,1)}), bf16[16,48,128]{2,1,0:T(8,128)(2,1)S(1)}, u32[]{:S(2)}, u32[]{:S(2)}) %all-to-all-start.4) | async-done | bytes 196640 | tf_op jit(solution)/shard_map/cond/branch_0_fun/all_to_all | solution.py:631
  149.3 2.1 %fusion.20 = f32[24,384]{1,0:T(8,128)S(1)} fusion(bf16[24,3072]{1,0:T(8,128)(2,1)S(1)} %bitcast.121, bf16[3072,384]{1,0:T(8,128)(2,1)} %get-tuple-element.147), kind=kOutput, calls=%fused_computation.65 | convolution fusion | flops 56623104 | bytes 2543616 | tf_op jit(solution)/shard_map/cond/branch_0_fun/dot_general | solution.py:722
  151.5 7.4 %collective-permute-start.6 = (bf16[24,192]{1,0:T(8,128)(2,1)S(1)}, bf16[24,192]{1,0:T(8,128)(2,1)S(1)}, u32[]{:S(2)}, u32[]{:S(2)}) collective-permute-start(bf16[24,192]{1,0:T(8,128)(2,1)S(1)} %select_convert_fusion), channel_id=1, source_target_pairs={{0,1},{1,0},{2,3},{3,2},{4,5},{5,4},{6,7},{7,6},{8,9},{9,8},{10,11... | collective-permute-start | bytes 27656 | tf_op jit(solution)/shard_map/cond/branch_0_fun/ppermute | solution.py:727
  158.8 0.8 collective-permute-done.6
  159.7 0.7 fusion.2
  (38 shorter events, 3.3 us)
Async XLA Ops:
  0.6 6.2 %collective-permute-start.35 = (bf16[3,8,384]{2,1,0:T(8,128)(2,1)}, bf16[3,8,384]{2,1,0:T(8,128)(2,1)S(1)}, u32[]{:S(2)}, u32[]{:S(2)}) collective-permute-start(bf16[3,8,384]{2,1,0:T(8,128)(2,1)} %param.16), channel_id=1, source_target_pairs={{96,0},{97,1},{98,2},{99,3},{100,4},{101,5},{102,6},{103,7},{104,8... | collective-permute-start | bytes 55304 | tf_op jit(solution)/shard_map/ppermute | solution.py:675
  1.9 10.1 %collective-permute-start.36 = (bf16[3,8,384]{2,1,0:T(8,128)(2,1)}, bf16[3,8,384]{2,1,0:T(8,128)(2,1)S(1)}, u32[]{:S(2)}, u32[]{:S(2)}) collective-permute-start(bf16[3,8,384]{2,1,0:T(8,128)(2,1)} %param.16), channel_id=1, source_target_pairs={{96,64},{97,65},{98,66},{99,67},{100,68},{101,69},{102,70},{103,71... | collective-permute-start | bytes 55304 | tf_op jit(solution)/shard_map/ppermute | solution.py:679
  6.8 5.2 %collective-permute-start.37 = (bf16[3,8,384]{2,1,0:T(8,128)(2,1)S(1)}, bf16[3,8,384]{2,1,0:T(8,128)(2,1)S(1)}, u32[]{:S(2)}, u32[]{:S(2)}) collective-permute-start(bf16[3,8,384]{2,1,0:T(8,128)(2,1)S(1)} %collective-permute-done.35), channel_id=1, source_target_pairs={{0,32},{1,33},{2,34},{3,35},{4,36},{5,37},{6,38},{7,39},{8,40},{9,... | collective-permute-start | bytes 55304 | tf_op jit(solution)/shard_map/ppermute | solution.py:651
  13.3 2.8 %copy-start.11 = (bf16[2,384,512]{2,1,0:T(8,128)(2,1)S(1)}, bf16[2,384,512]{2,1,0:T(8,128)(2,1)}, u32[]{:S(2)}) copy-start(bf16[2,384,512]{2,1,0:T(8,128)(2,1)} %get-tuple-element.122.w_kv) | copy-start | bytes 2359300 | tf_op jit(solution)/shard_map/cond
  13.3 2.8 %copy-start.16 = (bf16[3,8,384]{2,1,0:T(8,128)(2,1)S(1)}, bf16[3,8,384]{2,1,0:T(8,128)(2,1)}, u32[]{:S(2)}) copy-start(bf16[3,8,384]{2,1,0:T(8,128)(2,1)} %get-tuple-element.116.hidden) | copy-start | bytes 55300 | tf_op jit(solution)/shard_map/cond
  13.3 2.8 %copy-start.21 = (s32[256]{0:T(256)S(1)}, s32[256]{0:T(256)}, u32[]{:S(2)}) copy-start(s32[256]{0:T(256)} %get-tuple-element.115.order) | copy-start | bytes 3076 | tf_op jit(solution)/shard_map/cond
  13.9 24.6 %collective-permute-start.1 = (bf16[16,2,32,512]{3,2,1,0:T(8,128)(2,1)}, bf16[16,2,32,512]{3,2,1,0:T(8,128)(2,1)S(1)}, u32[]{:S(2)}, u32[]{:S(2)}) collective-permute-start(bf16[16,2,32,512]{3,2,1,0:T(8,128)(2,1)} %get-tuple-element.126), channel_id=1, source_target_pairs={{96,64},{97,65},{98,66},{99,67},{100,68},{101,69},{102,70},{103,71... | collective-permute-start | bytes 3145736 | tf_op jit(solution)/shard_map/cond/branch_0_fun/ppermute | solution.py:679
  14.7 25.7 %collective-permute-start = (bf16[16,2,32,512]{3,2,1,0:T(8,128)(2,1)}, bf16[16,2,32,512]{3,2,1,0:T(8,128)(2,1)S(1)}, u32[]{:S(2)}, u32[]{:S(2)}) collective-permute-start(bf16[16,2,32,512]{3,2,1,0:T(8,128)(2,1)} %get-tuple-element.113), channel_id=1, source_target_pairs={{96,0},{97,1},{98,2},{99,3},{100,4},{101,5},{102,6},{103,7},{104,8... | collective-permute-start | bytes 3145736 | tf_op jit(solution)/shard_map/cond/branch_0_fun/ppermute | solution.py:675
  20.8 17.7 %all-to-all-start = ((f32[16,32,256]{2,1,0:T(8,128)}), f32[16,32,256]{2,1,0:T(8,128)S(1)}, u32[]{:S(2)}, u32[]{:S(2)}) async-start(f32[16,32,256]{2,1,0:T(8,128)} %get-tuple-element.125), calls=%async_computation | async-start | bytes 1048576 | tf_op jit(solution)/shard_map/cond/branch_0_fun/all_to_all | solution.py:631
  40.3 1.0 copy-start.8
  41.3 36.0 %collective-permute-start.2 = (bf16[24,2,32,512]{3,2,1,0:T(8,128)(2,1)}, bf16[24,2,32,512]{3,2,1,0:T(8,128)(2,1)S(1)}, u32[]{:S(2)}, u32[]{:S(2)}) collective-permute-start(bf16[24,2,32,512]{3,2,1,0:T(8,128)(2,1)} %get-tuple-element.135), channel_id=1, source_target_pairs={{96,0},{97,1},{98,2},{99,3},{100,4},{101,5},{102,6},{103,7},{104,8... | collective-permute-start | bytes 4718600 | tf_op jit(solution)/shard_map/cond/branch_0_fun/ppermute | solution.py:675
  42.6 34.7 %collective-permute-start.3 = (bf16[24,2,32,512]{3,2,1,0:T(8,128)(2,1)}, bf16[24,2,32,512]{3,2,1,0:T(8,128)(2,1)}, u32[]{:S(2)}, u32[]{:S(2)}) collective-permute-start(bf16[24,2,32,512]{3,2,1,0:T(8,128)(2,1)} %get-tuple-element.137), channel_id=1, source_target_pairs={{96,64},{97,65},{98,66},{99,67},{100,68},{101,69},{102,70},{103,71... | collective-permute-start | bytes 4718600 | tf_op jit(solution)/shard_map/cond/branch_0_fun/ppermute | solution.py:679
  44.5 30.8 %collective-permute-start.4 = (bf16[16,2,32,512]{3,2,1,0:T(8,128)(2,1)}, bf16[16,2,32,512]{3,2,1,0:T(8,128)(2,1)}, u32[]{:S(2)}, u32[]{:S(2)}) collective-permute-start(bf16[16,2,32,512]{3,2,1,0:T(8,128)(2,1)} %copy-done.8), channel_id=1, source_target_pairs={{0,32},{1,33},{2,34},{3,35},{4,36},{5,37},{6,38},{7,39},{8,40},{9,... | collective-permute-start | bytes 3145736 | tf_op jit(solution)/shard_map/cond/branch_0_fun/ppermute | solution.py:683
  46.8 28.5 %collective-permute-start.5 = (bf16[16,2,32,512]{3,2,1,0:T(8,128)(2,1)S(1)}, bf16[16,2,32,512]{3,2,1,0:T(8,128)(2,1)}, u32[]{:S(2)}, u32[]{:S(2)}) collective-permute-start(bf16[16,2,32,512]{3,2,1,0:T(8,128)(2,1)S(1)} %collective-permute-done.1.refs_2_), channel_id=1, source_target_pairs={{64,32},{65,33},{66,34},{67,35},{68,36},{69,37},{70,38},{71,39},{7... | collective-permute-start | bytes 3145736 | tf_op jit(solution)/shard_map/cond/branch_0_fun/ppermute | solution.py:683
  64.6 12.7 %copy-start.9 = (bf16[16,2,32,512]{3,2,1,0:T(8,128)(2,1)S(1)}, bf16[16,2,32,512]{3,2,1,0:T(8,128)(2,1)}, u32[]{:S(2)}) copy-start(bf16[16,2,32,512]{3,2,1,0:T(8,128)(2,1)} %copy-done.8) | copy-start | bytes 3145732 | tf_op jit(solution)/shard_map/cond
  138.5 10.7 %all-to-all-start.4 = ((bf16[16,48,128]{2,1,0:T(8,128)(2,1)}), bf16[16,48,128]{2,1,0:T(8,128)(2,1)S(1)}, u32[]{:S(2)}, u32[]{:S(2)}) async-start(bf16[16,48,128]{2,1,0:T(8,128)(2,1)} %merge.5), calls=%async_computation.4 | async-start | bytes 393216 | tf_op jit(solution)/shard_map/cond/branch_0_fun/all_to_all | solution.py:631
  151.5 8.2 %collective-permute-start.6 = (bf16[24,192]{1,0:T(8,128)(2,1)S(1)}, bf16[24,192]{1,0:T(8,128)(2,1)S(1)}, u32[]{:S(2)}, u32[]{:S(2)}) collective-permute-start(bf16[24,192]{1,0:T(8,128)(2,1)S(1)} %select_convert_fusion), channel_id=1, source_target_pairs={{0,1},{1,0},{2,3},{3,2},{4,5},{5,4},{6,7},{7,6},{8,9},{9,8},{10,11... | collective-permute-start | bytes 27656 | tf_op jit(solution)/shard_map/cond/branch_0_fun/ppermute | solution.py:727

commit v4 on v3

--- a/solution.py
+++ b/solution.py
@@ -24,7 +24,7 @@
 HALF_ROWS = 48
 STAT_ROW = 40
 CHUNKS = 2
-ITEMS = ((16, 24), (20, 24), (23, 25), (26, 28), (32, 40))
+ITEMS = ((22, 26), (27, 31), (32, 40))
 BF16 = jnp.bfloat16
 F32 = jnp.float32
 I32 = jnp.int32
@@ -202,25 +202,17 @@
     return jnp.sum(jnp.where(same, lanes, 0.0), axis=1, keepdims=True)
 
 
-def project_kernel(
-    plan, order, hidden, by0, by1, by2, gain, w_query, w_kv, out, within, lhs, stats
-):
+def project_kernel(hidden, order, gain, w_query, w_kv, out, within, lhs, stats):
     step = pl.program_id(0)
 
     @pl.when(step == 0)
     def _():
         row = lax.broadcasted_iota(I32, (SLOTS, 1), 0)
-        request = jnp.full((SLOTS, 1), -1, I32)
-        for s in range(SLOTS):
-            request = jnp.where(row == s, plan[REQUEST + s], request)
         scale = gain[...].astype(F32)
         sums = []
         squares = []
         for t in range(STEPS):
             x = hidden[t].astype(F32)
-            moved = by0[t].astype(F32) + by1[t].astype(F32) + by2[t].astype(F32)
-            for r in range(SLOTS):
-                x = jnp.where(request == r, moved[r : r + 1, :], x)
             sums.append(jnp.sum(x, axis=1, keepdims=True))
             squares.append(jnp.sum(x * x, axis=1, keepdims=True))
             lhs[t * SLOTS : (t + 1) * SLOTS, :] = x * scale
@@ -262,11 +254,10 @@
             store(o, w_kv[o // 2, :, (o % 2) * 256 : (o % 2 + 1) * 256])
 
 
-def project(plan, order, hidden, by, gain, w_query, w_kv):
+def project(hidden, order, gain, w_query, w_kv):
     def whole(*shape):
         return pl.BlockSpec(shape, lambda i: (0,) * len(shape))
 
-    small = whole(3, 8, 384)
     return pl.pallas_call(
         project_kernel,
         out_shape=[
@@ -274,8 +265,10 @@
             jax.ShapeDtypeStruct((CTX,), I32),
         ],
         grid=(4,),
-        in_specs=[SMEM, SMEM, small, small, small, small, whole(1, 384)]
-        + [
+        in_specs=[
+            whole(3, 8, 384),
+            SMEM,
+            whole(1, 384),
             pl.BlockSpec((384, 1024), lambda i: (0, jnp.minimum(i, 2))),
             whole(2, 384, 512),
         ],
@@ -286,7 +279,7 @@
         ),
         compiler_params=params(12),
         name="project",
-    )(plan, order, hidden, *by, gain, w_query, w_kv)
+    )(hidden, order, gain, w_query, w_kv)
 
 
 def rotate_kernel(parts, cosine, sine, out):
@@ -369,50 +362,74 @@
     return jnp.where(row == STAT_ROW, MASKED_SCORE, 0.0).astype(BF16)
 
 
-def stay_kernel(plan, cache, query, entries, new_cache, sums):
+def attend_kernel(lengths, order, cache, query, entries, new_cache, sums):
     s = pl.program_id(0)
-    base = lax.axis_index("ctx") * RANGE
-    length = plan[NEW_LEN + s]
-    stays = plan[STAYS + s] > 0
-    some = jnp.logical_and(stays, base < length + STEPS)
-    full = jnp.logical_and(some, base + RANGE <= length)
-
-    @pl.when(full)
-    def _():
-        new_cache[...] = cache[...]
-
-    @pl.when(jnp.logical_and(some, jnp.logical_not(full)))
-    def _():
-        at = base + lax.broadcasted_iota(I32, (RANGE, 1), 0)
-        for kv in range(2):
-            block = jnp.where(at < length, cache[kv, 0], jnp.zeros((), BF16))
-            for t in range(STEPS):
-                block = jnp.where(at == length + t, entries[0, kv, t : t + 1, :], block)
-            new_cache[kv, 0] = block
+    inst = lax.axis_index("inst")
+    ctx = lax.axis_index("ctx")
+    retires = inst == INST - 1
+    length = lengths[inst * SLOTS + s]
+    some = jnp.logical_and(
+        length > 0, jnp.logical_or(retires, ctx * RANGE < length + STEPS)
+    )
 
     @pl.when(some)
     def _():
-        position = base + lax.broadcasted_iota(I32, (1, RANGE), 1)
+        lane = lax.broadcasted_iota(I32, (1, RANGE), 1)
+        position = jnp.zeros((1, RANGE), I32)
+        for b in range(CTX):
+            start = jnp.where(retires, order[ctx * CTX + b], ctx * CTX + b) * BLOCK
+            position = jnp.where(
+                lax.shift_right_logical(lane, 5) == b, start + lane - b * BLOCK, position
+            )
+
+        def build(b, carry):
+            start = jnp.where(retires, order[ctx * CTX + b], ctx * CTX + b) * BLOCK
+            rows = pl.ds(pl.multiple_of(b * BLOCK, BLOCK), BLOCK)
+
+            @pl.when(start + BLOCK <= length)
+            def _():
+                new_cache[:, 0, rows, :] = cache[:, 0, rows, :]
+
+            @pl.when(start >= length + STEPS)
+            def _():
+                new_cache[:, 0, rows, :] = jnp.zeros((2, BLOCK, FEATURES), BF16)
+
+            @pl.when(jnp.logical_and(start + BLOCK > length, start < length + STEPS))
+            def _():
+                at = start + lax.broadcasted_iota(I32, (BLOCK, 1), 0)
+                for kv in range(2):
+                    block = jnp.where(at < length, cache[kv, 0, rows, :], jnp.zeros((), BF16))
+                    for t in range(STEPS):
+                        block = jnp.where(at == length + t, entries[0, kv, t : t + 1, :], block)
+                    new_cache[kv, 0, rows, :] = block
+
+            return carry
+
+        lax.fori_loop(0, CTX, build, 0)
         halves = attend(new_cache[0, 0], new_cache[1, 0], query[0], position, length)
         for h in range(2):
             sums[0, h] = halves[h]
 
     @pl.when(jnp.logical_not(some))
     def _():
-        new_cache[...] = jnp.zeros_like(new_cache)
         for h in range(2):
             sums[0, h] = blank_message()
 
-
-def stay(plan, cache, query, entries):
+    @pl.when(jnp.logical_or(retires, jnp.logical_not(some)))
+    def _():
+        new_cache[...] = jnp.zeros_like(new_cache)
+
+
+def attend_slots(lengths, order, cache, query, entries):
     return pl.pallas_call(
-        stay_kernel,
+        attend_kernel,
         out_shape=[
             jax.ShapeDtypeStruct(cache.shape, BF16),
             jax.ShapeDtypeStruct((SLOTS, 2, HALF_ROWS, 128), BF16),
         ],
         grid=(SLOTS,),
         in_specs=[
+            SMEM,
             SMEM,
             pl.BlockSpec((2, 1, RANGE, FEATURES), lambda s: (0, s, 0, 0)),
             pl.BlockSpec((1, 2 * HALF_ROWS, 128), lambda s: (s, 0, 0)),
@@ -426,11 +443,11 @@
             flops=0, bytes_accessed=32 * 1024 * 1024, transcendentals=0
         ),
         compiler_params=params(24),
-        name="stay",
-    )(plan, cache, query, entries)
-
-
-def gather_kernel(items, plan, entries, *refs):
+        name="attend_slots",
+    )(lengths, order, cache, query, entries)
+
+
+def gather_kernel(items, plan, *refs):
     count = 4 * CHUNKS - 2
     arrived, (held, sem) = refs[:count], refs[count:]
     straight = (arrived[:CHUNKS], arrived[CHUNKS : 2 * CHUNKS])
@@ -469,82 +486,24 @@
 
     for j in range(MOVED):
 
-        @pl.when(plan[VALID + j] > 0)
-        def _(j=j):
-            slot = plan[SLOT + j]
-            length = plan[LENGTH + j]
-            count = plan[COUNT + j]
-            at = lax.broadcasted_iota(I32, (BLOCK, 1), 0)
-
-            def cut(c, carry):
-                start = plan[LOGICAL + c] * BLOCK
-
-                @pl.when(c < count)
-                def _():
-                    pltpu.make_async_copy(held.at[c, j], held.at[c, j], sem.at[c, j]).wait()
-
-                @pl.when(start >= length + STEPS)
-                def _():
-                    held[c, j] = jnp.zeros((2, BLOCK, FEATURES), BF16)
-
-                @pl.when(jnp.logical_and(start + BLOCK > length, start < length + STEPS))
-                def _():
-                    for kv in range(2):
-                        block = jnp.where(start + at < length, held[c, j, kv], jnp.zeros((), BF16))
-                        new = entries[slot, kv]
-                        for t in range(STEPS):
-                            block = jnp.where(start + at == length + t, new[t : t + 1, :], block)
-                        held[c, j, kv] = block
-
-                return carry
-
-            lax.fori_loop(0, CTX, cut, 0)
-
-
-def gather(items, plan, entries, arrived):
+        def wait(c, carry, j=j):
+            pltpu.make_async_copy(held.at[c, j], held.at[c, j], sem.at[c, j]).wait()
+            return carry
+
+        lax.fori_loop(0, plan[COUNT + j], wait, 0)
+
+
+def gather(items, plan, arrived):
     return pl.pallas_call(
         functools.partial(gather_kernel, items),
         out_shape=jax.ShapeDtypeStruct((CTX, MOVED, 2, BLOCK, FEATURES), BF16),
-        in_specs=[SMEM, VMEM] + [ANY] * len(arrived),
+        in_specs=[SMEM] + [ANY] * len(arrived),
         out_specs=VMEM,
         scratch_shapes=[pltpu.SemaphoreType.DMA((CTX, MOVED))],
         cost_estimate=pl.CostEstimate(flops=0, bytes_accessed=8 * 1024 * 1024, transcendentals=0),
         compiler_params=params(12),
         name="gather",
-    )(plan, entries, *arrived)
-
-
-def moved_kernel(plan, query, held, sums, new_sums):
-    new_sums[...] = sums[...]
-    lane = lax.broadcasted_iota(I32, (1, RANGE), 1)
-    position = jnp.zeros((1, RANGE), I32)
-    for c in range(CTX):
-        start = plan[LOGICAL + c] * BLOCK
-        position = jnp.where(
-            lax.shift_right_logical(lane, 5) == c, start + lane - c * BLOCK, position
-        )
-    for j in range(MOVED):
-
-        @pl.when(plan[VALID + j] > 0)
-        def _(j=j):
-            slot = plan[SLOT + j]
-            keys = held[:, j, 0].reshape(RANGE, FEATURES)
-            values = held[:, j, 1].reshape(RANGE, FEATURES)
-            halves = attend(keys, values, query[slot], position, plan[LENGTH + j])
-            for h in range(2):
-                new_sums[slot, h] = halves[h]
-
-
-def attend_moved(plan, query, held, sums):
-    return pl.pallas_call(
-        moved_kernel,
-        out_shape=jax.ShapeDtypeStruct(sums.shape, BF16),
-        in_specs=[SMEM, VMEM, VMEM, VMEM],
-        out_specs=VMEM,
-        cost_estimate=pl.CostEstimate(flops=0, bytes_accessed=12 * 1024 * 1024, transcendentals=0),
-        compiler_params=params(12),
-        name="moved",
-    )(plan, query, held, sums)
+    )(plan, *arrived)
 
 
 def merge_kernel(parts, out):
@@ -578,7 +537,10 @@
     )(parts)
 
 
-def place_kernel(plan, within, received, cache, new_cache, held, read_sem, write_sem):
+def place_kernel(
+    plan, within, received, cache, own, by0, by1, by2, new_cache, out, held, sent, read_sem, write_sem
+):
+    ctx = lax.axis_index("ctx")
     for j in range(MOVED):
 
         @pl.when(plan[VALID + j] > 0)
@@ -592,14 +554,50 @@
 
             lax.fori_loop(0, CTX, one, 0)
 
+    sent[...] = by0[...].astype(F32) + by1[...].astype(F32) + by2[...].astype(F32)
+    row = lax.broadcasted_iota(I32, (SLOTS, 1), 0)
+    request = jnp.full((SLOTS, 1), -1, I32)
+    for s in range(SLOTS):
+        request = jnp.where(row == s, plan[REQUEST + s], request)
+    stays = jnp.where(lax.axis_index("inst") == INST - 1, 0.0, 1.0)
+    for t in range(STEPS):
+        rows = own[t * SLOTS : (t + 1) * SLOTS, 1024:].astype(F32) * stays
+        for r in range(SLOTS):
+            at = t * SLOTS + r
+            rows = jnp.where(request == r, sent[at : at + 1, 1024:], rows)
+        out[t * SLOTS : (t + 1) * SLOTS, :] = rows
+
     for j in range(MOVED):
 
         @pl.when(plan[VALID + j] > 0)
         def _(j=j):
+            slot = plan[SLOT + j]
+            length = plan[LENGTH + j]
+            r = plan[REQUEST + slot]
             pltpu.make_async_copy(held.at[j], held.at[j], read_sem.at[j]).wait()
-            pltpu.make_async_copy(
-                held.at[j], new_cache.at[:, plan[SLOT + j]], write_sem.at[j]
-            ).start()
+
+            def cut(b, carry):
+                start = (ctx * CTX + b) * BLOCK
+                rows = pl.ds(pl.multiple_of(b * BLOCK, BLOCK), BLOCK)
+
+                @pl.when(start >= length + STEPS)
+                def _():
+                    held[j, :, rows, :] = jnp.zeros((2, BLOCK, FEATURES), BF16)
+
+                @pl.when(jnp.logical_and(start + BLOCK > length, start < length + STEPS))
+                def _():
+                    at = start + lax.broadcasted_iota(I32, (BLOCK, 1), 0)
+                    for kv in range(2):
+                        block = jnp.where(at < length, held[j, kv, rows, :], jnp.zeros((), BF16))
+                        for t in range(STEPS):
+                            new = sent[pl.ds(t * SLOTS + r, 1), kv * 512 : (kv + 1) * 512]
+                            block = jnp.where(at == length + t, new.astype(BF16), block)
+                        held[j, kv, rows, :] = block
+
+                return carry
+
+            lax.fori_loop(0, CTX, cut, 0)
+            pltpu.make_async_copy(held.at[j], new_cache.at[:, slot], write_sem.at[j]).start()
 
     for j in range(MOVED):
 
@@ -610,21 +608,25 @@
             ).wait()
 
 
-def place(plan, within, received, cache):
+def place(plan, within, received, cache, own, by):
     return pl.pallas_call(
         place_kernel,
-        out_shape=jax.ShapeDtypeStruct(cache.shape, BF16),
-        in_specs=[SMEM, SMEM, ANY, HBM],
-        out_specs=HBM,
+        out_shape=[
+            jax.ShapeDtypeStruct(cache.shape, BF16),
+            jax.ShapeDtypeStruct((24, 256), F32),
+        ],
+        in_specs=[SMEM, SMEM, ANY, HBM] + [VMEM] * 4,
+        out_specs=[HBM, VMEM],
         scratch_shapes=[
             pltpu.VMEM((MOVED, 2, RANGE, FEATURES), BF16),
+            pltpu.VMEM((24, 1280), F32),
             pltpu.SemaphoreType.DMA((MOVED,)),
             pltpu.SemaphoreType.DMA((MOVED,)),
         ],
         input_output_aliases={3: 0},
         compiler_params=params(12),
         name="place",
-    )(plan, within, received, cache)
+    )(plan, within, received, cache, own, *by)
 
 
 def swap(x):
@@ -647,21 +649,19 @@
     dest_slot,
     block_order,
 ):
-    by = [up(hidden), down(hidden)]
-    by.append(lax.ppermute(by[0], "inst", [(0, 1)]))
     plan = make_plan(lengths, dest_inst, dest_slot, block_order)
-    *by, plan = after(*by, plan)
     operands = (
-        plan, block_order, cache, hidden, by, norm_gain[None], w_query, key_value_weight, w_out
+        plan, cache, hidden, norm_gain[None], w_query, key_value_weight, w_out, lengths,
+        block_order,
     )
     return lax.switch(
         plan[NEED], [functools.partial(decode, items) for items in ITEMS], *operands
     )
 
 
-def angles(plan):
-    new_len = plan[NEW_LEN : NEW_LEN + SLOTS]
-    token = new_len[None, :] + jnp.arange(STEPS, dtype=I32)[:, None]
+def angles(lengths):
+    own = lax.dynamic_slice_in_dim(lengths, lax.axis_index("inst") * SLOTS, SLOTS)
+    token = own[None, :] + jnp.arange(STEPS, dtype=I32)[:, None]
     half = HEAD_SIZE // 2
     frequency = ROPE_BASE ** (-jnp.arange(half, dtype=F32) * 2.0 / HEAD_SIZE)
     angle = token.astype(F32).reshape(24, 1) * frequency
@@ -683,49 +683,46 @@
     return lax.ppermute(from_up, "inst", [(0, 1)]), lax.ppermute(from_down, "inst", [(2, 1)])
 
 
-def decode(items, plan, order, cache, hidden, by, gain, w_query, w_kv, w_out):
+def decode(items, plan, cache, hidden, gain, w_query, w_kv, w_out, lengths, order):
     packed_up, packed_down = pack(0, items[0], plan, cache)
     up_0, down_0 = up(packed_up), down(packed_down)
-    hidden, plan, packed_up = after(hidden, plan, packed_up)
-    cosine, sine = angles(plan)
-    projected, within = project(plan, order, hidden, by, gain, w_query, w_kv)
+    first = lax.axis_index("head") == 0
+    hidden, lengths, packed_up, first = after(hidden, lengths, packed_up, first)
+    cosine, sine = angles(lengths)
+    projected, within = project(hidden, order, gain, w_query, w_kv)
     projected, cosine, sine, plan = after(projected, cosine, sine, plan)
     packed_up, packed_down = pack(items[0], items[1], plan, cache)
-    parts, up_0, down_0, packed_up, packed_down = after(
-        swap(projected), up_0, down_0, packed_up, packed_down
-    )
+    parts, packed_up, packed_down = after(swap(projected), packed_up, packed_down)
     up_1, down_1 = up(packed_up), down(packed_down)
-    up_on, down_on = pass_on(up_0, down_0)
     turned = swap(rotate(parts, cosine, sine))
     turned = turned.reshape(32, STEPS, SLOTS, HEAD_SIZE)
     query = turned[:24].reshape(2, 12, STEPS, SLOTS, HEAD_SIZE).transpose(3, 0, 1, 2, 4)
     query = query.reshape(SLOTS, 2, 36, HEAD_SIZE)
     query = jnp.pad(query, ((0, 0), (0, 0), (0, HALF_ROWS - 36), (0, 0)))
     query = query.reshape(SLOTS, 2 * HALF_ROWS, HEAD_SIZE)
-    entries = turned[24:].reshape(2, 4, STEPS, SLOTS, HEAD_SIZE).transpose(3, 0, 2, 1, 4)
-    entries = entries.reshape(SLOTS, 2, STEPS, FEATURES)
+    rows = turned[24:].reshape(8, 24, HEAD_SIZE).transpose(1, 0, 2).reshape(24, 1024)
+    entries = rows.reshape(STEPS, SLOTS, 2, FEATURES).transpose(1, 2, 0, 3)
     entries = jnp.pad(entries, ((0, 0), (0, 0), (0, 8 - STEPS), (0, 0)))
 
-    new_cache, sums = stay(plan, cache, query, entries)
-    entries, sums = after(entries, sums)
-    arrived = [up_0, up_1, down_0, down_1, up_on, down_on]
-    held = gather(items, plan, entries, arrived)
-    sums = attend_moved(plan, query, held, sums)
-    sums, held = after(swap(sums.reshape(CTX, HALF_ROWS, HEAD_SIZE)), held)
-    sums, received = after(sums, swap(held))
-    attended = swap(merge(sums))
-    new_cache = place(plan, within, received, new_cache)
-    attended, new_cache = after(attended, new_cache)
-
+    new_cache, sums = attend_slots(lengths, order, cache, query, entries)
+    sums, up_0, down_0 = after(sums, up_0, down_0)
+    up_on, down_on = pass_on(up_0, down_0)
+    attended = swap(merge(swap(sums.reshape(CTX, HALF_ROWS, HEAD_SIZE))))
     attended = attended[:, :36].reshape(SLOTS, 2, 12, STEPS, HEAD_SIZE)
     attended = attended.transpose(3, 0, 1, 2, 4).reshape(24, 24 * HEAD_SIZE)
     projected = jnp.dot(attended, w_out, preferred_element_type=F32)
+    projected, up_1 = after(projected, up_1)
+    held = gather(items, plan, [up_0, up_1, down_0, down_1, up_on, down_on])
     mine, other = projected[:, :192], projected[:, 192:]
-    first = lax.axis_index("head") == 0
     keep = jnp.where(first, mine, other)
     send_half = jnp.where(first, other, mine).astype(BF16)
     got = lax.ppermute(send_half, "head", [(0, 1), (1, 0)])
     attn_out = (keep + got.astype(F32)).astype(BF16)
+    own = jnp.concatenate([rows, attn_out, jnp.zeros((24, 64), BF16)], axis=1)
+    by = [lax.ppermute(own, "inst", [(INST - 1, i)]) for i in range(INST - 1)]
+    *by, own, held = after(*by, own, held)
+    new_cache, attn_out = place(plan, within, swap(held), new_cache, own, by)
+    attn_out = attn_out[:, :192].astype(BF16)
     return new_cache, attn_out.reshape(STEPS, SLOTS, 192)
 
 

time: 162 us -> 151 us (0.932)
  waiting for transfers between devices: 20.1 us -> 15.1 us
  Pallas kernels: 32.2 us -> 28.5 us
  blocking collectives: 69.3 us -> 71.7 us
  starting transfers between devices: 31.5 us -> 29.3 us
  matrix products: 2.08 us -> 0.43 us
    ppermute x3 -> x2, waiting for transfers between devices: 7.99 us -> 0.01 us  [up(): return lax.ppermute(x, 'inst', [(INST - 1, 0)])]
    ppermute x1 -> x3, waiting for transfers between devices: 0.01 us -> 4.35 us  [decode(): by = [lax.ppermute(own, 'inst', [(INST - 1, i)]) for i in range(INST - 1)]]
    all_to_all x2 -> x1, starting transfers between devices: 11.7 us -> 8.43 us  [swap(): return lax.all_to_all(x, 'ctx', split_axis=0, concat_axis=0, tiled=True)]
    all_to_all x3 -> x4, blocking collectives: 69.3 us -> 71.7 us  [swap(): return lax.all_to_all(x, 'ctx', split_axis=0, concat_axis=0, tiled=True)]
    ppermute x1, starting transfers between devices: 2.32 us -> 4.54 us  [pass_on(): lax.ppermute(from_up, 'inst', [(0, 1)])]
    ppermute x1, starting transfers between devices: 7.38 us -> 5.5 us  [decode(): got = lax.ppermute(send_half, 'head', [(0, 1), (1, 0)])]
    dot_general x1, matrix products: 2.08 us -> 0.43 us  [decode(): projected = jnp.dot(attended, w_out, preferred_element_type=F32)]
    all_to_all x2 -> x1, waiting for transfers between devices: 11.2 us -> 9.88 us  [swap(): return lax.all_to_all(x, 'ctx', split_axis=0, concat_axis=0, tiled=True)]
  transfers between devices with their start and end apart: 12 -> 11, of which waited for: 6 -> 3; matrix products, arithmetic and copies ran while one was open for 1% -> 1% of each run, Pallas kernels for 15% -> 13%
where the time goes in v4:
time: 151 us; the launch traced here: 149 us
  blocking collectives  71.7 us (47%)
  starting transfers between devices  29.3 us (19%)
  Pallas kernels  28.5 us (19%)
  waiting for transfers between devices  15.1 us (10%)
  local copies, waits for them, and re-layouts  2.4 us (2%)
    all_to_all x4, blocking collectives, swap(): return lax.all_to_all(x, 'ctx', split_axis=0, concat_axis=0, tiled=True)  71.7 us
    pallas_call x1, Pallas kernels, attend_slots(): pl.pallas_call(attend_kernel, out_shape=[jax.ShapeDtypeStruct(cache.shape...  12.1 us
    all_to_all x1, waiting for transfers between devices, swap(): return lax.all_to_all(x, 'ctx', split_axis=0, concat_axis=0, tiled=True)  9.88 us
    all_to_all x1, starting transfers between devices, swap(): return lax.all_to_all(x, 'ctx', split_axis=0, concat_axis=0, tiled=True)  8.43 us
    ppermute x1, starting transfers between devices, decode(): got = lax.ppermute(send_half, 'head', [(0, 1), (1, 0)])  5.5 us
    pallas_call x1, Pallas kernels, place(): pl.pallas_call(place_kernel, out_shape=[jax.ShapeDtypeStruct(cache.shape,...  5.15 us
    ppermute x1, starting transfers between devices, pass_on(): lax.ppermute(from_up, 'inst', [(0, 1)])  4.54 us
    ppermute x3, waiting for transfers between devices, decode(): by = [lax.ppermute(own, 'inst', [(INST - 1, i)]) for i in range(INST - 1)]  4.35 us
  transfers between devices with their start and end apart: 11, of which 3 were waited for; matrix products, arithmetic and copies ran while one was open for 1% of the time, Pallas kernels for 13%

profile of v4, /device:TPU:1, one launch (start us, length us, event | category | flops | bytes accessed | tf_op | source)
XLA Modules:
  0.0 149.4 jit_solution(7101972473995651717)
XLA Ops:
  0.6 3.2 %plan.1 = s32[416]{0:T(512)S(1)} custom-call(s32[32]{0:T(128)} %lengths.1, s32[8]{0:T(128)} %dest_inst.1, s32[8]{0:T(128)} %dest_slot.1, s32[256]{0:T(256)} %order.1), custom_call_target="tpu_custom_call" | custom-call | tf_op jit(solution)/shard_map/plan/pallas_call | solution.py:141
  3.8 0.7 broadcast_in_dim.31
  4.5 0.6 slice.66
  5.8 143.7 %conditional.1 = (bf16[2,8,512,512]{3,2,1,0:T(8,128)(2,1)}, bf16[3,8,192]{2,1,0:T(8,128)(2,1)}) conditional(s32[]{:T(128)} %bitcast.36, (s32[416]{0:T(512)S(1)}, bf16[2,8,512,512]{3,2,1,0:T(8,128)(2,1)}, bf16[3,8,384]{2,1,0:T(8,128)(2,1)}, s32[32]{0:T(128)}, s32[256]{0:T(256)}, /*index=5*/bf16[1,384]{1,0:T(2,128)(2,1)S(1)}, ...), branch_computations={%region_0.1_spmd, %region_1.2_spmd, %region_2.3_spmd} | conditional | flops 157321904 | bytes 155730128 | solution.py:657
  5.8 0.6 pack.6
  6.5 1.4 collective-permute-start
  7.9 1.9 %collective-permute-start.1 = (bf16[22,2,32,512]{3,2,1,0:T(8,128)(2,1)}, bf16[22,2,32,512]{3,2,1,0:T(8,128)(2,1)}, u32[]{:S(2)}, u32[]{:S(2)}) collective-permute-start(bf16[22,2,32,512]{3,2,1,0:T(8,128)(2,1)} %get-tuple-element.76), channel_id=1, source_target_pairs={{96,64},{97,65},{98,66},{99,67},{100,68},{101,69},{102,70},{103,71... | collective-permute-start | bytes 4325384 | tf_op jit(solution)/shard_map/cond/branch_0_fun/ppermute | solution.py:679
  10.1 3.5 %project.3 = (f32[16,32,256]{2,1,0:T(8,128)}, s32[16]{0:T(128)S(1)}) custom-call(bf16[3,8,384]{2,1,0:T(8,128)(2,1)S(1)} %copy-done.9, s32[256]{0:T(256)S(1)} %copy-done.12, bf16[1,384]{1,0:T(2,128)(2,1)S(1)} %get-tuple-element.61.gain, bf16[384,3072]{1,0:T(8,128)(2,1)S(1)} %copy-done.3, bf16[2,384,512]{2,1,0:T(8,128)(2,1)S(1)} %copy-done.6), custom_call_target="tpu_custom_call" | custom-call | flops 100663296 | bytes 3145728 | tf_op jit(solution)/shard_map/cond/branch_0_fun/project/pallas_call | solution.py:261
  13.7 8.4 %all-to-all-start = ((f32[16,32,256]{2,1,0:T(8,128)}), f32[16,32,256]{2,1,0:T(8,128)S(1)}, u32[]{:S(2)}, u32[]{:S(2)}) async-start(f32[16,32,256]{2,1,0:T(8,128)} %get-tuple-element.68), calls=%async_computation | async-start | bytes 1048576 | tf_op jit(solution)/shard_map/cond/branch_0_fun/all_to_all | solution.py:633
  22.1 0.6 pack.7
  22.7 9.9 %all-to-all-done.parts = f32[16,32,256]{2,1,0:T(8,128)S(1)} async-done(((f32[16,32,256]{2,1,0:T(8,128)}), f32[16,32,256]{2,1,0:T(8,128)S(1)}, u32[]{:S(2)}, u32[]{:S(2)}) %all-to-all-start) | async-done | bytes 524320 | tf_op jit(solution)/shard_map/cond/branch_0_fun/all_to_all | solution.py:633
  32.6 1.3 collective-permute-start.2
  33.9 1.9 %collective-permute-start.7 = (bf16[26,2,32,512]{3,2,1,0:T(8,128)(2,1)}, bf16[26,2,32,512]{3,2,1,0:T(8,128)(2,1)}, u32[]{:S(2)}, u32[]{:S(2)}) collective-permute-start(bf16[26,2,32,512]{3,2,1,0:T(8,128)(2,1)} %get-tuple-element.84), channel_id=1, source_target_pairs={{96,64},{97,65},{98,66},{99,67},{100,68},{101,69},{102,70},{103,71... | collective-permute-start | bytes 5111816 | tf_op jit(solution)/shard_map/cond/branch_0_fun/ppermute | solution.py:679
  35.8 0.2 rotate.3
  36.0 10.4 %all_to_all.60 = bf16[16,2,24,128]{3,2,1,0:T(8,128)(2,1)S(1)} all-to-all(bf16[16,2,24,128]{3,2,1,0:T(8,128)(2,1)S(1)} %rotate.3), channel_id=1, replica_groups=mesh['inst'=4,'ctx'=16,'head'=2] {'ctx'}, dimensions={0} | all-to-all | bytes 393216 | tf_op jit(solution)/shard_map/cond/branch_0_fun/all_to_all | solution.py:633
  46.6 12.1 %attend_slots.3 = (bf16[2,8,512,512]{3,2,1,0:T(8,128)(2,1)}, bf16[8,2,48,128]{3,2,1,0:T(8,128)(2,1)S(1)}) custom-call(s32[32]{0:T(128)S(1)} %copy-done.15, s32[256]{0:T(256)S(1)} %copy-done.12, bf16[2,8,512,512]{3,2,1,0:T(8,128)(2,1)} %get-tuple-element.57.cache, bf16[8,96,128]{2,1,0:T(8,128)(2,1)S(1)} %bitcast.79, bf16[8,2,8,512]{3,2,1,0:T(8,128)(2,1)S(1)} %pad.15.entries), custom_call_target="tpu_custom_call" | custom-call | bytes 33554432 | tf_op jit(solution)/shard_map/cond/branch_0_fun/attend_slots/pallas_call | solution.py:424
  58.7 4.5 %collective-permute-start.8 = (bf16[22,2,32,512]{3,2,1,0:T(8,128)(2,1)}, bf16[22,2,32,512]{3,2,1,0:T(8,128)(2,1)}, u32[]{:S(2)}, u32[]{:S(2)}) collective-permute-start(bf16[22,2,32,512]{3,2,1,0:T(8,128)(2,1)} %collective-permute-done.refs_0_), channel_id=1, source_target_pairs={{0,32},{1,33},{2,34},{3,35},{4,36},{5,37},{6,38},{7,39},{8,40},{9,... | collective-permute-start | bytes 4325384 | tf_op jit(solution)/shard_map/cond/branch_0_fun/ppermute | solution.py:683
  63.3 1.8 %collective-permute-start.9 = (bf16[22,2,32,512]{3,2,1,0:T(8,128)(2,1)}, bf16[22,2,32,512]{3,2,1,0:T(8,128)(2,1)}, u32[]{:S(2)}, u32[]{:S(2)}) collective-permute-start(bf16[22,2,32,512]{3,2,1,0:T(8,128)(2,1)} %collective-permute-done.1.refs_2_), channel_id=1, source_target_pairs={{64,32},{65,33},{66,34},{67,35},{68,36},{69,37},{70,38},{71,39},{7... | collective-permute-start | bytes 4325384 | tf_op jit(solution)/shard_map/cond/branch_0_fun/ppermute | solution.py:683
  65.0 9.8 %all_to_all.61.parts = bf16[16,48,128]{2,1,0:T(8,128)(2,1)S(1)} all-to-all(bf16[16,48,128]{2,1,0:T(8,128)(2,1)S(1)} %bitcast.82), channel_id=1, replica_groups=mesh['inst'=4,'ctx'=16,'head'=2] {'ctx'}, dimensions={0} | all-to-all | bytes 393216 | tf_op jit(solution)/shard_map/cond/branch_0_fun/all_to_all | solution.py:633
  74.9 0.2 merge.3
  75.1 10.2 %all_to_all.62 = bf16[16,48,128]{2,1,0:T(8,128)(2,1)S(1)} all-to-all(bf16[16,48,128]{2,1,0:T(8,128)(2,1)S(1)} %merge.3), channel_id=1, replica_groups=mesh['inst'=4,'ctx'=16,'head'=2] {'ctx'}, dimensions={0} | all-to-all | bytes 393216 | tf_op jit(solution)/shard_map/cond/branch_0_fun/all_to_all | solution.py:633
  85.4 0.4 fusion.12
  85.9 5.5 %collective-permute-start.3 = (bf16[24,192]{1,0:T(8,128)(2,1)S(1)}, bf16[24,192]{1,0:T(8,128)(2,1)S(1)}, u32[]{:S(2)}, u32[]{:S(2)}) collective-permute-start(bf16[24,192]{1,0:T(8,128)(2,1)S(1)} %select_convert_fusion), channel_id=1, source_target_pairs={{0,1},{1,0},{2,3},{3,2},{4,5},{5,4},{6,7},{7,6},{8,9},{9,8},{10,11... | collective-permute-start | bytes 27656 | tf_op jit(solution)/shard_map/cond/branch_0_fun/ppermute | solution.py:719
  91.4 0.8 collective-permute-done.3
  92.4 1.3 collective-permute-start.4
  93.7 0.7 collective-permute-start.5
  94.4 0.7 collective-permute-start.6
  95.1 3.0 %gather.3 = bf16[16,3,2,32,512]{4,3,2,1,0:T(8,128)(2,1)S(1)} custom-call(s32[416]{0:T(512)S(1)} %get-tuple-element.66.plan, bf16[22,2,32,512]{3,2,1,0:T(8,128)(2,1)} %collective-permute-done.refs_0_, bf16[26,2,32,512]{3,2,1,0:T(8,128)(2,1)S(1)} %collective-permute-done.2.refs_1_, bf16[22,2,32,512]{3,2,1,0:T(8,128)(2,1)} %collective-permute-done.1.refs_2_, ...), custom_call_target="tpu_custom_call" | custom-call | bytes 8388608 | tf_op jit(solution)/shard_map/cond/branch_0_fun/gather/pallas_call | solution.py:497
  98.1 4.3 %collective-permute-done.4.by0 = bf16[24,1280]{1,0:T(8,128)(2,1)S(1)} collective-permute-done((bf16[24,1280]{1,0:T(8,128)(2,1)S(1)}, bf16[24,1280]{1,0:T(8,128)(2,1)S(1)}, u32[]{:S(2)}, u32[]{:S(2)}) %collective-permute-start.4) | collective-permute-done | bytes 61472 | tf_op jit(solution)/shard_map/cond/branch_0_fun/ppermute | solution.py:722
  102.4 41.3 %all_to_all.63.received = bf16[16,3,2,32,512]{4,3,2,1,0:T(8,128)(2,1)S(1)} all-to-all(bf16[16,3,2,32,512]{4,3,2,1,0:T(8,128)(2,1)S(1)} %gather.3), channel_id=1, replica_groups=mesh['inst'=4,'ctx'=16,'head'=2] {'ctx'}, dimensions={0} | all-to-all | bytes 6291456 | tf_op jit(solution)/shard_map/cond/branch_0_fun/all_to_all | solution.py:633
  143.7 5.1 %place.3 = (bf16[2,8,512,512]{3,2,1,0:T(8,128)(2,1)}, f32[24,256]{1,0:T(8,128)S(1)}) custom-call(s32[416]{0:T(512)S(1)} %get-tuple-element.66.plan, s32[16]{0:T(128)S(1)} %get-tuple-element.67.within, bf16[16,3,2,32,512]{4,3,2,1,0:T(8,128)(2,1)S(1)} %all_to_all.63.received, ...), custom_call_target="tpu_custom_call", output_to_operand_aliasing={{0}: (3, {})} | custom-call | tf_op jit(solution)/shard_map/cond/branch_0_fun/place/pallas_call | solution.py:612
  148.8 0.6 fusion.2
  (42 shorter events, 0.9 us)
Async XLA Ops:
  5.8 4.0 %copy-start.15 = (s32[32]{0:T(128)S(1)}, s32[32]{0:T(128)}, u32[]{:S(2)}) copy-start(s32[32]{0:T(128)} %get-tuple-element.65.lengths) | copy-start | bytes 388 | tf_op jit(solution)/shard_map/cond
  5.8 4.3 %copy-start.3 = (bf16[384,3072]{1,0:T(8,128)(2,1)S(1)}, bf16[384,3072]{1,0:T(8,128)(2,1)}, u32[]{:S(2)}) copy-start(bf16[384,3072]{1,0:T(8,128)(2,1)} %get-tuple-element.62.w_query) | copy-start | bytes 7077892 | tf_op jit(solution)/shard_map/cond
  5.8 4.3 %copy-start.6 = (bf16[2,384,512]{2,1,0:T(8,128)(2,1)S(1)}, bf16[2,384,512]{2,1,0:T(8,128)(2,1)}, u32[]{:S(2)}) copy-start(bf16[2,384,512]{2,1,0:T(8,128)(2,1)} %get-tuple-element.63.w_kv) | copy-start | bytes 2359300 | tf_op jit(solution)/shard_map/cond
  5.8 4.3 %copy-start.9 = (bf16[3,8,384]{2,1,0:T(8,128)(2,1)S(1)}, bf16[3,8,384]{2,1,0:T(8,128)(2,1)}, u32[]{:S(2)}) copy-start(bf16[3,8,384]{2,1,0:T(8,128)(2,1)} %get-tuple-element.59.hidden) | copy-start | bytes 55300 | tf_op jit(solution)/shard_map/cond
  5.8 4.3 %copy-start.12 = (s32[256]{0:T(256)S(1)}, s32[256]{0:T(256)}, u32[]{:S(2)}) copy-start(s32[256]{0:T(256)} %get-tuple-element.60.order) | copy-start | bytes 3076 | tf_op jit(solution)/shard_map/cond
  6.5 52.3 %collective-permute-start = (bf16[22,2,32,512]{3,2,1,0:T(8,128)(2,1)}, bf16[22,2,32,512]{3,2,1,0:T(8,128)(2,1)}, u32[]{:S(2)}, u32[]{:S(2)}) collective-permute-start(bf16[22,2,32,512]{3,2,1,0:T(8,128)(2,1)} %get-tuple-element.58), channel_id=1, source_target_pairs={{96,0},{97,1},{98,2},{99,3},{100,4},{101,5},{102,6},{103,7},{104,8... | collective-permute-start | bytes 4325384 | tf_op jit(solution)/shard_map/cond/branch_0_fun/ppermute | solution.py:675
  7.9 50.8 %collective-permute-start.1 = (bf16[22,2,32,512]{3,2,1,0:T(8,128)(2,1)}, bf16[22,2,32,512]{3,2,1,0:T(8,128)(2,1)}, u32[]{:S(2)}, u32[]{:S(2)}) collective-permute-start(bf16[22,2,32,512]{3,2,1,0:T(8,128)(2,1)} %get-tuple-element.76), channel_id=1, source_target_pairs={{96,64},{97,65},{98,66},{99,67},{100,68},{101,69},{102,70},{103,71... | collective-permute-start | bytes 4325384 | tf_op jit(solution)/shard_map/cond/branch_0_fun/ppermute | solution.py:679
  13.7 18.9 %all-to-all-start = ((f32[16,32,256]{2,1,0:T(8,128)}), f32[16,32,256]{2,1,0:T(8,128)S(1)}, u32[]{:S(2)}, u32[]{:S(2)}) async-start(f32[16,32,256]{2,1,0:T(8,128)} %get-tuple-element.68), calls=%async_computation | async-start | bytes 1048576 | tf_op jit(solution)/shard_map/cond/branch_0_fun/all_to_all | solution.py:633
  32.6 53.2 %collective-permute-start.2 = (bf16[26,2,32,512]{3,2,1,0:T(8,128)(2,1)}, bf16[26,2,32,512]{3,2,1,0:T(8,128)(2,1)S(1)}, u32[]{:S(2)}, u32[]{:S(2)}) collective-permute-start(bf16[26,2,32,512]{3,2,1,0:T(8,128)(2,1)} %get-tuple-element.79), channel_id=1, source_target_pairs={{96,0},{97,1},{98,2},{99,3},{100,4},{101,5},{102,6},{103,7},{104,8... | collective-permute-start | bytes 5111816 | tf_op jit(solution)/shard_map/cond/branch_0_fun/ppermute | solution.py:675
  33.9 60.5 %collective-permute-start.7 = (bf16[26,2,32,512]{3,2,1,0:T(8,128)(2,1)}, bf16[26,2,32,512]{3,2,1,0:T(8,128)(2,1)}, u32[]{:S(2)}, u32[]{:S(2)}) collective-permute-start(bf16[26,2,32,512]{3,2,1,0:T(8,128)(2,1)} %get-tuple-element.84), channel_id=1, source_target_pairs={{96,64},{97,65},{98,66},{99,67},{100,68},{101,69},{102,70},{103,71... | collective-permute-start | bytes 5111816 | tf_op jit(solution)/shard_map/cond/branch_0_fun/ppermute | solution.py:679
  46.6 38.7 %copy-start = (bf16[3072,384]{1,0:T(8,128)(2,1)S(1)}, bf16[3072,384]{1,0:T(8,128)(2,1)}, u32[]{:S(2)}) copy-start(bf16[3072,384]{1,0:T(8,128)(2,1)} %get-tuple-element.78) | copy-start | bytes 7077892 | tf_op jit(solution)/shard_map/cond
  58.7 36.3 %collective-permute-start.8 = (bf16[22,2,32,512]{3,2,1,0:T(8,128)(2,1)}, bf16[22,2,32,512]{3,2,1,0:T(8,128)(2,1)}, u32[]{:S(2)}, u32[]{:S(2)}) collective-permute-start(bf16[22,2,32,512]{3,2,1,0:T(8,128)(2,1)} %collective-permute-done.refs_0_), channel_id=1, source_target_pairs={{0,32},{1,33},{2,34},{3,35},{4,36},{5,37},{6,38},{7,39},{8,40},{9,... | collective-permute-start | bytes 4325384 | tf_op jit(solution)/shard_map/cond/branch_0_fun/ppermute | solution.py:683
  63.3 31.8 %collective-permute-start.9 = (bf16[22,2,32,512]{3,2,1,0:T(8,128)(2,1)}, bf16[22,2,32,512]{3,2,1,0:T(8,128)(2,1)}, u32[]{:S(2)}, u32[]{:S(2)}) collective-permute-start(bf16[22,2,32,512]{3,2,1,0:T(8,128)(2,1)} %collective-permute-done.1.refs_2_), channel_id=1, source_target_pairs={{64,32},{65,33},{66,34},{67,35},{68,36},{69,37},{70,38},{71,39},{7... | collective-permute-start | bytes 4325384 | tf_op jit(solution)/shard_map/cond/branch_0_fun/ppermute | solution.py:683
  85.9 6.3 %collective-permute-start.3 = (bf16[24,192]{1,0:T(8,128)(2,1)S(1)}, bf16[24,192]{1,0:T(8,128)(2,1)S(1)}, u32[]{:S(2)}, u32[]{:S(2)}) collective-permute-start(bf16[24,192]{1,0:T(8,128)(2,1)S(1)} %select_convert_fusion), channel_id=1, source_target_pairs={{0,1},{1,0},{2,3},{3,2},{4,5},{5,4},{6,7},{7,6},{8,9},{9,8},{10,11... | collective-permute-start | bytes 27656 | tf_op jit(solution)/shard_map/cond/branch_0_fun/ppermute | solution.py:719
  92.4 10.0 %collective-permute-start.4 = (bf16[24,1280]{1,0:T(8,128)(2,1)S(1)}, bf16[24,1280]{1,0:T(8,128)(2,1)S(1)}, u32[]{:S(2)}, u32[]{:S(2)}) collective-permute-start(bf16[24,1280]{1,0:T(8,128)(2,1)S(1)} %concatenate.20.own), channel_id=1, source_target_pairs={{96,0},{97,1},{98,2},{99,3},{100,4},{101,5},{102,6},{103,7},{104,8... | collective-permute-start | bytes 184328 | tf_op jit(solution)/shard_map/cond/branch_0_fun/ppermute | solution.py:722
  93.7 8.7 %collective-permute-start.5 = (bf16[24,1280]{1,0:T(8,128)(2,1)S(1)}, bf16[24,1280]{1,0:T(8,128)(2,1)S(1)}, u32[]{:S(2)}, u32[]{:S(2)}) collective-permute-start(bf16[24,1280]{1,0:T(8,128)(2,1)S(1)} %concatenate.20.own), channel_id=1, source_target_pairs={{96,32},{97,33},{98,34},{99,35},{100,36},{101,37},{102,38},{103,39... | collective-permute-start | bytes 184328 | tf_op jit(solution)/shard_map/cond/branch_0_fun/ppermute | solution.py:722
  94.4 8.0 %collective-permute-start.6 = (bf16[24,1280]{1,0:T(8,128)(2,1)S(1)}, bf16[24,1280]{1,0:T(8,128)(2,1)S(1)}, u32[]{:S(2)}, u32[]{:S(2)}) collective-permute-start(bf16[24,1280]{1,0:T(8,128)(2,1)S(1)} %concatenate.20.own), channel_id=1, source_target_pairs={{96,64},{97,65},{98,66},{99,67},{100,68},{101,69},{102,70},{103,71... | collective-permute-start | bytes 184328 | tf_op jit(solution)/shard_map/cond/branch_0_fun/ppermute | solution.py:722

commit v5 on v4

--- a/solution.py
+++ b/solution.py
@@ -382,15 +382,13 @@
                 lax.shift_right_logical(lane, 5) == b, start + lane - b * BLOCK, position
             )
 
+        new_cache[...] = cache[...]
+
         def build(b, carry):
             start = jnp.where(retires, order[ctx * CTX + b], ctx * CTX + b) * BLOCK
             rows = pl.ds(pl.multiple_of(b * BLOCK, BLOCK), BLOCK)
 
-            @pl.when(start + BLOCK <= length)
-            def _():
-                new_cache[:, 0, rows, :] = cache[:, 0, rows, :]
-
-            @pl.when(start >= length + STEPS)
+            @pl.when(jnp.logical_and(start >= length + STEPS, jnp.logical_not(retires)))
             def _():
                 new_cache[:, 0, rows, :] = jnp.zeros((2, BLOCK, FEATURES), BF16)
 
@@ -405,7 +403,8 @@
 
             return carry
 
-        lax.fori_loop(0, CTX, build, 0)
+        whole = jnp.logical_and(jnp.logical_not(retires), (ctx + 1) * RANGE <= length)
+        lax.fori_loop(0, jnp.where(whole, 0, CTX), build, 0)
         halves = attend(new_cache[0, 0], new_cache[1, 0], query[0], position, length)
         for h in range(2):
             sums[0, h] = halves[h]
@@ -538,22 +537,10 @@
 
 
 def place_kernel(
-    plan, within, received, cache, own, by0, by1, by2, new_cache, out, held, sent, read_sem, write_sem
+    plan, within, received, cache, own, by0, by1, by2, new_cache, out, fixed, empty, sent, sem
 ):
     ctx = lax.axis_index("ctx")
-    for j in range(MOVED):
-
-        @pl.when(plan[VALID + j] > 0)
-        def _(j=j):
-            def one(d, carry):
-                rows = pl.ds(pl.multiple_of(within[d] * BLOCK, BLOCK), BLOCK)
-                pltpu.make_async_copy(
-                    received.at[d, j], held.at[j, :, rows, :], read_sem.at[j]
-                ).start()
-                return carry
-
-            lax.fori_loop(0, CTX, one, 0)
-
+    empty[...] = jnp.zeros_like(empty)
     sent[...] = by0[...].astype(F32) + by1[...].astype(F32) + by2[...].astype(F32)
     row = lax.broadcasted_iota(I32, (SLOTS, 1), 0)
     request = jnp.full((SLOTS, 1), -1, I32)
@@ -574,38 +561,43 @@
             slot = plan[SLOT + j]
             length = plan[LENGTH + j]
             r = plan[REQUEST + slot]
-            pltpu.make_async_copy(held.at[j], held.at[j], read_sem.at[j]).wait()
-
-            def cut(b, carry):
+
+            def one(d, carry):
+                b = within[d]
                 start = (ctx * CTX + b) * BLOCK
                 rows = pl.ds(pl.multiple_of(b * BLOCK, BLOCK), BLOCK)
+                target = new_cache.at[:, slot, rows, :]
+
+                @pl.when(start + BLOCK <= length)
+                def _():
+                    pltpu.make_async_copy(received.at[d, j], target, sem.at[j]).start()
 
                 @pl.when(start >= length + STEPS)
                 def _():
-                    held[j, :, rows, :] = jnp.zeros((2, BLOCK, FEATURES), BF16)
+                    pltpu.make_async_copy(empty, target, sem.at[j]).start()
 
                 @pl.when(jnp.logical_and(start + BLOCK > length, start < length + STEPS))
                 def _():
                     at = start + lax.broadcasted_iota(I32, (BLOCK, 1), 0)
+                    half = lax.bitwise_and(b, 1)
                     for kv in range(2):
-                        block = jnp.where(at < length, held[j, kv, rows, :], jnp.zeros((), BF16))
+                        block = jnp.where(at < length, received[d, j, kv], jnp.zeros((), BF16))
                         for t in range(STEPS):
                             new = sent[pl.ds(t * SLOTS + r, 1), kv * 512 : (kv + 1) * 512]
                             block = jnp.where(at == length + t, new.astype(BF16), block)
-                        held[j, kv, rows, :] = block
+                        fixed[j, half, kv] = block
+                    pltpu.make_async_copy(fixed.at[j, half], target, sem.at[j]).start()
 
                 return carry
 
-            lax.fori_loop(0, CTX, cut, 0)
-            pltpu.make_async_copy(held.at[j], new_cache.at[:, slot], write_sem.at[j]).start()
+            lax.fori_loop(0, CTX, one, 0)
 
     for j in range(MOVED):
 
         @pl.when(plan[VALID + j] > 0)
         def _(j=j):
-            pltpu.make_async_copy(
-                held.at[j], new_cache.at[:, plan[SLOT + j]], write_sem.at[j]
-            ).wait()
+            whole = new_cache.at[:, plan[SLOT + j]]
+            pltpu.make_async_copy(whole, whole, sem.at[j]).wait()
 
 
 def place(plan, within, received, cache, own, by):
@@ -615,12 +607,12 @@
             jax.ShapeDtypeStruct(cache.shape, BF16),
             jax.ShapeDtypeStruct((24, 256), F32),
         ],
-        in_specs=[SMEM, SMEM, ANY, HBM] + [VMEM] * 4,
+        in_specs=[SMEM, SMEM, VMEM, HBM] + [VMEM] * 4,
         out_specs=[HBM, VMEM],
         scratch_shapes=[
-            pltpu.VMEM((MOVED, 2, RANGE, FEATURES), BF16),
+            pltpu.VMEM((MOVED, 2, 2, BLOCK, FEATURES), BF16),
+            pltpu.VMEM((2, BLOCK, FEATURES), BF16),
             pltpu.VMEM((24, 1280), F32),
-            pltpu.SemaphoreType.DMA((MOVED,)),
             pltpu.SemaphoreType.DMA((MOVED,)),
         ],
         input_output_aliases={3: 0},

time: 151 us -> 148 us (0.980)
  Pallas kernels: 28.5 us -> 23.9 us
    pallas_call x1, Pallas kernels: 5.15 us -> 2.26 us  [place(): pl.pallas_call(place_kernel, out_shape=[jax.ShapeDtypeStruct(cache.shape,...]
  transfers between devices with their start and end apart: 11 -> 11, of which waited for: 3 -> 3; matrix products, arithmetic and copies ran while one was open for 1% -> 1% of each run, Pallas kernels for 13% -> 12%
where the time goes in v5:
time: 148 us; the launch traced here: 146 us
  blocking collectives  72.1 us (49%)
  starting transfers between devices  28.9 us (20%)
  Pallas kernels  23.9 us (16%)
  waiting for transfers between devices  16.4 us (11%)
  local copies, waits for them, and re-layouts  2.4 us (2%)
    all_to_all x4, blocking collectives, swap(): return lax.all_to_all(x, 'ctx', split_axis=0, concat_axis=0, tiled=True)  72.1 us
    pallas_call x1, Pallas kernels, attend_slots(): pl.pallas_call(attend_kernel, out_shape=[jax.ShapeDtypeStruct(cache.shape...  10.9 us
    all_to_all x1, waiting for transfers between devices, swap(): return lax.all_to_all(x, 'ctx', split_axis=0, concat_axis=0, tiled=True)  9.88 us
    all_to_all x1, starting transfers between devices, swap(): return lax.all_to_all(x, 'ctx', split_axis=0, concat_axis=0, tiled=True)  8.43 us
    ppermute x3, waiting for transfers between devices, decode(): by = [lax.ppermute(own, 'inst', [(INST - 1, i)]) for i in range(INST - 1)]  5.66 us
    ppermute x1, starting transfers between devices, decode(): got = lax.ppermute(send_half, 'head', [(0, 1), (1, 0)])  5.51 us
    ppermute x1, starting transfers between devices, pass_on(): lax.ppermute(from_up, 'inst', [(0, 1)])  4.11 us
    ppermute x2, starting transfers between devices, down(): return lax.ppermute(x, 'inst', [(INST - 1, 2)])  3.72 us
  transfers between devices with their start and end apart: 11, of which 3 were waited for; matrix products, arithmetic and copies ran while one was open for 1% of the time, Pallas kernels for 12%

profile of v5, /device:TPU:1, one launch (start us, length us, event | category | flops | bytes accessed | tf_op | source)
XLA Modules:
  0.0 146.0 jit_solution(2952090875450654153)
XLA Ops:
  0.6 3.0 %plan.1 = s32[416]{0:T(512)S(1)} custom-call(s32[32]{0:T(128)} %lengths.1, s32[8]{0:T(128)} %dest_inst.1, s32[8]{0:T(128)} %dest_slot.1, s32[256]{0:T(256)} %order.1), custom_call_target="tpu_custom_call" | custom-call | tf_op jit(solution)/shard_map/plan/pallas_call | solution.py:141
  3.6 0.7 broadcast_in_dim.31
  4.3 0.6 slice.66
  5.5 140.5 %conditional.1 = (bf16[2,8,512,512]{3,2,1,0:T(8,128)(2,1)}, bf16[3,8,192]{2,1,0:T(8,128)(2,1)}) conditional(s32[]{:T(128)} %bitcast.36, (s32[416]{0:T(512)S(1)}, bf16[2,8,512,512]{3,2,1,0:T(8,128)(2,1)}, bf16[3,8,384]{2,1,0:T(8,128)(2,1)}, s32[32]{0:T(128)}, s32[256]{0:T(256)}, /*index=5*/bf16[1,384]{1,0:T(2,128)(2,1)S(1)}, ...), branch_computations={%region_0.1_spmd, %region_1.2_spmd, %region_2.3_spmd} | conditional | flops 157321904 | bytes 155730128 | solution.py:649
  5.6 0.6 pack.6
  6.2 1.4 collective-permute-start
  7.7 1.9 %collective-permute-start.1 = (bf16[22,2,32,512]{3,2,1,0:T(8,128)(2,1)}, bf16[22,2,32,512]{3,2,1,0:T(8,128)(2,1)}, u32[]{:S(2)}, u32[]{:S(2)}) collective-permute-start(bf16[22,2,32,512]{3,2,1,0:T(8,128)(2,1)} %get-tuple-element.76), channel_id=1, source_target_pairs={{96,64},{97,65},{98,66},{99,67},{100,68},{101,69},{102,70},{103,71... | collective-permute-start | bytes 4325384 | tf_op jit(solution)/shard_map/cond/branch_0_fun/ppermute | solution.py:671
  9.9 3.5 %project.3 = (f32[16,32,256]{2,1,0:T(8,128)}, s32[16]{0:T(128)S(1)}) custom-call(bf16[3,8,384]{2,1,0:T(8,128)(2,1)S(1)} %copy-done.9, s32[256]{0:T(256)S(1)} %copy-done.12, bf16[1,384]{1,0:T(2,128)(2,1)S(1)} %get-tuple-element.61.gain, bf16[384,3072]{1,0:T(8,128)(2,1)S(1)} %copy-done.3, bf16[2,384,512]{2,1,0:T(8,128)(2,1)S(1)} %copy-done.6), custom_call_target="tpu_custom_call" | custom-call | flops 100663296 | bytes 3145728 | tf_op jit(solution)/shard_map/cond/branch_0_fun/project/pallas_call | solution.py:261
  13.4 8.4 %all-to-all-start = ((f32[16,32,256]{2,1,0:T(8,128)}), f32[16,32,256]{2,1,0:T(8,128)S(1)}, u32[]{:S(2)}, u32[]{:S(2)}) async-start(f32[16,32,256]{2,1,0:T(8,128)} %get-tuple-element.68), calls=%async_computation | async-start | bytes 1048576 | tf_op jit(solution)/shard_map/cond/branch_0_fun/all_to_all | solution.py:625
  21.9 0.6 pack.7
  22.5 9.9 %all-to-all-done.parts = f32[16,32,256]{2,1,0:T(8,128)S(1)} async-done(((f32[16,32,256]{2,1,0:T(8,128)}), f32[16,32,256]{2,1,0:T(8,128)S(1)}, u32[]{:S(2)}, u32[]{:S(2)}) %all-to-all-start) | async-done | bytes 524320 | tf_op jit(solution)/shard_map/cond/branch_0_fun/all_to_all | solution.py:625
  32.4 1.3 collective-permute-start.2
  33.7 1.9 %collective-permute-start.7 = (bf16[26,2,32,512]{3,2,1,0:T(8,128)(2,1)}, bf16[26,2,32,512]{3,2,1,0:T(8,128)(2,1)}, u32[]{:S(2)}, u32[]{:S(2)}) collective-permute-start(bf16[26,2,32,512]{3,2,1,0:T(8,128)(2,1)} %get-tuple-element.84), channel_id=1, source_target_pairs={{96,64},{97,65},{98,66},{99,67},{100,68},{101,69},{102,70},{103,71... | collective-permute-start | bytes 5111816 | tf_op jit(solution)/shard_map/cond/branch_0_fun/ppermute | solution.py:671
  35.5 0.2 rotate.3
  35.7 10.4 %all_to_all.60 = bf16[16,2,24,128]{3,2,1,0:T(8,128)(2,1)S(1)} all-to-all(bf16[16,2,24,128]{3,2,1,0:T(8,128)(2,1)S(1)} %rotate.3), channel_id=1, replica_groups=mesh['inst'=4,'ctx'=16,'head'=2] {'ctx'}, dimensions={0} | all-to-all | bytes 393216 | tf_op jit(solution)/shard_map/cond/branch_0_fun/all_to_all | solution.py:625
  46.4 10.9 %attend_slots.3 = (bf16[2,8,512,512]{3,2,1,0:T(8,128)(2,1)}, bf16[8,2,48,128]{3,2,1,0:T(8,128)(2,1)S(1)}) custom-call(s32[32]{0:T(128)S(1)} %copy-done.15, s32[256]{0:T(256)S(1)} %copy-done.12, bf16[2,8,512,512]{3,2,1,0:T(8,128)(2,1)} %get-tuple-element.57.cache, bf16[8,96,128]{2,1,0:T(8,128)(2,1)S(1)} %bitcast.79, bf16[8,2,8,512]{3,2,1,0:T(8,128)(2,1)S(1)} %pad.15.entries), custom_call_target="tpu_custom_call" | custom-call | bytes 33554432 | tf_op jit(solution)/shard_map/cond/branch_0_fun/attend_slots/pallas_call | solution.py:423
  57.3 4.1 %collective-permute-start.8 = (bf16[22,2,32,512]{3,2,1,0:T(8,128)(2,1)}, bf16[22,2,32,512]{3,2,1,0:T(8,128)(2,1)}, u32[]{:S(2)}, u32[]{:S(2)}) collective-permute-start(bf16[22,2,32,512]{3,2,1,0:T(8,128)(2,1)} %collective-permute-done.refs_0_), channel_id=1, source_target_pairs={{0,32},{1,33},{2,34},{3,35},{4,36},{5,37},{6,38},{7,39},{8,40},{9,... | collective-permute-start | bytes 4325384 | tf_op jit(solution)/shard_map/cond/branch_0_fun/ppermute | solution.py:675
  61.4 1.8 %collective-permute-start.9 = (bf16[22,2,32,512]{3,2,1,0:T(8,128)(2,1)}, bf16[22,2,32,512]{3,2,1,0:T(8,128)(2,1)}, u32[]{:S(2)}, u32[]{:S(2)}) collective-permute-start(bf16[22,2,32,512]{3,2,1,0:T(8,128)(2,1)} %collective-permute-done.1.refs_2_), channel_id=1, source_target_pairs={{64,32},{65,33},{66,34},{67,35},{68,36},{69,37},{70,38},{71,39},{7... | collective-permute-start | bytes 4325384 | tf_op jit(solution)/shard_map/cond/branch_0_fun/ppermute | solution.py:675
  63.1 10.2 %all_to_all.61.parts = bf16[16,48,128]{2,1,0:T(8,128)(2,1)S(1)} all-to-all(bf16[16,48,128]{2,1,0:T(8,128)(2,1)S(1)} %bitcast.82), channel_id=1, replica_groups=mesh['inst'=4,'ctx'=16,'head'=2] {'ctx'}, dimensions={0} | all-to-all | bytes 393216 | tf_op jit(solution)/shard_map/cond/branch_0_fun/all_to_all | solution.py:625
  73.3 0.2 merge.3
  73.6 10.2 %all_to_all.62 = bf16[16,48,128]{2,1,0:T(8,128)(2,1)S(1)} all-to-all(bf16[16,48,128]{2,1,0:T(8,128)(2,1)S(1)} %merge.3), channel_id=1, replica_groups=mesh['inst'=4,'ctx'=16,'head'=2] {'ctx'}, dimensions={0} | all-to-all | bytes 393216 | tf_op jit(solution)/shard_map/cond/branch_0_fun/all_to_all | solution.py:625
  83.8 0.4 fusion.12
  84.4 5.5 %collective-permute-start.3 = (bf16[24,192]{1,0:T(8,128)(2,1)S(1)}, bf16[24,192]{1,0:T(8,128)(2,1)S(1)}, u32[]{:S(2)}, u32[]{:S(2)}) collective-permute-start(bf16[24,192]{1,0:T(8,128)(2,1)S(1)} %select_convert_fusion), channel_id=1, source_target_pairs={{0,1},{1,0},{2,3},{3,2},{4,5},{5,4},{6,7},{7,6},{8,9},{9,8},{10,11... | collective-permute-start | bytes 27656 | tf_op jit(solution)/shard_map/cond/branch_0_fun/ppermute | solution.py:711
  89.9 0.8 collective-permute-done.3
  90.9 1.3 collective-permute-start.4
  92.2 0.7 collective-permute-start.5
  92.9 0.7 collective-permute-start.6
  93.5 2.7 %gather.3 = bf16[16,3,2,32,512]{4,3,2,1,0:T(8,128)(2,1)S(1)} custom-call(s32[416]{0:T(512)S(1)} %get-tuple-element.66.plan, bf16[22,2,32,512]{3,2,1,0:T(8,128)(2,1)} %collective-permute-done.refs_0_, bf16[26,2,32,512]{3,2,1,0:T(8,128)(2,1)S(1)} %collective-permute-done.2.refs_1_, bf16[22,2,32,512]{3,2,1,0:T(8,128)(2,1)} %collective-permute-done.1.refs_2_, ...), custom_call_target="tpu_custom_call" | custom-call | bytes 8388608 | tf_op jit(solution)/shard_map/cond/branch_0_fun/gather/pallas_call | solution.py:496
  96.2 5.7 %collective-permute-done.4.by0 = bf16[24,1280]{1,0:T(8,128)(2,1)S(1)} collective-permute-done((bf16[24,1280]{1,0:T(8,128)(2,1)S(1)}, bf16[24,1280]{1,0:T(8,128)(2,1)S(1)}, u32[]{:S(2)}, u32[]{:S(2)}) %collective-permute-start.4) | collective-permute-done | bytes 61472 | tf_op jit(solution)/shard_map/cond/branch_0_fun/ppermute | solution.py:714
  101.9 41.3 %all_to_all.63.received = bf16[16,3,2,32,512]{4,3,2,1,0:T(8,128)(2,1)S(1)} all-to-all(bf16[16,3,2,32,512]{4,3,2,1,0:T(8,128)(2,1)S(1)} %gather.3), channel_id=1, replica_groups=mesh['inst'=4,'ctx'=16,'head'=2] {'ctx'}, dimensions={0} | all-to-all | bytes 6291456 | tf_op jit(solution)/shard_map/cond/branch_0_fun/all_to_all | solution.py:625
  143.2 2.3 %place.3 = (bf16[2,8,512,512]{3,2,1,0:T(8,128)(2,1)}, f32[24,256]{1,0:T(8,128)S(1)}) custom-call(s32[416]{0:T(512)S(1)} %get-tuple-element.66.plan, s32[16]{0:T(128)S(1)} %get-tuple-element.67.within, bf16[16,3,2,32,512]{4,3,2,1,0:T(8,128)(2,1)S(1)} %all_to_all.63.received, ...), custom_call_target="tpu_custom_call", output_to_operand_aliasing={{0}: (3, {})} | custom-call | tf_op jit(solution)/shard_map/cond/branch_0_fun/place/pallas_call | solution.py:604
  145.4 0.6 fusion.2
  (42 shorter events, 0.9 us)
Async XLA Ops:
  5.5 4.0 %copy-start.15 = (s32[32]{0:T(128)S(1)}, s32[32]{0:T(128)}, u32[]{:S(2)}) copy-start(s32[32]{0:T(128)} %get-tuple-element.65.lengths) | copy-start | bytes 388 | tf_op jit(solution)/shard_map/cond
  5.6 4.3 %copy-start.3 = (bf16[384,3072]{1,0:T(8,128)(2,1)S(1)}, bf16[384,3072]{1,0:T(8,128)(2,1)}, u32[]{:S(2)}) copy-start(bf16[384,3072]{1,0:T(8,128)(2,1)} %get-tuple-element.62.w_query) | copy-start | bytes 7077892 | tf_op jit(solution)/shard_map/cond
  5.6 4.3 %copy-start.6 = (bf16[2,384,512]{2,1,0:T(8,128)(2,1)S(1)}, bf16[2,384,512]{2,1,0:T(8,128)(2,1)}, u32[]{:S(2)}) copy-start(bf16[2,384,512]{2,1,0:T(8,128)(2,1)} %get-tuple-element.63.w_kv) | copy-start | bytes 2359300 | tf_op jit(solution)/shard_map/cond
  5.6 4.3 %copy-start.9 = (bf16[3,8,384]{2,1,0:T(8,128)(2,1)S(1)}, bf16[3,8,384]{2,1,0:T(8,128)(2,1)}, u32[]{:S(2)}) copy-start(bf16[3,8,384]{2,1,0:T(8,128)(2,1)} %get-tuple-element.59.hidden) | copy-start | bytes 55300 | tf_op jit(solution)/shard_map/cond
  5.6 4.3 %copy-start.12 = (s32[256]{0:T(256)S(1)}, s32[256]{0:T(256)}, u32[]{:S(2)}) copy-start(s32[256]{0:T(256)} %get-tuple-element.60.order) | copy-start | bytes 3076 | tf_op jit(solution)/shard_map/cond
  6.2 51.0 %collective-permute-start = (bf16[22,2,32,512]{3,2,1,0:T(8,128)(2,1)}, bf16[22,2,32,512]{3,2,1,0:T(8,128)(2,1)}, u32[]{:S(2)}, u32[]{:S(2)}) collective-permute-start(bf16[22,2,32,512]{3,2,1,0:T(8,128)(2,1)} %get-tuple-element.58), channel_id=1, source_target_pairs={{96,0},{97,1},{98,2},{99,3},{100,4},{101,5},{102,6},{103,7},{104,8... | collective-permute-start | bytes 4325384 | tf_op jit(solution)/shard_map/cond/branch_0_fun/ppermute | solution.py:667
  7.7 49.6 %collective-permute-start.1 = (bf16[22,2,32,512]{3,2,1,0:T(8,128)(2,1)}, bf16[22,2,32,512]{3,2,1,0:T(8,128)(2,1)}, u32[]{:S(2)}, u32[]{:S(2)}) collective-permute-start(bf16[22,2,32,512]{3,2,1,0:T(8,128)(2,1)} %get-tuple-element.76), channel_id=1, source_target_pairs={{96,64},{97,65},{98,66},{99,67},{100,68},{101,69},{102,70},{103,71... | collective-permute-start | bytes 4325384 | tf_op jit(solution)/shard_map/cond/branch_0_fun/ppermute | solution.py:671
  13.4 18.9 %all-to-all-start = ((f32[16,32,256]{2,1,0:T(8,128)}), f32[16,32,256]{2,1,0:T(8,128)S(1)}, u32[]{:S(2)}, u32[]{:S(2)}) async-start(f32[16,32,256]{2,1,0:T(8,128)} %get-tuple-element.68), calls=%async_computation | async-start | bytes 1048576 | tf_op jit(solution)/shard_map/cond/branch_0_fun/all_to_all | solution.py:625
  32.4 51.9 %collective-permute-start.2 = (bf16[26,2,32,512]{3,2,1,0:T(8,128)(2,1)}, bf16[26,2,32,512]{3,2,1,0:T(8,128)(2,1)S(1)}, u32[]{:S(2)}, u32[]{:S(2)}) collective-permute-start(bf16[26,2,32,512]{3,2,1,0:T(8,128)(2,1)} %get-tuple-element.79), channel_id=1, source_target_pairs={{96,0},{97,1},{98,2},{99,3},{100,4},{101,5},{102,6},{103,7},{104,8... | collective-permute-start | bytes 5111816 | tf_op jit(solution)/shard_map/cond/branch_0_fun/ppermute | solution.py:667
  33.7 59.2 %collective-permute-start.7 = (bf16[26,2,32,512]{3,2,1,0:T(8,128)(2,1)}, bf16[26,2,32,512]{3,2,1,0:T(8,128)(2,1)}, u32[]{:S(2)}, u32[]{:S(2)}) collective-permute-start(bf16[26,2,32,512]{3,2,1,0:T(8,128)(2,1)} %get-tuple-element.84), channel_id=1, source_target_pairs={{96,64},{97,65},{98,66},{99,67},{100,68},{101,69},{102,70},{103,71... | collective-permute-start | bytes 5111816 | tf_op jit(solution)/shard_map/cond/branch_0_fun/ppermute | solution.py:671
  46.4 37.4 %copy-start = (bf16[3072,384]{1,0:T(8,128)(2,1)S(1)}, bf16[3072,384]{1,0:T(8,128)(2,1)}, u32[]{:S(2)}) copy-start(bf16[3072,384]{1,0:T(8,128)(2,1)} %get-tuple-element.78) | copy-start | bytes 7077892 | tf_op jit(solution)/shard_map/cond
  57.3 36.3 %collective-permute-start.8 = (bf16[22,2,32,512]{3,2,1,0:T(8,128)(2,1)}, bf16[22,2,32,512]{3,2,1,0:T(8,128)(2,1)}, u32[]{:S(2)}, u32[]{:S(2)}) collective-permute-start(bf16[22,2,32,512]{3,2,1,0:T(8,128)(2,1)} %collective-permute-done.refs_0_), channel_id=1, source_target_pairs={{0,32},{1,33},{2,34},{3,35},{4,36},{5,37},{6,38},{7,39},{8,40},{9,... | collective-permute-start | bytes 4325384 | tf_op jit(solution)/shard_map/cond/branch_0_fun/ppermute | solution.py:675
  61.4 32.2 %collective-permute-start.9 = (bf16[22,2,32,512]{3,2,1,0:T(8,128)(2,1)}, bf16[22,2,32,512]{3,2,1,0:T(8,128)(2,1)}, u32[]{:S(2)}, u32[]{:S(2)}) collective-permute-start(bf16[22,2,32,512]{3,2,1,0:T(8,128)(2,1)} %collective-permute-done.1.refs_2_), channel_id=1, source_target_pairs={{64,32},{65,33},{66,34},{67,35},{68,36},{69,37},{70,38},{71,39},{7... | collective-permute-start | bytes 4325384 | tf_op jit(solution)/shard_map/cond/branch_0_fun/ppermute | solution.py:675
  84.4 6.3 %collective-permute-start.3 = (bf16[24,192]{1,0:T(8,128)(2,1)S(1)}, bf16[24,192]{1,0:T(8,128)(2,1)S(1)}, u32[]{:S(2)}, u32[]{:S(2)}) collective-permute-start(bf16[24,192]{1,0:T(8,128)(2,1)S(1)} %select_convert_fusion), channel_id=1, source_target_pairs={{0,1},{1,0},{2,3},{3,2},{4,5},{5,4},{6,7},{7,6},{8,9},{9,8},{10,11... | collective-permute-start | bytes 27656 | tf_op jit(solution)/shard_map/cond/branch_0_fun/ppermute | solution.py:711
  90.9 11.0 %collective-permute-start.4 = (bf16[24,1280]{1,0:T(8,128)(2,1)S(1)}, bf16[24,1280]{1,0:T(8,128)(2,1)S(1)}, u32[]{:S(2)}, u32[]{:S(2)}) collective-permute-start(bf16[24,1280]{1,0:T(8,128)(2,1)S(1)} %concatenate.20.own), channel_id=1, source_target_pairs={{96,0},{97,1},{98,2},{99,3},{100,4},{101,5},{102,6},{103,7},{104,8... | collective-permute-start | bytes 184328 | tf_op jit(solution)/shard_map/cond/branch_0_fun/ppermute | solution.py:714
  92.2 9.7 %collective-permute-start.5 = (bf16[24,1280]{1,0:T(8,128)(2,1)S(1)}, bf16[24,1280]{1,0:T(8,128)(2,1)S(1)}, u32[]{:S(2)}, u32[]{:S(2)}) collective-permute-start(bf16[24,1280]{1,0:T(8,128)(2,1)S(1)} %concatenate.20.own), channel_id=1, source_target_pairs={{96,32},{97,33},{98,34},{99,35},{100,36},{101,37},{102,38},{103,39... | collective-permute-start | bytes 184328 | tf_op jit(solution)/shard_map/cond/branch_0_fun/ppermute | solution.py:714
  92.9 9.0 %collective-permute-start.6 = (bf16[24,1280]{1,0:T(8,128)(2,1)S(1)}, bf16[24,1280]{1,0:T(8,128)(2,1)S(1)}, u32[]{:S(2)}, u32[]{:S(2)}) collective-permute-start(bf16[24,1280]{1,0:T(8,128)(2,1)S(1)} %concatenate.20.own), channel_id=1, source_target_pairs={{96,64},{97,65},{98,66},{99,67},{100,68},{101,69},{102,70},{103,71... | collective-permute-start | bytes 184328 | tf_op jit(solution)/shard_map/cond/branch_0_fun/ppermute | solution.py:714

commit v6 on v5

--- a/solution.py
+++ b/solution.py
@@ -382,32 +382,49 @@
                 lax.shift_right_logical(lane, 5) == b, start + lane - b * BLOCK, position
             )
 
-        new_cache[...] = cache[...]
-
-        def build(b, carry):
-            start = jnp.where(retires, order[ctx * CTX + b], ctx * CTX + b) * BLOCK
-            rows = pl.ds(pl.multiple_of(b * BLOCK, BLOCK), BLOCK)
-
-            @pl.when(jnp.logical_and(start >= length + STEPS, jnp.logical_not(retires)))
-            def _():
-                new_cache[:, 0, rows, :] = jnp.zeros((2, BLOCK, FEATURES), BF16)
-
-            @pl.when(jnp.logical_and(start + BLOCK > length, start < length + STEPS))
-            def _():
-                at = start + lax.broadcasted_iota(I32, (BLOCK, 1), 0)
-                for kv in range(2):
-                    block = jnp.where(at < length, cache[kv, 0, rows, :], jnp.zeros((), BF16))
-                    for t in range(STEPS):
-                        block = jnp.where(at == length + t, entries[0, kv, t : t + 1, :], block)
-                    new_cache[kv, 0, rows, :] = block
-
-            return carry
-
-        whole = jnp.logical_and(jnp.logical_not(retires), (ctx + 1) * RANGE <= length)
-        lax.fori_loop(0, jnp.where(whole, 0, CTX), build, 0)
-        halves = attend(new_cache[0, 0], new_cache[1, 0], query[0], position, length)
-        for h in range(2):
-            sums[0, h] = halves[h]
+        def meets(b, found):
+            start = order[ctx * CTX + b] * BLOCK
+            here = jnp.logical_and(start + BLOCK > length, start < length + STEPS)
+            return jnp.where(here, 1, found)
+
+        found = lax.fori_loop(0, jnp.where(retires, CTX, 0), meets, jnp.int32(0))
+        direct = jnp.logical_and(retires, found == 0)
+
+        def finish(keys, values):
+            halves = attend(keys, values, query[0], position, length)
+            for h in range(2):
+                sums[0, h] = halves[h]
+
+        @pl.when(direct)
+        def _():
+            finish(cache[0, 0], cache[1, 0])
+
+        @pl.when(jnp.logical_not(direct))
+        def _():
+            new_cache[...] = cache[...]
+
+            def build(b, carry):
+                start = jnp.where(retires, order[ctx * CTX + b], ctx * CTX + b) * BLOCK
+                rows = pl.ds(pl.multiple_of(b * BLOCK, BLOCK), BLOCK)
+
+                @pl.when(jnp.logical_and(start >= length + STEPS, jnp.logical_not(retires)))
+                def _():
+                    new_cache[:, 0, rows, :] = jnp.zeros((2, BLOCK, FEATURES), BF16)
+
+                @pl.when(jnp.logical_and(start + BLOCK > length, start < length + STEPS))
+                def _():
+                    at = start + lax.broadcasted_iota(I32, (BLOCK, 1), 0)
+                    for kv in range(2):
+                        block = jnp.where(at < length, cache[kv, 0, rows, :], jnp.zeros((), BF16))
+                        for t in range(STEPS):
+                            block = jnp.where(at == length + t, entries[0, kv, t : t + 1, :], block)
+                        new_cache[kv, 0, rows, :] = block
+
+                return carry
+
+            whole = jnp.logical_and(jnp.logical_not(retires), (ctx + 1) * RANGE <= length)
+            lax.fori_loop(0, jnp.where(whole, 0, CTX), build, 0)
+            finish(new_cache[0, 0], new_cache[1, 0])
 
     @pl.when(jnp.logical_not(some))
     def _():

time: 148 us -> 147 us (level)
  transfers between devices with their start and end apart: 11 -> 11, of which waited for: 3 -> 3; matrix products, arithmetic and copies ran while one was open for 1% -> 1% of each run, Pallas kernels for 12% -> 13%
where the time goes in v6:
time: 147 us; the launch traced here: 145 us
  blocking collectives  71.7 us (49%)
  starting transfers between devices  28.2 us (19%)
  Pallas kernels  24.6 us (17%)
  waiting for transfers between devices  15.7 us (11%)
  local copies, waits for them, and re-layouts  2.4 us (2%)
    all_to_all x4, blocking collectives, swap(): return lax.all_to_all(x, 'ctx', split_axis=0, concat_axis=0, tiled=True)  71.7 us
    pallas_call x1, Pallas kernels, attend_slots(): pl.pallas_call(attend_kernel, out_shape=[jax.ShapeDtypeStruct(cache.shape...  11.8 us
    all_to_all x1, waiting for transfers between devices, swap(): return lax.all_to_all(x, 'ctx', split_axis=0, concat_axis=0, tiled=True)  9.88 us
    all_to_all x1, starting transfers between devices, swap(): return lax.all_to_all(x, 'ctx', split_axis=0, concat_axis=0, tiled=True)  8.43 us
    ppermute x1, starting transfers between devices, decode(): got = lax.ppermute(send_half, 'head', [(0, 1), (1, 0)])  5.55 us
    ppermute x3, waiting for transfers between devices, decode(): by = [lax.ppermute(own, 'inst', [(INST - 1, i)]) for i in range(INST - 1)]  4.96 us
    ppermute x2, starting transfers between devices, down(): return lax.ppermute(x, 'inst', [(INST - 1, 2)])  3.72 us
    pallas_call x1, Pallas kernels, project(): pl.pallas_call(project_kernel, out_shape=[jax.ShapeDtypeStruct((CTX, 32,...  3.49 us
  transfers between devices with their start and end apart: 11, of which 3 were waited for; matrix products, arithmetic and copies ran while one was open for 1% of the time, Pallas kernels for 13%

profile of v6, /device:TPU:1, one launch (start us, length us, event | category | flops | bytes accessed | tf_op | source)
XLA Modules:
  0.0 145.0 jit_solution(2598481357371037758)
XLA Ops:
  0.6 2.7 %plan.1 = s32[416]{0:T(512)S(1)} custom-call(s32[32]{0:T(128)} %lengths.1, s32[8]{0:T(128)} %dest_inst.1, s32[8]{0:T(128)} %dest_slot.1, s32[256]{0:T(256)} %order.1), custom_call_target="tpu_custom_call" | custom-call | tf_op jit(solution)/shard_map/plan/pallas_call | solution.py:141
  3.3 0.7 broadcast_in_dim.31
  4.0 0.6 slice.66
  5.2 139.7 %conditional.1 = (bf16[2,8,512,512]{3,2,1,0:T(8,128)(2,1)}, bf16[3,8,192]{2,1,0:T(8,128)(2,1)}) conditional(s32[]{:T(128)} %bitcast.36, (s32[416]{0:T(512)S(1)}, bf16[2,8,512,512]{3,2,1,0:T(8,128)(2,1)}, bf16[3,8,384]{2,1,0:T(8,128)(2,1)}, s32[32]{0:T(128)}, s32[256]{0:T(256)}, /*index=5*/bf16[1,384]{1,0:T(2,128)(2,1)S(1)}, ...), branch_computations={%region_0.1_spmd, %region_1.2_spmd, %region_2.3_spmd} | conditional | flops 157321904 | bytes 155730128 | solution.py:666
  5.3 0.6 pack.6
  5.9 1.4 collective-permute-start
  7.4 1.9 %collective-permute-start.1 = (bf16[22,2,32,512]{3,2,1,0:T(8,128)(2,1)}, bf16[22,2,32,512]{3,2,1,0:T(8,128)(2,1)}, u32[]{:S(2)}, u32[]{:S(2)}) collective-permute-start(bf16[22,2,32,512]{3,2,1,0:T(8,128)(2,1)} %get-tuple-element.76), channel_id=1, source_target_pairs={{96,64},{97,65},{98,66},{99,67},{100,68},{101,69},{102,70},{103,71... | collective-permute-start | bytes 4325384 | tf_op jit(solution)/shard_map/cond/branch_0_fun/ppermute | solution.py:688
  9.6 3.5 %project.3 = (f32[16,32,256]{2,1,0:T(8,128)}, s32[16]{0:T(128)S(1)}) custom-call(bf16[3,8,384]{2,1,0:T(8,128)(2,1)S(1)} %copy-done.9, s32[256]{0:T(256)S(1)} %copy-done.12, bf16[1,384]{1,0:T(2,128)(2,1)S(1)} %get-tuple-element.61.gain, bf16[384,3072]{1,0:T(8,128)(2,1)S(1)} %copy-done.3, bf16[2,384,512]{2,1,0:T(8,128)(2,1)S(1)} %copy-done.6), custom_call_target="tpu_custom_call" | custom-call | flops 100663296 | bytes 3145728 | tf_op jit(solution)/shard_map/cond/branch_0_fun/project/pallas_call | solution.py:261
  13.2 8.4 %all-to-all-start = ((f32[16,32,256]{2,1,0:T(8,128)}), f32[16,32,256]{2,1,0:T(8,128)S(1)}, u32[]{:S(2)}, u32[]{:S(2)}) async-start(f32[16,32,256]{2,1,0:T(8,128)} %get-tuple-element.68), calls=%async_computation | async-start | bytes 1048576 | tf_op jit(solution)/shard_map/cond/branch_0_fun/all_to_all | solution.py:642
  21.6 0.6 pack.7
  22.2 9.9 %all-to-all-done.parts = f32[16,32,256]{2,1,0:T(8,128)S(1)} async-done(((f32[16,32,256]{2,1,0:T(8,128)}), f32[16,32,256]{2,1,0:T(8,128)S(1)}, u32[]{:S(2)}, u32[]{:S(2)}) %all-to-all-start) | async-done | bytes 524320 | tf_op jit(solution)/shard_map/cond/branch_0_fun/all_to_all | solution.py:642
  32.1 1.3 collective-permute-start.2
  33.4 1.9 %collective-permute-start.7 = (bf16[26,2,32,512]{3,2,1,0:T(8,128)(2,1)}, bf16[26,2,32,512]{3,2,1,0:T(8,128)(2,1)}, u32[]{:S(2)}, u32[]{:S(2)}) collective-permute-start(bf16[26,2,32,512]{3,2,1,0:T(8,128)(2,1)} %get-tuple-element.84), channel_id=1, source_target_pairs={{96,64},{97,65},{98,66},{99,67},{100,68},{101,69},{102,70},{103,71... | collective-permute-start | bytes 5111816 | tf_op jit(solution)/shard_map/cond/branch_0_fun/ppermute | solution.py:688
  35.3 0.2 rotate.3
  35.5 10.4 %all_to_all.60 = bf16[16,2,24,128]{3,2,1,0:T(8,128)(2,1)S(1)} all-to-all(bf16[16,2,24,128]{3,2,1,0:T(8,128)(2,1)S(1)} %rotate.3), channel_id=1, replica_groups=mesh['inst'=4,'ctx'=16,'head'=2] {'ctx'}, dimensions={0} | all-to-all | bytes 393216 | tf_op jit(solution)/shard_map/cond/branch_0_fun/all_to_all | solution.py:642
  46.1 11.8 %attend_slots.3 = (bf16[2,8,512,512]{3,2,1,0:T(8,128)(2,1)}, bf16[8,2,48,128]{3,2,1,0:T(8,128)(2,1)S(1)}) custom-call(s32[32]{0:T(128)S(1)} %copy-done.15, s32[256]{0:T(256)S(1)} %copy-done.12, bf16[2,8,512,512]{3,2,1,0:T(8,128)(2,1)} %get-tuple-element.57.cache, bf16[8,96,128]{2,1,0:T(8,128)(2,1)S(1)} %bitcast.79, bf16[8,2,8,512]{3,2,1,0:T(8,128)(2,1)S(1)} %pad.15.entries), custom_call_target="tpu_custom_call" | custom-call | bytes 33554432 | tf_op jit(solution)/shard_map/cond/branch_0_fun/attend_slots/pallas_call | solution.py:440
  57.9 3.4 %collective-permute-start.8 = (bf16[22,2,32,512]{3,2,1,0:T(8,128)(2,1)}, bf16[22,2,32,512]{3,2,1,0:T(8,128)(2,1)}, u32[]{:S(2)}, u32[]{:S(2)}) collective-permute-start(bf16[22,2,32,512]{3,2,1,0:T(8,128)(2,1)} %collective-permute-done.refs_0_), channel_id=1, source_target_pairs={{0,32},{1,33},{2,34},{3,35},{4,36},{5,37},{6,38},{7,39},{8,40},{9,... | collective-permute-start | bytes 4325384 | tf_op jit(solution)/shard_map/cond/branch_0_fun/ppermute | solution.py:692
  61.3 1.8 %collective-permute-start.9 = (bf16[22,2,32,512]{3,2,1,0:T(8,128)(2,1)}, bf16[22,2,32,512]{3,2,1,0:T(8,128)(2,1)}, u32[]{:S(2)}, u32[]{:S(2)}) collective-permute-start(bf16[22,2,32,512]{3,2,1,0:T(8,128)(2,1)} %collective-permute-done.1.refs_2_), channel_id=1, source_target_pairs={{64,32},{65,33},{66,34},{67,35},{68,36},{69,37},{70,38},{71,39},{7... | collective-permute-start | bytes 4325384 | tf_op jit(solution)/shard_map/cond/branch_0_fun/ppermute | solution.py:692
  63.1 9.8 %all_to_all.61.parts = bf16[16,48,128]{2,1,0:T(8,128)(2,1)S(1)} all-to-all(bf16[16,48,128]{2,1,0:T(8,128)(2,1)S(1)} %bitcast.82), channel_id=1, replica_groups=mesh['inst'=4,'ctx'=16,'head'=2] {'ctx'}, dimensions={0} | all-to-all | bytes 393216 | tf_op jit(solution)/shard_map/cond/branch_0_fun/all_to_all | solution.py:642
  72.8 0.2 merge.3
  73.1 10.2 %all_to_all.62 = bf16[16,48,128]{2,1,0:T(8,128)(2,1)S(1)} all-to-all(bf16[16,48,128]{2,1,0:T(8,128)(2,1)S(1)} %merge.3), channel_id=1, replica_groups=mesh['inst'=4,'ctx'=16,'head'=2] {'ctx'}, dimensions={0} | all-to-all | bytes 393216 | tf_op jit(solution)/shard_map/cond/branch_0_fun/all_to_all | solution.py:642
  83.4 0.4 fusion.12
  83.9 5.6 %collective-permute-start.3 = (bf16[24,192]{1,0:T(8,128)(2,1)S(1)}, bf16[24,192]{1,0:T(8,128)(2,1)S(1)}, u32[]{:S(2)}, u32[]{:S(2)}) collective-permute-start(bf16[24,192]{1,0:T(8,128)(2,1)S(1)} %select_convert_fusion), channel_id=1, source_target_pairs={{0,1},{1,0},{2,3},{3,2},{4,5},{5,4},{6,7},{7,6},{8,9},{9,8},{10,11... | collective-permute-start | bytes 27656 | tf_op jit(solution)/shard_map/cond/branch_0_fun/ppermute | solution.py:728
  89.4 0.8 collective-permute-done.3
  90.4 1.3 collective-permute-start.4
  91.7 0.7 collective-permute-start.5
  92.4 0.7 collective-permute-start.6
  93.1 2.8 %gather.3 = bf16[16,3,2,32,512]{4,3,2,1,0:T(8,128)(2,1)S(1)} custom-call(s32[416]{0:T(512)S(1)} %get-tuple-element.66.plan, bf16[22,2,32,512]{3,2,1,0:T(8,128)(2,1)} %collective-permute-done.refs_0_, bf16[26,2,32,512]{3,2,1,0:T(8,128)(2,1)S(1)} %collective-permute-done.2.refs_1_, bf16[22,2,32,512]{3,2,1,0:T(8,128)(2,1)} %collective-permute-done.1.refs_2_, ...), custom_call_target="tpu_custom_call" | custom-call | bytes 8388608 | tf_op jit(solution)/shard_map/cond/branch_0_fun/gather/pallas_call | solution.py:513
  95.9 5.0 %collective-permute-done.4.by0 = bf16[24,1280]{1,0:T(8,128)(2,1)S(1)} collective-permute-done((bf16[24,1280]{1,0:T(8,128)(2,1)S(1)}, bf16[24,1280]{1,0:T(8,128)(2,1)S(1)}, u32[]{:S(2)}, u32[]{:S(2)}) %collective-permute-start.4) | collective-permute-done | bytes 61472 | tf_op jit(solution)/shard_map/cond/branch_0_fun/ppermute | solution.py:731
  100.8 41.3 %all_to_all.63.received = bf16[16,3,2,32,512]{4,3,2,1,0:T(8,128)(2,1)S(1)} all-to-all(bf16[16,3,2,32,512]{4,3,2,1,0:T(8,128)(2,1)S(1)} %gather.3), channel_id=1, replica_groups=mesh['inst'=4,'ctx'=16,'head'=2] {'ctx'}, dimensions={0} | all-to-all | bytes 6291456 | tf_op jit(solution)/shard_map/cond/branch_0_fun/all_to_all | solution.py:642
  142.1 2.3 %place.3 = (bf16[2,8,512,512]{3,2,1,0:T(8,128)(2,1)}, f32[24,256]{1,0:T(8,128)S(1)}) custom-call(s32[416]{0:T(512)S(1)} %get-tuple-element.66.plan, s32[16]{0:T(128)S(1)} %get-tuple-element.67.within, bf16[16,3,2,32,512]{4,3,2,1,0:T(8,128)(2,1)S(1)} %all_to_all.63.received, ...), custom_call_target="tpu_custom_call", output_to_operand_aliasing={{0}: (3, {})} | custom-call | tf_op jit(solution)/shard_map/cond/branch_0_fun/place/pallas_call | solution.py:621
  144.4 0.6 fusion.2
  (42 shorter events, 0.9 us)
Async XLA Ops:
  5.3 4.0 %copy-start.15 = (s32[32]{0:T(128)S(1)}, s32[32]{0:T(128)}, u32[]{:S(2)}) copy-start(s32[32]{0:T(128)} %get-tuple-element.65.lengths) | copy-start | bytes 388 | tf_op jit(solution)/shard_map/cond
  5.3 4.3 %copy-start.3 = (bf16[384,3072]{1,0:T(8,128)(2,1)S(1)}, bf16[384,3072]{1,0:T(8,128)(2,1)}, u32[]{:S(2)}) copy-start(bf16[384,3072]{1,0:T(8,128)(2,1)} %get-tuple-element.62.w_query) | copy-start | bytes 7077892 | tf_op jit(solution)/shard_map/cond
  5.3 4.3 %copy-start.6 = (bf16[2,384,512]{2,1,0:T(8,128)(2,1)S(1)}, bf16[2,384,512]{2,1,0:T(8,128)(2,1)}, u32[]{:S(2)}) copy-start(bf16[2,384,512]{2,1,0:T(8,128)(2,1)} %get-tuple-element.63.w_kv) | copy-start | bytes 2359300 | tf_op jit(solution)/shard_map/cond
  5.3 4.3 %copy-start.9 = (bf16[3,8,384]{2,1,0:T(8,128)(2,1)S(1)}, bf16[3,8,384]{2,1,0:T(8,128)(2,1)}, u32[]{:S(2)}) copy-start(bf16[3,8,384]{2,1,0:T(8,128)(2,1)} %get-tuple-element.59.hidden) | copy-start | bytes 55300 | tf_op jit(solution)/shard_map/cond
  5.3 4.3 %copy-start.12 = (s32[256]{0:T(256)S(1)}, s32[256]{0:T(256)}, u32[]{:S(2)}) copy-start(s32[256]{0:T(256)} %get-tuple-element.60.order) | copy-start | bytes 3076 | tf_op jit(solution)/shard_map/cond
  5.9 52.0 %collective-permute-start = (bf16[22,2,32,512]{3,2,1,0:T(8,128)(2,1)}, bf16[22,2,32,512]{3,2,1,0:T(8,128)(2,1)}, u32[]{:S(2)}, u32[]{:S(2)}) collective-permute-start(bf16[22,2,32,512]{3,2,1,0:T(8,128)(2,1)} %get-tuple-element.58), channel_id=1, source_target_pairs={{96,0},{97,1},{98,2},{99,3},{100,4},{101,5},{102,6},{103,7},{104,8... | collective-permute-start | bytes 4325384 | tf_op jit(solution)/shard_map/cond/branch_0_fun/ppermute | solution.py:684
  7.4 50.5 %collective-permute-start.1 = (bf16[22,2,32,512]{3,2,1,0:T(8,128)(2,1)}, bf16[22,2,32,512]{3,2,1,0:T(8,128)(2,1)}, u32[]{:S(2)}, u32[]{:S(2)}) collective-permute-start(bf16[22,2,32,512]{3,2,1,0:T(8,128)(2,1)} %get-tuple-element.76), channel_id=1, source_target_pairs={{96,64},{97,65},{98,66},{99,67},{100,68},{101,69},{102,70},{103,71... | collective-permute-start | bytes 4325384 | tf_op jit(solution)/shard_map/cond/branch_0_fun/ppermute | solution.py:688
  13.2 18.9 %all-to-all-start = ((f32[16,32,256]{2,1,0:T(8,128)}), f32[16,32,256]{2,1,0:T(8,128)S(1)}, u32[]{:S(2)}, u32[]{:S(2)}) async-start(f32[16,32,256]{2,1,0:T(8,128)} %get-tuple-element.68), calls=%async_computation | async-start | bytes 1048576 | tf_op jit(solution)/shard_map/cond/branch_0_fun/all_to_all | solution.py:642
  32.1 51.7 %collective-permute-start.2 = (bf16[26,2,32,512]{3,2,1,0:T(8,128)(2,1)}, bf16[26,2,32,512]{3,2,1,0:T(8,128)(2,1)S(1)}, u32[]{:S(2)}, u32[]{:S(2)}) collective-permute-start(bf16[26,2,32,512]{3,2,1,0:T(8,128)(2,1)} %get-tuple-element.79), channel_id=1, source_target_pairs={{96,0},{97,1},{98,2},{99,3},{100,4},{101,5},{102,6},{103,7},{104,8... | collective-permute-start | bytes 5111816 | tf_op jit(solution)/shard_map/cond/branch_0_fun/ppermute | solution.py:684
  33.4 59.0 %collective-permute-start.7 = (bf16[26,2,32,512]{3,2,1,0:T(8,128)(2,1)}, bf16[26,2,32,512]{3,2,1,0:T(8,128)(2,1)}, u32[]{:S(2)}, u32[]{:S(2)}) collective-permute-start(bf16[26,2,32,512]{3,2,1,0:T(8,128)(2,1)} %get-tuple-element.84), channel_id=1, source_target_pairs={{96,64},{97,65},{98,66},{99,67},{100,68},{101,69},{102,70},{103,71... | collective-permute-start | bytes 5111816 | tf_op jit(solution)/shard_map/cond/branch_0_fun/ppermute | solution.py:688
  46.1 37.2 %copy-start = (bf16[3072,384]{1,0:T(8,128)(2,1)S(1)}, bf16[3072,384]{1,0:T(8,128)(2,1)}, u32[]{:S(2)}) copy-start(bf16[3072,384]{1,0:T(8,128)(2,1)} %get-tuple-element.78) | copy-start | bytes 7077892 | tf_op jit(solution)/shard_map/cond
  57.9 35.2 %collective-permute-start.8 = (bf16[22,2,32,512]{3,2,1,0:T(8,128)(2,1)}, bf16[22,2,32,512]{3,2,1,0:T(8,128)(2,1)}, u32[]{:S(2)}, u32[]{:S(2)}) collective-permute-start(bf16[22,2,32,512]{3,2,1,0:T(8,128)(2,1)} %collective-permute-done.refs_0_), channel_id=1, source_target_pairs={{0,32},{1,33},{2,34},{3,35},{4,36},{5,37},{6,38},{7,39},{8,40},{9,... | collective-permute-start | bytes 4325384 | tf_op jit(solution)/shard_map/cond/branch_0_fun/ppermute | solution.py:692
  61.3 31.8 %collective-permute-start.9 = (bf16[22,2,32,512]{3,2,1,0:T(8,128)(2,1)}, bf16[22,2,32,512]{3,2,1,0:T(8,128)(2,1)}, u32[]{:S(2)}, u32[]{:S(2)}) collective-permute-start(bf16[22,2,32,512]{3,2,1,0:T(8,128)(2,1)} %collective-permute-done.1.refs_2_), channel_id=1, source_target_pairs={{64,32},{65,33},{66,34},{67,35},{68,36},{69,37},{70,38},{71,39},{7... | collective-permute-start | bytes 4325384 | tf_op jit(solution)/shard_map/cond/branch_0_fun/ppermute | solution.py:692
  83.9 6.4 %collective-permute-start.3 = (bf16[24,192]{1,0:T(8,128)(2,1)S(1)}, bf16[24,192]{1,0:T(8,128)(2,1)S(1)}, u32[]{:S(2)}, u32[]{:S(2)}) collective-permute-start(bf16[24,192]{1,0:T(8,128)(2,1)S(1)} %select_convert_fusion), channel_id=1, source_target_pairs={{0,1},{1,0},{2,3},{3,2},{4,5},{5,4},{6,7},{7,6},{8,9},{9,8},{10,11... | collective-permute-start | bytes 27656 | tf_op jit(solution)/shard_map/cond/branch_0_fun/ppermute | solution.py:728
  90.4 10.4 %collective-permute-start.4 = (bf16[24,1280]{1,0:T(8,128)(2,1)S(1)}, bf16[24,1280]{1,0:T(8,128)(2,1)S(1)}, u32[]{:S(2)}, u32[]{:S(2)}) collective-permute-start(bf16[24,1280]{1,0:T(8,128)(2,1)S(1)} %concatenate.20.own), channel_id=1, source_target_pairs={{96,0},{97,1},{98,2},{99,3},{100,4},{101,5},{102,6},{103,7},{104,8... | collective-permute-start | bytes 184328 | tf_op jit(solution)/shard_map/cond/branch_0_fun/ppermute | solution.py:731
  91.7 9.1 %collective-permute-start.5 = (bf16[24,1280]{1,0:T(8,128)(2,1)S(1)}, bf16[24,1280]{1,0:T(8,128)(2,1)S(1)}, u32[]{:S(2)}, u32[]{:S(2)}) collective-permute-start(bf16[24,1280]{1,0:T(8,128)(2,1)S(1)} %concatenate.20.own), channel_id=1, source_target_pairs={{96,32},{97,33},{98,34},{99,35},{100,36},{101,37},{102,38},{103,39... | collective-permute-start | bytes 184328 | tf_op jit(solution)/shard_map/cond/branch_0_fun/ppermute | solution.py:731
  92.4 8.4 %collective-permute-start.6 = (bf16[24,1280]{1,0:T(8,128)(2,1)S(1)}, bf16[24,1280]{1,0:T(8,128)(2,1)S(1)}, u32[]{:S(2)}, u32[]{:S(2)}) collective-permute-start(bf16[24,1280]{1,0:T(8,128)(2,1)S(1)} %concatenate.20.own), channel_id=1, source_target_pairs={{96,64},{97,65},{98,66},{99,67},{100,68},{101,69},{102,70},{103,71... | collective-permute-start | bytes 184328 | tf_op jit(solution)/shard_map/cond/branch_0_fun/ppermute | solution.py:731
